TPU v7x, 256 devices: a whole 4x4x8 slice. The times are simulated.
256 devices in a mesh: tst: 64 (over y, z, core), req: 4 (over x).
Axes of the slice: x: 4, y: 4, z: 8, core: 2. Of those that a mesh axis runs over, the one named last changes fastest.
Arguments:
- coverage_tiles: bfloat16 [32768, 128, 128], P(('tst', 'req')), may hold values from 0 to 0.0006904602
- tile_rows: int32 [32768], P(('tst', 'req')), may hold values from 0 to 127
- tile_cols: int32 [32768], P(('tst', 'req')), may hold values from 0 to 63
- tile_counts: int32 [256], P(('tst', 'req')), may hold values from 32 to 128, as said below
- test_costs: float32 [524288], P('tst'), may hold values from 0.05 to 1.5, as said below
- runtimes: float32 [524288], P('tst'), may hold values from 0.05 to 4.5, as said below
- time_limit: float32 [1], replicated, may hold values from 0 to 0.2
- demand: float32 [65536], P('req'), may hold values from 0.1 to 0.6
- primal_start: float32 [524288], P('tst'), may hold values from 0 to 1
- dual_start: float32 [65536], P('req'), may hold values from 0 to 0.5
- limit_dual_start: float32 [1], replicated, may hold values from 0.5 to 1.5
- restarts: int32 [3], replicated, may hold values from 0 to 1
Outputs:
- primal_out: float32 [524288], P('tst')
- dual_out: float32 [65536], P('req')
- limit_dual: float32 [1], replicated
- move_norms: float32 [3, 2], replicated
Inputs may be any that keep to these rules, and one draw needn't show every extreme that they name: `tile_counts`: live slots of a device; some device has all 128 live in every draw. `test_costs`: positive costs. `runtimes`: positive running times.
All inputs are finite; a program needn't handle non-finite values.
Results may differ from a plain program's by a relative error of at most 0.0003.
Values may be sent and summed in bfloat16 or wider, within the bound.
No kernel may reach another device: no remote copies, remote signals or barrier semaphores. Data moves between devices by JAX's collectives and lax.ppermute only.
A program may use at most 64 MiB of HBM per device.

v0:
```python
import functools

import jax
import jax.numpy as jnp
from jax import lax
from jax.experimental import pallas as pl
from jax.experimental.pallas import tpu as pltpu
from jax.sharding import PartitionSpec as P

ITERS = 3
LANES = 128
STAT_ROWS = 8
GROUP = 16
KEPT = 6

step_primal = 0.6
step_dual = 0.6

VMEM = pl.BlockSpec(memory_space=pltpu.VMEM)
HBM = pl.BlockSpec(memory_space=pltpu.HBM)
F32 = jnp.float32
BF16 = jnp.bfloat16


def struct(*shape, dtype=F32):
    return jax.ShapeDtypeStruct(shape, dtype)


def stat_rows(*given):
    return jnp.concatenate([*given, jnp.zeros((STAT_ROWS - len(given), LANES), F32)], axis=0)


def sum_four(parts, rows):
    a, b, c, d = [part[rows, :] for part in parts]
    return (a + b) + (c + d)


def slot_count(params, iteration):
    seen = jnp.ones((1, LANES), F32)
    for earlier in range(iteration):
        seen = jnp.where(params[1 + earlier : 2 + earlier, :] == 1.0, 1.0, seen + 1.0)
    return seen


def average(params, iteration, total, new):
    restart_now = params[1 + iteration : 2 + iteration, :] == 1.0
    return (
        jnp.where(restart_now, total / slot_count(params, iteration), new),
        jnp.where(restart_now, 0.0, total),
    )


def spread(picked, group):
    rows = picked[group * GROUP : (group + 1) * GROUP, :]
    row_ids = lax.broadcasted_iota(jnp.int32, rows.shape, 0)
    return jnp.concatenate(
        [jnp.where(row_ids == offset, rows, 0.0) for offset in range(GROUP)], axis=1
    ).astype(BF16)


def gather_rows(pick, source):
    return jnp.dot(pick, source.astype(BF16), preferred_element_type=F32)


def scatter_sum(place, contrib):
    return jnp.dot(place, contrib, preferred_element_type=F32, precision=lax.Precision.HIGHEST)


def pull_group(picked, tiles, group):
    block = tiles[group][...].reshape(GROUP * LANES, LANES)
    return jnp.dot(spread(picked, group), block, preferred_element_type=F32)


def load_group(picked, tiles, group):
    block = jnp.concatenate([tiles[group][offset] for offset in range(GROUP)], axis=1)
    return lax.dot_general(
        spread(picked, group), block, (((1,), (1,)), ((), ())), preferred_element_type=F32
    )


def list_of(fetched):
    return [fetched.at[n] for n in range(fetched.shape[0])]


def rest_kernel(tiles_in, after, *refs):
    kept, sems = refs[:-1], refs[-1]
    copies = []
    for n, target in enumerate(kept):
        part = tiles_in.at[pl.ds((KEPT + n) * GROUP, GROUP)]
        copies.append(pltpu.make_async_copy(part, target, sems.at[n]))
        copies[-1].start()
    for copy in copies:
        copy.wait()


def first_pull_kernel(
    tiles_in, dual_in, rows_in, cols_in, live_in, pull_out, pick_rows, place_rows, pick_cols, place_cols, *refs
):
    slots = tiles_in.shape[0]
    groups = slots // GROUP
    kept, (fetched, dual, rows, cols, live, sems, tile_sems) = refs[:KEPT], refs[KEPT:]
    tiles = [*kept, *list_of(fetched)]
    small = []
    for n, (source, target) in enumerate(((rows_in, rows), (cols_in, cols), (live_in, live), (dual_in, dual))):
        small.append(pltpu.make_async_copy(source, target, sems.at[n]))
        small[-1].start()
    chunks = []
    for n in range(groups):
        chunks.append(pltpu.make_async_copy(tiles_in.at[pl.ds(n * GROUP, GROUP)], tiles[n], tile_sems.at[n]))
        chunks[-1].start()
    for copy in small:
        copy.wait()
    req_blocks = dual.shape[0]
    test_blocks = pull_out.shape[0] - STAT_ROWS
    alive = lax.broadcasted_iota(jnp.int32, (1, slots), 1) < live[...]
    at_row = lax.broadcasted_iota(jnp.int32, (req_blocks, slots), 0) == rows[...]
    at_col = lax.broadcasted_iota(jnp.int32, (test_blocks, slots), 0) == cols[...]
    one_row = jnp.where(at_row, 1.0, 0.0)
    one_col = jnp.where(at_col, 1.0, 0.0)
    place_rows[...] = jnp.where(alive, one_row, 0.0)
    place_cols[...] = jnp.where(alive, one_col, 0.0)
    pick = one_row.T.astype(BF16)
    pick_rows[...] = pick
    pick_cols[...] = jnp.concatenate([one_col, jnp.zeros((slots - test_blocks, slots), F32)], axis=0).T.astype(BF16)
    picked = gather_rows(pick, dual[...])
    contrib = []
    for group in range(groups):
        chunks[group].wait()
        contrib.append(pull_group(picked, tiles, group))
    pull_out[:test_blocks, :] = scatter_sum(place_cols[...], jnp.concatenate(contrib, axis=0))
    pull_out[test_blocks:, :] = jnp.zeros((STAT_ROWS, LANES), F32)


def update_dual(iteration, inverse_tests, summed, params, dual, sum_dual, scal, demand):
    req_blocks = dual.shape[0]
    load = summed[:req_blocks, :]
    stats = summed[req_blocks:, :]
    spent = jnp.sum(stats[0:1, :], axis=1, keepdims=True) * inverse_tests
    bdual = scal[0:1, :]
    bdual_new = jnp.maximum(bdual + step_dual * (spent - params[0:1, :]), 0.0)
    old = dual[...]
    new = jnp.maximum(old + step_dual * (demand[...] - load), 0.0)
    dual_sq = jnp.sum((new - old) ** 2, axis=0, keepdims=True)
    total = new if sum_dual is None else sum_dual[...] + new
    dual_next, total_next = average(params, iteration, total, new)
    bdual_next, bdual_total = average(params, iteration, scal[1:2, :] + bdual_new, bdual_new)
    scal_next = stat_rows(bdual_next, bdual_total, (bdual_new - bdual) ** 2, stats[1:2, :])
    return dual_next, total_next, scal_next, dual_sq


def dual_pull_kernel(iteration, inverse_tests, *refs):
    summed, params, pick_rows, place_cols, dual, scal, demand, *refs = refs
    groups = pick_rows.shape[0] // GROUP
    tiles, refs = refs[:groups], refs[groups:]
    sum_dual = refs.pop(0) if iteration > 0 else None
    pull_out, dual_out, sum_out, scal_out = refs
    dual_next, total_next, scal_next, dual_sq = update_dual(
        iteration, inverse_tests, summed, params, dual, sum_dual, scal, demand
    )
    dual_out[...] = dual_next
    sum_out[...] = total_next
    scal_out[...] = scal_next
    picked = gather_rows(pick_rows[...], dual_next)
    contrib = [pull_group(picked, tiles, group) for group in range(groups)]
    test_blocks = pull_out.shape[0] - STAT_ROWS
    pull_out[:test_blocks, :] = scatter_sum(place_cols[...], jnp.concatenate(contrib, axis=0))
    pull_out[test_blocks:, :] = stat_rows(dual_sq)


def dual_last_kernel(
    iteration, inverse_tests, summed, params, dual, scal, demand, sum_dual, dual_out, scal_out, sq_out
):
    dual_next, _, scal_next, dual_sq = update_dual(
        iteration, inverse_tests, summed, params, dual, sum_dual, scal, demand
    )
    dual_out[...] = dual_next
    scal_out[...] = scal_next
    sq_out[...] = stat_rows(dual_sq)


def primal_load_kernel(iteration, *refs):
    pull_own, pull_1, pull_2, pull_3, params, pick_cols, place_rows, primal, scal, costs, runtimes, *refs = refs
    slots = pick_cols.shape[0]
    groups = slots // GROUP
    tiles, refs = refs[:groups], refs[groups:]
    sum_primal = refs.pop(0) if iteration > 0 else None
    load_out, primal_out, sum_out, sq_out = refs
    test_blocks = primal.shape[0]
    parts = (pull_own, pull_1, pull_2, pull_3)
    pull = sum_four(parts, slice(0, test_blocks))
    sq_out[...] = sum_four(parts, slice(test_blocks, test_blocks + STAT_ROWS))
    old = primal[...]
    new = jnp.clip(old - step_primal * (costs[...] - pull + scal[0:1, :] * runtimes[...]), 0.0, 1.0)
    extrap = (2.0 * new - old).astype(BF16).astype(F32)
    total = new if sum_primal is None else sum_primal[...] + new
    primal_next, total_next = average(params, iteration, total, new)
    primal_out[...] = primal_next
    sum_out[...] = total_next
    padded = jnp.concatenate([extrap, jnp.zeros((slots - test_blocks, LANES), F32)], axis=0)
    picked = gather_rows(pick_cols[...], padded)
    contrib = [load_group(picked, tiles, group) for group in range(groups)]
    req_blocks = load_out.shape[0] - STAT_ROWS
    load_out[:req_blocks, :] = scatter_sum(place_rows[...], jnp.concatenate(contrib, axis=0))
    load_out[req_blocks:, :] = stat_rows(
        jnp.sum(runtimes[...] * extrap, axis=0, keepdims=True),
        jnp.sum((new - old) ** 2, axis=0, keepdims=True),
    )


def norms_kernel(sq_0, sq_1, last_0, last_1, last_2, last_3, scal_0, scal_1, scal_2, norms_out):
    row_ids = lax.broadcasted_iota(jnp.int32, norms_out.shape, 0)
    col_ids = lax.broadcasted_iota(jnp.int32, norms_out.shape, 1)
    last = sum_four((last_0, last_1, last_2, last_3), slice(0, 1))
    out = jnp.zeros(norms_out.shape, F32)
    for k, (sq, scal) in enumerate(((sq_0[0:1, :], scal_0), (sq_1[0:1, :], scal_1), (last, scal_2))):
        move_dual = jnp.sum(sq, axis=1, keepdims=True) + scal[2:3, 0:1]
        move_primal = jnp.sum(scal[3:4, :], axis=1, keepdims=True)
        out = jnp.where(col_ids == k, jnp.where(row_ids == 0, move_primal, move_dual), out)
    norms_out[...] = out


def results_kernel(params, state_own, state_other, norms_own, norms_other, dual_out, limit_out, norms_out):
    mine = params[1 + ITERS : 2 + ITERS, :] == 1.0
    req_blocks = dual_out.shape[0]
    dual_out[...] = jnp.where(mine, state_own[:req_blocks, :], state_other[:req_blocks, :])
    limit_out[...] = jnp.where(mine, state_own[req_blocks : req_blocks + 1, :], state_other[req_blocks : req_blocks + 1, :])[:, :1]
    norms_out[...] = jnp.where(mine[:, :ITERS], norms_own[...], norms_other[...])


def call(body, outs, specs, scratch=()):
    return pl.pallas_call(
        body,
        out_shape=outs,
        in_specs=specs,
        out_specs=jax.tree.map(lambda _: VMEM, outs),
        scratch_shapes=list(scratch),
        compiler_params=pltpu.CompilerParams(vmem_limit_bytes=(50 if HBM in specs else 16) * 1024 * 1024),
    )


def per_device(
    n_y, n_z,
    coverage_tiles, tile_rows, tile_cols, tile_counts, test_costs, runtimes, time_limit, demand,
    primal_start, dual_start, limit_dual_start, restarts,
):
    slots = coverage_tiles.shape[0]
    test_blocks = test_costs.shape[0] // LANES
    req_blocks = demand.shape[0] // LANES
    inverse_tests = 1.0 / (test_costs.shape[0] * lax.axis_size("tst"))
    costs = test_costs.reshape(test_blocks, LANES)
    runs = runtimes.reshape(test_blocks, LANES)
    want = demand.reshape(req_blocks, LANES)
    primal = primal_start.reshape(test_blocks, LANES)
    dual = dual_start.reshape(req_blocks, LANES)

    far_core = lax.axis_index("tst") % 2 == 1

    n_req = lax.axis_size("req")

    def on_mesh(x, move):
        pairs = []
        for y in range(n_y):
            for z in range(n_z):
                for c in range(2):
                    for r in range(n_req):
                        to_y, to_z, to_c, to_r = move(y, z, c, r)
                        source = ((y * n_z + z) * 2 + c) * n_req + r
                        pairs.append((source, ((to_y * n_z + to_z) * 2 + to_c) * n_req + to_r))
        return lax.ppermute(x, ("tst", "req"), pairs)

    def swap_core(x):
        return on_mesh(x, lambda y, z, c, r: (y, z, 1 - c, r))

    def chips(x, y_bits, z_bits):
        return on_mesh(x, lambda y, z, c, r: (y ^ y_bits, z ^ z_bits, c, r) if c == 1 else (y, z, c, r ^ 1))

    def on_req(x):
        return [lax.ppermute(x, "req", [(i, i ^ bit) for i in range(n_req)]) for bit in (1, 3, 2)]

    def total_tst(x):
        with jax.named_scope("sum_core"):
            x = x + swap_core(x)
        with jax.named_scope("sum_y"):
            a, b, c = [chips(x, bits, 0) for bits in (1, 3, 2)]
            x = (x + a) + (b + c)
        with jax.named_scope("sum_z_inner"):
            a, b, c = [chips(x, 0, bits) for bits in (1, 3, 2)]
            x = (x + a) + (b + c)
        with jax.named_scope("sum_z_outer"):
            x = x + chips(x, 0, n_z - 2)
        return x

    def hand_on(x):
        with jax.named_scope("back_core"):
            return jnp.where(far_core, x, swap_core(x))

    wide = lambda x: jnp.broadcast_to(x.astype(F32).reshape(-1, 1), (x.shape[0], LANES))
    params = jnp.concatenate(
        [wide(time_limit), wide(restarts), wide(far_core.reshape(1)), jnp.zeros((STAT_ROWS - 2 - ITERS, LANES), F32)], axis=0
    )
    scal = jnp.concatenate([wide(limit_dual_start), jnp.zeros((STAT_ROWS - 1, LANES), F32)], axis=0)
    big_t = struct(test_blocks, LANES)
    big_r = struct(req_blocks, LANES)
    small = struct(STAT_ROWS, LANES)
    pull_shape = struct(test_blocks + STAT_ROWS, LANES)
    load_shape = struct(req_blocks + STAT_ROWS, LANES)
    group_shape = struct(GROUP, LANES, LANES, dtype=BF16)
    rest = slots // GROUP - KEPT
    sq_list, scal_list = [], []
    sum_primal = sum_dual = ()
    for iteration in range(ITERS):
        if iteration == 0:
            given = (
                coverage_tiles, dual, tile_rows.reshape(1, slots), tile_cols.reshape(1, slots), tile_counts.reshape(1, 1)
            )
            pull, pick_rows, place_rows, pick_cols, place_cols, *tiles = call(
                first_pull_kernel,
                (
                    pull_shape, struct(slots, req_blocks, dtype=BF16), struct(req_blocks, slots),
                    struct(slots, slots, dtype=BF16), struct(test_blocks, slots),
                    *[group_shape] * KEPT,
                ),
                [HBM] * len(given),
                [pltpu.VMEM((rest, *group_shape.shape), BF16), *[pltpu.VMEM(x.shape, x.dtype) for x in given[1:]]]
                + [pltpu.SemaphoreType.DMA((n,)) for n in (len(given) - 1, slots // GROUP)],
            )(*given)
            tiles += call(
                rest_kernel, [group_shape] * rest, [HBM, VMEM], [pltpu.SemaphoreType.DMA((rest,))]
            )(coverage_tiles, pick_cols)
        else:
            given = (summed, params, pick_rows, place_cols, dual, scal, want, *tiles, *sum_dual)
            pull, dual, total, scal = call(
                functools.partial(dual_pull_kernel, iteration - 1, inverse_tests),
                (pull_shape, big_r, big_r, small), [VMEM] * len(given),
            )(*given)
            sum_dual = (total,)
            scal_list.append(scal)
        with jax.named_scope("sum_req"):
            parts = [pull, *on_req(pull)]
        given = (*parts, params, pick_cols, place_rows, primal, scal, costs, runs, *tiles, *sum_primal)
        load, primal, total, sq = call(
            functools.partial(primal_load_kernel, iteration), (load_shape, big_t, big_t, small), [VMEM] * len(given)
        )(*given)
        sum_primal = (total,)
        if iteration > 0:
            sq_list.append(sq)
        summed = total_tst(load)
        if iteration < ITERS - 1:
            summed = hand_on(summed)
    dual, scal, sq = call(
        functools.partial(dual_last_kernel, ITERS - 1, inverse_tests), (big_r, small, small), [VMEM] * 6
    )(summed, params, dual, scal, want, *sum_dual)
    scal_list.append(scal)
    with jax.named_scope("sum_req_last"):
        moves = [lambda y, z, c, r, bit=bit: (y, z, c, r ^ bit) if c == 1 else (y ^ 1, z, c, r) for bit in (1, 3, 2)]
        last = [sq, *[on_mesh(sq, move) for move in moves]]
    norms = call(norms_kernel, struct(2, ITERS), [VMEM] * 9)(*sq_list, *last, *scal_list)
    state = jnp.concatenate([dual, scal], axis=0)
    with jax.named_scope("back_core"):
        other = swap_core(state), swap_core(norms)
    dual, limit, norms = call(results_kernel, (big_r, struct(1, 1), struct(2, ITERS)), [VMEM] * 5)(
        params, state, other[0], norms, other[1]
    )
    return primal.reshape(-1), dual.reshape(-1), limit.reshape(1), norms.T


def solution(mesh):
    n_y = 4
    n_z = mesh.shape["tst"] // (2 * n_y)
    return jax.shard_map(
        functools.partial(per_device, n_y, n_z),
        mesh=mesh,
        in_specs=(
            P(("tst", "req"), None, None),
            P(("tst", "req")),
            P(("tst", "req")),
            P(("tst", "req")),
            P("tst"),
            P("tst"),
            P(),
            P("req"),
            P("tst"),
            P("req"),
            P(),
            P(),
        ),
        out_specs=(P("tst"), P("req"), P(), P()),
        check_vma=False,
    )
```

profile of v0, /device:TPU:1, one launch (start us, length us, event | category | flops | bytes accessed | tf_op | source)
XLA Modules:
  0.0 112.3 jit_solution(5033167657061107476)
XLA Ops:
  3.4 3.0 %shard_map.147 = (f32[72,128]{1,0:T(8,128)S(1)}, bf16[128,128]{1,0:T(8,128)(2,1)S(1)}, f32[128,128]{1,0:T(8,128)S(1)}, bf16[128,128]{1,0:T(8,128)(2,1)S(1)}, f32...) custom-call(bf16[128,128,128]{2,1,0:T(8,128)(2,1)} %tiles_in.3, ...), custom_call_target="tpu_custom_call" | custom-call | tf_op jit(solution)/shard_map/pallas_call | solution.py:316
  6.4 3.7 %collective-permute-start.2 = (f32[72,128]{1,0:T(8,128)S(1)}, f32[72,128]{1,0:T(8,128)S(1)}, u32[]{:S(2)}, u32[]{:S(2)}) collective-permute-start(f32[72,128]{1,0:T(8,128)S(1)} %get-tuple-element.41.refs_0_), channel_id=1, source_target_pairs={{0,2},{1,3},{2,0},{3,1},{4,6},{5,7},{6,4},{7,5},{8,10},{9,11},{10,... | collective-permute-start | bytes 110600 | tf_op jit(solution)/shard_map/sum_req/ppermute | solution.py:278
  14.6 2.1 %shard_map.149 = (f32[136,128]{1,0:T(8,128)S(1)}, f32[64,128]{1,0:T(8,128)S(1)}, f32[64,128]{1,0:T(8,128)S(1)}, f32[8,128]{1,0:T(8,128)}) custom-call(f32[72,128]{1,0:T(8,128)S(1)} %get-tuple-element.41.refs_0_, f32[72,128]{1,0:T(8,128)S(1)} %collective-permute-done.refs_1_, f32[72,128]{1,0:T(8,128)S(1)} %collective-permute-done.1.refs_2_, ...), custom_call_target="tpu_custom_call" | custom-call | tf_op jit(solution)/shard_map/pallas_call | solution.py:341
  16.6 2.2 %collective-permute-start.3 = (f32[136,128]{1,0:T(8,128)S(1)}, f32[136,128]{1,0:T(8,128)S(1)}, u32[]{:S(2)}, u32[]{:S(2)}) collective-permute-start(f32[136,128]{1,0:T(8,128)S(1)} %get-tuple-element.52), channel_id=1, source_target_pairs={{0,4},{1,5},{2,6},{3,7},{4,0},{5,1},{6,2},{7,3},{8,12},{9,13},{10,... | collective-permute-start | bytes 208904 | tf_op jit(solution)/shard_map/sum_core/ppermute | solution.py:269
  19.7 2.6 %collective-permute-start.6 = (f32[136,128]{1,0:T(8,128)S(1)}, f32[136,128]{1,0:T(8,128)S(1)}, u32[]{:S(2)}, u32[]{:S(2)}) collective-permute-start(f32[136,128]{1,0:T(8,128)S(1)} %add.79), channel_id=1, source_target_pairs={{0,1},{1,0},{2,3},{3,2},{4,132},{5,133},{6,134},{7,135},{8,9},{9,8... | collective-permute-start | bytes 208904 | tf_op jit(solution)/shard_map/sum_y/ppermute | solution.py:269
  24.5 2.2 %collective-permute-done.5 = f32[136,128]{1,0:T(8,128)S(1)} collective-permute-done((f32[136,128]{1,0:T(8,128)S(1)}, f32[136,128]{1,0:T(8,128)S(1)}, u32[]{:S(2)}, u32[]{:S(2)}) %collective-permute-start.5) | collective-permute-done | bytes 69664 | tf_op jit(solution)/shard_map/sum_y/ppermute | solution.py:269
  26.7 3.1 %collective-permute-start.9 = (f32[136,128]{1,0:T(8,128)S(1)}, f32[136,128]{1,0:T(8,128)S(1)}, u32[]{:S(2)}, u32[]{:S(2)}) collective-permute-start(f32[136,128]{1,0:T(8,128)S(1)} %add_add_fusion.5), channel_id=1, source_target_pairs={{0,1},{1,0},{2,3},{3,2},{4,20},{5,21},{6,22},{7,23},{8,9},{9,8},{1... | collective-permute-start | bytes 208904 | tf_op jit(solution)/shard_map/sum_z_inner/ppermute | solution.py:269
  31.5 3.4 %collective-permute-done.8 = f32[136,128]{1,0:T(8,128)S(1)} collective-permute-done((f32[136,128]{1,0:T(8,128)S(1)}, f32[136,128]{1,0:T(8,128)S(1)}, u32[]{:S(2)}, u32[]{:S(2)}) %collective-permute-start.8) | collective-permute-done | bytes 69664 | tf_op jit(solution)/shard_map/sum_z_inner/ppermute | solution.py:269
  35.2 3.7 %collective-permute-start.10 = (f32[136,128]{1,0:T(8,128)S(1)}, f32[136,128]{1,0:T(8,128)S(1)}, u32[]{:S(2)}, u32[]{:S(2)}) collective-permute-start(f32[136,128]{1,0:T(8,128)S(1)} %add_add_fusion.4), channel_id=1, source_target_pairs={{0,1},{1,0},{2,3},{3,2},{4,52},{5,53},{6,54},{7,55},{8,9},{9,8},{1... | collective-permute-start | bytes 208904 | tf_op jit(solution)/shard_map/sum_z_outer/ppermute | solution.py:269
  38.9 1.7 %collective-permute-done.10 = f32[136,128]{1,0:T(8,128)S(1)} collective-permute-done((f32[136,128]{1,0:T(8,128)S(1)}, f32[136,128]{1,0:T(8,128)S(1)}, u32[]{:S(2)}, u32[]{:S(2)}) %collective-permute-start.10) | collective-permute-done | bytes 69664 | tf_op jit(solution)/shard_map/sum_z_outer/ppermute | solution.py:269
  43.1 2.6 %collective-permute-start.14 = (f32[72,128]{1,0:T(8,128)S(1)}, f32[72,128]{1,0:T(8,128)S(1)}, u32[]{:S(2)}, u32[]{:S(2)}) collective-permute-start(f32[72,128]{1,0:T(8,128)S(1)} %get-tuple-element.55.refs_0_), channel_id=1, source_target_pairs={{0,2},{1,3},{2,0},{3,1},{4,6},{5,7},{6,4},{7,5},{8,10},{9,11},{10,... | collective-permute-start | bytes 110600 | tf_op jit(solution)/shard_map/sum_req/ppermute | solution.py:278
  47.4 2.3 %collective-permute-done.13.refs_2_ = f32[72,128]{1,0:T(8,128)S(1)} collective-permute-done((f32[72,128]{1,0:T(8,128)S(1)}, f32[72,128]{1,0:T(8,128)S(1)}, u32[]{:S(2)}, u32[]{:S(2)}) %collective-permute-start.13) | collective-permute-done | bytes 36896 | tf_op jit(solution)/shard_map/sum_req/ppermute | solution.py:278
  49.8 1.6 %shard_map.151 = (f32[136,128]{1,0:T(8,128)S(1)}, f32[64,128]{1,0:T(8,128)S(1)}, f32[64,128]{1,0:T(8,128)S(1)}, f32[8,128]{1,0:T(8,128)S(1)}) custom-call(f32[72,128]{1,0:T(8,128)S(1)} %get-tuple-element.55.refs_0_, f32[72,128]{1,0:T(8,128)S(1)} %collective-permute-done.12.refs_1_, f32[72,128]{1,0:T(8,128)S(1)} %collective-permute-done.13.refs_2_, ...), custom_call_target="tpu_custom_call" | custom-call | tf_op jit(solution)/shard_map/pallas_call | solution.py:341
  51.4 1.9 %collective-permute-start.15 = (f32[136,128]{1,0:T(8,128)S(1)}, f32[136,128]{1,0:T(8,128)S(1)}, u32[]{:S(2)}, u32[]{:S(2)}) collective-permute-start(f32[136,128]{1,0:T(8,128)S(1)} %get-tuple-element.59), channel_id=1, source_target_pairs={{0,4},{1,5},{2,6},{3,7},{4,0},{5,1},{6,2},{7,3},{8,12},{9,13},{10,... | collective-permute-start | bytes 208904 | tf_op jit(solution)/shard_map/sum_core/ppermute | solution.py:269
  54.1 1.9 %collective-permute-start.18 = (f32[136,128]{1,0:T(8,128)S(1)}, f32[136,128]{1,0:T(8,128)S(1)}, u32[]{:S(2)}, u32[]{:S(2)}) collective-permute-start(f32[136,128]{1,0:T(8,128)S(1)} %add.87), channel_id=1, source_target_pairs={{0,1},{1,0},{2,3},{3,2},{4,132},{5,133},{6,134},{7,135},{8,9},{9,8... | collective-permute-start | bytes 208904 | tf_op jit(solution)/shard_map/sum_y/ppermute | solution.py:269
  56.9 2.0 %collective-permute-done.18 = f32[136,128]{1,0:T(8,128)S(1)} collective-permute-done((f32[136,128]{1,0:T(8,128)S(1)}, f32[136,128]{1,0:T(8,128)S(1)}, u32[]{:S(2)}, u32[]{:S(2)}) %collective-permute-start.18) | collective-permute-done | bytes 69664 | tf_op jit(solution)/shard_map/sum_y/ppermute | solution.py:269
  58.9 1.5 %collective-permute-done.17 = f32[136,128]{1,0:T(8,128)S(1)} collective-permute-done((f32[136,128]{1,0:T(8,128)S(1)}, f32[136,128]{1,0:T(8,128)S(1)}, u32[]{:S(2)}, u32[]{:S(2)}) %collective-permute-start.17) | collective-permute-done | bytes 69664 | tf_op jit(solution)/shard_map/sum_y/ppermute | solution.py:269
  60.4 2.4 %collective-permute-start.21 = (f32[136,128]{1,0:T(8,128)S(1)}, f32[136,128]{1,0:T(8,128)S(1)}, u32[]{:S(2)}, u32[]{:S(2)}) collective-permute-start(f32[136,128]{1,0:T(8,128)S(1)} %add_add_fusion.3), channel_id=1, source_target_pairs={{0,1},{1,0},{2,3},{3,2},{4,20},{5,21},{6,22},{7,23},{8,9},{9,8},{1... | collective-permute-start | bytes 208904 | tf_op jit(solution)/shard_map/sum_z_inner/ppermute | solution.py:269
  62.8 1.6 %collective-permute-start.20 = (f32[136,128]{1,0:T(8,128)S(1)}, f32[136,128]{1,0:T(8,128)S(1)}, u32[]{:S(2)}, u32[]{:S(2)}) collective-permute-start(f32[136,128]{1,0:T(8,128)S(1)} %add_add_fusion.3), channel_id=1, source_target_pairs={{0,1},{1,0},{2,3},{3,2},{4,28},{5,29},{6,30},{7,31},{8,9},{9,8},{1... | collective-permute-start | bytes 208904 | tf_op jit(solution)/shard_map/sum_z_inner/ppermute | solution.py:269
  64.5 3.4 %collective-permute-done.20 = f32[136,128]{1,0:T(8,128)S(1)} collective-permute-done((f32[136,128]{1,0:T(8,128)S(1)}, f32[136,128]{1,0:T(8,128)S(1)}, u32[]{:S(2)}, u32[]{:S(2)}) %collective-permute-start.20) | collective-permute-done | bytes 69664 | tf_op jit(solution)/shard_map/sum_z_inner/ppermute | solution.py:269
  68.4 2.2 %collective-permute-start.22 = (f32[136,128]{1,0:T(8,128)S(1)}, f32[136,128]{1,0:T(8,128)S(1)}, u32[]{:S(2)}, u32[]{:S(2)}) collective-permute-start(f32[136,128]{1,0:T(8,128)S(1)} %add_add_fusion.2), channel_id=1, source_target_pairs={{0,1},{1,0},{2,3},{3,2},{4,52},{5,53},{6,54},{7,55},{8,9},{9,8},{1... | collective-permute-start | bytes 208904 | tf_op jit(solution)/shard_map/sum_z_outer/ppermute | solution.py:269
  70.6 3.1 %collective-permute-done.22 = f32[136,128]{1,0:T(8,128)S(1)} collective-permute-done((f32[136,128]{1,0:T(8,128)S(1)}, f32[136,128]{1,0:T(8,128)S(1)}, u32[]{:S(2)}, u32[]{:S(2)}) %collective-permute-start.22) | collective-permute-done | bytes 69664 | tf_op jit(solution)/shard_map/sum_z_outer/ppermute | solution.py:269
  78.8 1.7 %collective-permute-done.26.refs_3_ = f32[72,128]{1,0:T(8,128)S(1)} collective-permute-done((f32[72,128]{1,0:T(8,128)S(1)}, f32[72,128]{1,0:T(8,128)S(1)}, u32[]{:S(2)}, u32[]{:S(2)}) %collective-permute-start.26) | collective-permute-done | bytes 36896 | tf_op jit(solution)/shard_map/sum_req/ppermute | solution.py:278
  81.5 2.0 %shard_map.153 = (f32[136,128]{1,0:T(8,128)S(1)}, f32[64,128]{1,0:T(8,128)}, f32[64,128]{1,0:T(8,128)}, f32[8,128]{1,0:T(8,128)S(1)}) custom-call(f32[72,128]{1,0:T(8,128)S(1)} %get-tuple-element.62.refs_0_, f32[72,128]{1,0:T(8,128)S(1)} %collective-permute-done.24.refs_1_, f32[72,128]{1,0:T(8,128)S(1)} %collective-permute-done.25.refs_2_, ...), custom_call_target="tpu_custom_call" | custom-call | tf_op jit(solution)/shard_map/pallas_call | solution.py:341
  85.8 1.8 %collective-permute-start.30 = (f32[136,128]{1,0:T(8,128)S(1)}, f32[136,128]{1,0:T(8,128)S(1)}, u32[]{:S(2)}, u32[]{:S(2)}) collective-permute-start(f32[136,128]{1,0:T(8,128)S(1)} %add.95), channel_id=1, source_target_pairs={{0,1},{1,0},{2,3},{3,2},{4,132},{5,133},{6,134},{7,135},{8,9},{9,8... | collective-permute-start | bytes 208904 | tf_op jit(solution)/shard_map/sum_y/ppermute | solution.py:269
  88.6 2.0 %collective-permute-done.30 = f32[136,128]{1,0:T(8,128)S(1)} collective-permute-done((f32[136,128]{1,0:T(8,128)S(1)}, f32[136,128]{1,0:T(8,128)S(1)}, u32[]{:S(2)}, u32[]{:S(2)}) %collective-permute-start.30) | collective-permute-done | bytes 69664 | tf_op jit(solution)/shard_map/sum_y/ppermute | solution.py:269
  93.2 1.6 %collective-permute-start.32 = (f32[136,128]{1,0:T(8,128)S(1)}, f32[136,128]{1,0:T(8,128)S(1)}, u32[]{:S(2)}, u32[]{:S(2)}) collective-permute-start(f32[136,128]{1,0:T(8,128)S(1)} %add_add_fusion.1), channel_id=1, source_target_pairs={{0,1},{1,0},{2,3},{3,2},{4,28},{5,29},{6,30},{7,31},{8,9},{9,8},{1... | collective-permute-start | bytes 208904 | tf_op jit(solution)/shard_map/sum_z_inner/ppermute | solution.py:269
  94.8 2.1 %collective-permute-done.33 = f32[136,128]{1,0:T(8,128)S(1)} collective-permute-done((f32[136,128]{1,0:T(8,128)S(1)}, f32[136,128]{1,0:T(8,128)S(1)}, u32[]{:S(2)}, u32[]{:S(2)}) %collective-permute-start.33) | collective-permute-done | bytes 69664 | tf_op jit(solution)/shard_map/sum_z_inner/ppermute | solution.py:269
  98.7 2.3 %collective-permute-start.34 = (f32[136,128]{1,0:T(8,128)S(1)}, f32[136,128]{1,0:T(8,128)S(1)}, u32[]{:S(2)}, u32[]{:S(2)}) collective-permute-start(f32[136,128]{1,0:T(8,128)S(1)} %add_add_fusion), channel_id=1, source_target_pairs={{0,1},{1,0},{2,3},{3,2},{4,52},{5,53},{6,54},{7,55},{8,9},{9,8},{1... | collective-permute-start | bytes 208904 | tf_op jit(solution)/shard_map/sum_z_outer/ppermute | solution.py:269
  101.0 3.0 %collective-permute-done.34 = f32[136,128]{1,0:T(8,128)S(1)} collective-permute-done((f32[136,128]{1,0:T(8,128)S(1)}, f32[136,128]{1,0:T(8,128)S(1)}, u32[]{:S(2)}, u32[]{:S(2)}) %collective-permute-start.34) | collective-permute-done | bytes 69664 | tf_op jit(solution)/shard_map/sum_z_outer/ppermute | solution.py:269
  104.5 2.1 %collective-permute-start.38 = (f32[8,128]{1,0:T(8,128)S(1)}, f32[8,128]{1,0:T(8,128)S(1)}, u32[]{:S(2)}, u32[]{:S(2)}) collective-permute-start(f32[8,128]{1,0:T(8,128)S(1)} %get-tuple-element.74.last_0), channel_id=1, source_target_pairs={{0,64},{1,65},{2,66},{3,67},{4,6},{5,7},{6,4},{7,5},{8,72},{9,73},... | collective-permute-start | bytes 12296 | tf_op jit(solution)/shard_map/sum_req_last/ppermute | solution.py:269
  108.6 1.7 %collective-permute-done.37.last_2 = f32[8,128]{1,0:T(8,128)S(1)} collective-permute-done((f32[8,128]{1,0:T(8,128)S(1)}, f32[8,128]{1,0:T(8,128)S(1)}, u32[]{:S(2)}, u32[]{:S(2)}) %collective-permute-start.37) | collective-permute-done | bytes 4128 | tf_op jit(solution)/shard_map/sum_req_last/ppermute | solution.py:269
  (96 shorter events, 35.1 us)
Async XLA Ops:
  6.4 7.9 %collective-permute-start.2 = (f32[72,128]{1,0:T(8,128)S(1)}, f32[72,128]{1,0:T(8,128)S(1)}, u32[]{:S(2)}, u32[]{:S(2)}) collective-permute-start(f32[72,128]{1,0:T(8,128)S(1)} %get-tuple-element.41.refs_0_), channel_id=1, source_target_pairs={{0,2},{1,3},{2,0},{3,1},{4,6},{5,7},{6,4},{7,5},{8,10},{9,11},{10,... | collective-permute-start | bytes 110600 | tf_op jit(solution)/shard_map/sum_req/ppermute | solution.py:278
  10.1 4.3 %collective-permute-start.1 = (f32[72,128]{1,0:T(8,128)S(1)}, f32[72,128]{1,0:T(8,128)S(1)}, u32[]{:S(2)}, u32[]{:S(2)}) collective-permute-start(f32[72,128]{1,0:T(8,128)S(1)} %get-tuple-element.41.refs_0_), channel_id=1, source_target_pairs={{0,3},{1,2},{2,1},{3,0},{4,7},{5,6},{6,5},{7,4},{8,11},{9,10},{10,... | collective-permute-start | bytes 110600 | tf_op jit(solution)/shard_map/sum_req/ppermute | solution.py:278
  10.9 3.5 %collective-permute-start = (f32[72,128]{1,0:T(8,128)S(1)}, f32[72,128]{1,0:T(8,128)S(1)}, u32[]{:S(2)}, u32[]{:S(2)}) collective-permute-start(f32[72,128]{1,0:T(8,128)S(1)} %get-tuple-element.41.refs_0_), channel_id=1, source_target_pairs={{0,1},{1,0},{2,3},{3,2},{4,5},{5,4},{6,7},{7,6},{8,9},{9,8},{10,11... | collective-permute-start | bytes 110600 | tf_op jit(solution)/shard_map/sum_req/ppermute | solution.py:278
  19.7 4.8 %collective-permute-start.6 = (f32[136,128]{1,0:T(8,128)S(1)}, f32[136,128]{1,0:T(8,128)S(1)}, u32[]{:S(2)}, u32[]{:S(2)}) collective-permute-start(f32[136,128]{1,0:T(8,128)S(1)} %add.79), channel_id=1, source_target_pairs={{0,1},{1,0},{2,3},{3,2},{4,132},{5,133},{6,134},{7,135},{8,9},{9,8... | collective-permute-start | bytes 208904 | tf_op jit(solution)/shard_map/sum_y/ppermute | solution.py:269
  22.3 4.4 %collective-permute-start.5 = (f32[136,128]{1,0:T(8,128)S(1)}, f32[136,128]{1,0:T(8,128)S(1)}, u32[]{:S(2)}, u32[]{:S(2)}) collective-permute-start(f32[136,128]{1,0:T(8,128)S(1)} %add.79), channel_id=1, source_target_pairs={{0,1},{1,0},{2,3},{3,2},{4,196},{5,197},{6,198},{7,199},{8,9},{9,8... | collective-permute-start | bytes 208904 | tf_op jit(solution)/shard_map/sum_y/ppermute | solution.py:269
  23.1 3.6 %collective-permute-start.4 = (f32[136,128]{1,0:T(8,128)S(1)}, f32[136,128]{1,0:T(8,128)S(1)}, u32[]{:S(2)}, u32[]{:S(2)}) collective-permute-start(f32[136,128]{1,0:T(8,128)S(1)} %add.79), channel_id=1, source_target_pairs={{0,1},{1,0},{2,3},{3,2},{4,68},{5,69},{6,70},{7,71},{8,9},{9,8},{1... | collective-permute-start | bytes 208904 | tf_op jit(solution)/shard_map/sum_y/ppermute | solution.py:269
  26.7 4.8 %collective-permute-start.9 = (f32[136,128]{1,0:T(8,128)S(1)}, f32[136,128]{1,0:T(8,128)S(1)}, u32[]{:S(2)}, u32[]{:S(2)}) collective-permute-start(f32[136,128]{1,0:T(8,128)S(1)} %add_add_fusion.5), channel_id=1, source_target_pairs={{0,1},{1,0},{2,3},{3,2},{4,20},{5,21},{6,22},{7,23},{8,9},{9,8},{1... | collective-permute-start | bytes 208904 | tf_op jit(solution)/shard_map/sum_z_inner/ppermute | solution.py:269
  29.8 5.1 %collective-permute-start.8 = (f32[136,128]{1,0:T(8,128)S(1)}, f32[136,128]{1,0:T(8,128)S(1)}, u32[]{:S(2)}, u32[]{:S(2)}) collective-permute-start(f32[136,128]{1,0:T(8,128)S(1)} %add_add_fusion.5), channel_id=1, source_target_pairs={{0,1},{1,0},{2,3},{3,2},{4,28},{5,29},{6,30},{7,31},{8,9},{9,8},{1... | collective-permute-start | bytes 208904 | tf_op jit(solution)/shard_map/sum_z_inner/ppermute | solution.py:269
  31.3 3.9 %collective-permute-start.7 = (f32[136,128]{1,0:T(8,128)S(1)}, f32[136,128]{1,0:T(8,128)S(1)}, u32[]{:S(2)}, u32[]{:S(2)}) collective-permute-start(f32[136,128]{1,0:T(8,128)S(1)} %add_add_fusion.5), channel_id=1, source_target_pairs={{0,1},{1,0},{2,3},{3,2},{4,12},{5,13},{6,14},{7,15},{8,9},{9,8},{1... | collective-permute-start | bytes 208904 | tf_op jit(solution)/shard_map/sum_z_inner/ppermute | solution.py:269
  35.2 5.5 %collective-permute-start.10 = (f32[136,128]{1,0:T(8,128)S(1)}, f32[136,128]{1,0:T(8,128)S(1)}, u32[]{:S(2)}, u32[]{:S(2)}) collective-permute-start(f32[136,128]{1,0:T(8,128)S(1)} %add_add_fusion.4), channel_id=1, source_target_pairs={{0,1},{1,0},{2,3},{3,2},{4,52},{5,53},{6,54},{7,55},{8,9},{9,8},{1... | collective-permute-start | bytes 208904 | tf_op jit(solution)/shard_map/sum_z_outer/ppermute | solution.py:269
  43.1 4.3 %collective-permute-start.14 = (f32[72,128]{1,0:T(8,128)S(1)}, f32[72,128]{1,0:T(8,128)S(1)}, u32[]{:S(2)}, u32[]{:S(2)}) collective-permute-start(f32[72,128]{1,0:T(8,128)S(1)} %get-tuple-element.55.refs_0_), channel_id=1, source_target_pairs={{0,2},{1,3},{2,0},{3,1},{4,6},{5,7},{6,4},{7,5},{8,10},{9,11},{10,... | collective-permute-start | bytes 110600 | tf_op jit(solution)/shard_map/sum_req/ppermute | solution.py:278
  45.8 4.0 %collective-permute-start.13 = (f32[72,128]{1,0:T(8,128)S(1)}, f32[72,128]{1,0:T(8,128)S(1)}, u32[]{:S(2)}, u32[]{:S(2)}) collective-permute-start(f32[72,128]{1,0:T(8,128)S(1)} %get-tuple-element.55.refs_0_), channel_id=1, source_target_pairs={{0,3},{1,2},{2,1},{3,0},{4,7},{5,6},{6,5},{7,4},{8,11},{9,10},{10,... | collective-permute-start | bytes 110600 | tf_op jit(solution)/shard_map/sum_req/ppermute | solution.py:278
  54.1 4.8 %collective-permute-start.18 = (f32[136,128]{1,0:T(8,128)S(1)}, f32[136,128]{1,0:T(8,128)S(1)}, u32[]{:S(2)}, u32[]{:S(2)}) collective-permute-start(f32[136,128]{1,0:T(8,128)S(1)} %add.87), channel_id=1, source_target_pairs={{0,1},{1,0},{2,3},{3,2},{4,132},{5,133},{6,134},{7,135},{8,9},{9,8... | collective-permute-start | bytes 208904 | tf_op jit(solution)/shard_map/sum_y/ppermute | solution.py:269
  56.0 4.4 %collective-permute-start.17 = (f32[136,128]{1,0:T(8,128)S(1)}, f32[136,128]{1,0:T(8,128)S(1)}, u32[]{:S(2)}, u32[]{:S(2)}) collective-permute-start(f32[136,128]{1,0:T(8,128)S(1)} %add.87), channel_id=1, source_target_pairs={{0,1},{1,0},{2,3},{3,2},{4,196},{5,197},{6,198},{7,199},{8,9},{9,8... | collective-permute-start | bytes 208904 | tf_op jit(solution)/shard_map/sum_y/ppermute | solution.py:269
  56.8 3.6 %collective-permute-start.16 = (f32[136,128]{1,0:T(8,128)S(1)}, f32[136,128]{1,0:T(8,128)S(1)}, u32[]{:S(2)}, u32[]{:S(2)}) collective-permute-start(f32[136,128]{1,0:T(8,128)S(1)} %add.87), channel_id=1, source_target_pairs={{0,1},{1,0},{2,3},{3,2},{4,68},{5,69},{6,70},{7,71},{8,9},{9,8},{1... | collective-permute-start | bytes 208904 | tf_op jit(solution)/shard_map/sum_y/ppermute | solution.py:269
  60.4 4.1 %collective-permute-start.21 = (f32[136,128]{1,0:T(8,128)S(1)}, f32[136,128]{1,0:T(8,128)S(1)}, u32[]{:S(2)}, u32[]{:S(2)}) collective-permute-start(f32[136,128]{1,0:T(8,128)S(1)} %add_add_fusion.3), channel_id=1, source_target_pairs={{0,1},{1,0},{2,3},{3,2},{4,20},{5,21},{6,22},{7,23},{8,9},{9,8},{1... | collective-permute-start | bytes 208904 | tf_op jit(solution)/shard_map/sum_z_inner/ppermute | solution.py:269
  62.8 5.1 %collective-permute-start.20 = (f32[136,128]{1,0:T(8,128)S(1)}, f32[136,128]{1,0:T(8,128)S(1)}, u32[]{:S(2)}, u32[]{:S(2)}) collective-permute-start(f32[136,128]{1,0:T(8,128)S(1)} %add_add_fusion.3), channel_id=1, source_target_pairs={{0,1},{1,0},{2,3},{3,2},{4,28},{5,29},{6,30},{7,31},{8,9},{9,8},{1... | collective-permute-start | bytes 208904 | tf_op jit(solution)/shard_map/sum_z_inner/ppermute | solution.py:269
  64.4 3.9 %collective-permute-start.19 = (f32[136,128]{1,0:T(8,128)S(1)}, f32[136,128]{1,0:T(8,128)S(1)}, u32[]{:S(2)}, u32[]{:S(2)}) collective-permute-start(f32[136,128]{1,0:T(8,128)S(1)} %add_add_fusion.3), channel_id=1, source_target_pairs={{0,1},{1,0},{2,3},{3,2},{4,12},{5,13},{6,14},{7,15},{8,9},{9,8},{1... | collective-permute-start | bytes 208904 | tf_op jit(solution)/shard_map/sum_z_inner/ppermute | solution.py:269
  68.4 5.4 %collective-permute-start.22 = (f32[136,128]{1,0:T(8,128)S(1)}, f32[136,128]{1,0:T(8,128)S(1)}, u32[]{:S(2)}, u32[]{:S(2)}) collective-permute-start(f32[136,128]{1,0:T(8,128)S(1)} %add_add_fusion.2), channel_id=1, source_target_pairs={{0,1},{1,0},{2,3},{3,2},{4,52},{5,53},{6,54},{7,55},{8,9},{9,8},{1... | collective-permute-start | bytes 208904 | tf_op jit(solution)/shard_map/sum_z_outer/ppermute | solution.py:269
  76.1 4.3 %collective-permute-start.26 = (f32[72,128]{1,0:T(8,128)S(1)}, f32[72,128]{1,0:T(8,128)S(1)}, u32[]{:S(2)}, u32[]{:S(2)}) collective-permute-start(f32[72,128]{1,0:T(8,128)S(1)} %get-tuple-element.62.refs_0_), channel_id=1, source_target_pairs={{0,2},{1,3},{2,0},{3,1},{4,6},{5,7},{6,4},{7,5},{8,10},{9,11},{10,... | collective-permute-start | bytes 110600 | tf_op jit(solution)/shard_map/sum_req/ppermute | solution.py:278
  77.3 4.1 %collective-permute-start.25 = (f32[72,128]{1,0:T(8,128)S(1)}, f32[72,128]{1,0:T(8,128)S(1)}, u32[]{:S(2)}, u32[]{:S(2)}) collective-permute-start(f32[72,128]{1,0:T(8,128)S(1)} %get-tuple-element.62.refs_0_), channel_id=1, source_target_pairs={{0,3},{1,2},{2,1},{3,0},{4,7},{5,6},{6,5},{7,4},{8,11},{9,10},{10,... | collective-permute-start | bytes 110600 | tf_op jit(solution)/shard_map/sum_req/ppermute | solution.py:278
  78.2 3.3 %collective-permute-start.24 = (f32[72,128]{1,0:T(8,128)S(1)}, f32[72,128]{1,0:T(8,128)S(1)}, u32[]{:S(2)}, u32[]{:S(2)}) collective-permute-start(f32[72,128]{1,0:T(8,128)S(1)} %get-tuple-element.62.refs_0_), channel_id=1, source_target_pairs={{0,1},{1,0},{2,3},{3,2},{4,5},{5,4},{6,7},{7,6},{8,9},{9,8},{10,11... | collective-permute-start | bytes 110600 | tf_op jit(solution)/shard_map/sum_req/ppermute | solution.py:278
  85.8 4.8 %collective-permute-start.30 = (f32[136,128]{1,0:T(8,128)S(1)}, f32[136,128]{1,0:T(8,128)S(1)}, u32[]{:S(2)}, u32[]{:S(2)}) collective-permute-start(f32[136,128]{1,0:T(8,128)S(1)} %add.95), channel_id=1, source_target_pairs={{0,1},{1,0},{2,3},{3,2},{4,132},{5,133},{6,134},{7,135},{8,9},{9,8... | collective-permute-start | bytes 208904 | tf_op jit(solution)/shard_map/sum_y/ppermute | solution.py:269
  87.6 4.4 %collective-permute-start.29 = (f32[136,128]{1,0:T(8,128)S(1)}, f32[136,128]{1,0:T(8,128)S(1)}, u32[]{:S(2)}, u32[]{:S(2)}) collective-permute-start(f32[136,128]{1,0:T(8,128)S(1)} %add.95), channel_id=1, source_target_pairs={{0,1},{1,0},{2,3},{3,2},{4,196},{5,197},{6,198},{7,199},{8,9},{9,8... | collective-permute-start | bytes 208904 | tf_op jit(solution)/shard_map/sum_y/ppermute | solution.py:269
  88.3 3.7 %collective-permute-start.28 = (f32[136,128]{1,0:T(8,128)S(1)}, f32[136,128]{1,0:T(8,128)S(1)}, u32[]{:S(2)}, u32[]{:S(2)}) collective-permute-start(f32[136,128]{1,0:T(8,128)S(1)} %add.95), channel_id=1, source_target_pairs={{0,1},{1,0},{2,3},{3,2},{4,68},{5,69},{6,70},{7,71},{8,9},{9,8},{1... | collective-permute-start | bytes 208904 | tf_op jit(solution)/shard_map/sum_y/ppermute | solution.py:269
  92.0 4.9 %collective-permute-start.33 = (f32[136,128]{1,0:T(8,128)S(1)}, f32[136,128]{1,0:T(8,128)S(1)}, u32[]{:S(2)}, u32[]{:S(2)}) collective-permute-start(f32[136,128]{1,0:T(8,128)S(1)} %add_add_fusion.1), channel_id=1, source_target_pairs={{0,1},{1,0},{2,3},{3,2},{4,20},{5,21},{6,22},{7,23},{8,9},{9,8},{1... | collective-permute-start | bytes 208904 | tf_op jit(solution)/shard_map/sum_z_inner/ppermute | solution.py:269
  93.2 5.1 %collective-permute-start.32 = (f32[136,128]{1,0:T(8,128)S(1)}, f32[136,128]{1,0:T(8,128)S(1)}, u32[]{:S(2)}, u32[]{:S(2)}) collective-permute-start(f32[136,128]{1,0:T(8,128)S(1)} %add_add_fusion.1), channel_id=1, source_target_pairs={{0,1},{1,0},{2,3},{3,2},{4,28},{5,29},{6,30},{7,31},{8,9},{9,8},{1... | collective-permute-start | bytes 208904 | tf_op jit(solution)/shard_map/sum_z_inner/ppermute | solution.py:269
  94.8 3.9 %collective-permute-start.31 = (f32[136,128]{1,0:T(8,128)S(1)}, f32[136,128]{1,0:T(8,128)S(1)}, u32[]{:S(2)}, u32[]{:S(2)}) collective-permute-start(f32[136,128]{1,0:T(8,128)S(1)} %add_add_fusion.1), channel_id=1, source_target_pairs={{0,1},{1,0},{2,3},{3,2},{4,12},{5,13},{6,14},{7,15},{8,9},{9,8},{1... | collective-permute-start | bytes 208904 | tf_op jit(solution)/shard_map/sum_z_inner/ppermute | solution.py:269
  98.7 5.4 %collective-permute-start.34 = (f32[136,128]{1,0:T(8,128)S(1)}, f32[136,128]{1,0:T(8,128)S(1)}, u32[]{:S(2)}, u32[]{:S(2)}) collective-permute-start(f32[136,128]{1,0:T(8,128)S(1)} %add_add_fusion), channel_id=1, source_target_pairs={{0,1},{1,0},{2,3},{3,2},{4,52},{5,53},{6,54},{7,55},{8,9},{9,8},{1... | collective-permute-start | bytes 208904 | tf_op jit(solution)/shard_map/sum_z_outer/ppermute | solution.py:269
  104.2 7.5 %collective-permute-start.35 = (f32[136,128]{1,0:T(8,128)S(1)}, f32[136,128]{1,0:T(8,128)S(1)}, u32[]{:S(2)}, u32[]{:S(2)}) collective-permute-start(f32[136,128]{1,0:T(8,128)S(1)} %constant_dynamic-update-slice_fusion.state_own), channel_id=1, source_target_pairs={{0,4},{1,5},{2,6},{3,7},{4,0},{5,1},{6,2},{7,3},{8,12},{9,13},{10,... | collective-permute-start | bytes 208904 | tf_op jit(solution)/shard_map/back_core/ppermute | solution.py:269
  104.5 4.0 %collective-permute-start.38 = (f32[8,128]{1,0:T(8,128)S(1)}, f32[8,128]{1,0:T(8,128)S(1)}, u32[]{:S(2)}, u32[]{:S(2)}) collective-permute-start(f32[8,128]{1,0:T(8,128)S(1)} %get-tuple-element.74.last_0), channel_id=1, source_target_pairs={{0,64},{1,65},{2,66},{3,67},{4,6},{5,7},{6,4},{7,5},{8,72},{9,73},... | collective-permute-start | bytes 12296 | tf_op jit(solution)/shard_map/sum_req_last/ppermute | solution.py:269
  106.6 3.7 %collective-permute-start.37 = (f32[8,128]{1,0:T(8,128)S(1)}, f32[8,128]{1,0:T(8,128)S(1)}, u32[]{:S(2)}, u32[]{:S(2)}) collective-permute-start(f32[8,128]{1,0:T(8,128)S(1)} %get-tuple-element.74.last_0), channel_id=1, source_target_pairs={{0,64},{1,65},{2,66},{3,67},{4,7},{5,6},{6,5},{7,4},{8,72},{9,73},... | collective-permute-start | bytes 12296 | tf_op jit(solution)/shard_map/sum_req_last/ppermute | solution.py:269
  (16 other events, 111.8 us)
where the time goes:
time: 113 us; the launch traced here: 112 us
  starting transfers between devices  48.9 us (43%)
  waiting for transfers between devices  44.7 us (40%)
  Pallas kernels  12.8 us (11%)
  between operations  2.79 us (2%)
  local copies, waits for them, and re-layouts  2.32 us (2%)
    ppermute x31, waiting for transfers between devices, on_mesh(): return lax.ppermute(x, ('tst', 'req'), pairs)  38.7 us
    ppermute x31, starting transfers between devices, on_mesh(): return lax.ppermute(x, ('tst', 'req'), pairs)  38.2 us
    ppermute x9, starting transfers between devices, on_req(): lax.ppermute(x, 'req', [(i, i ^ bit) for i in range(n_req)])  10.7 us
    ppermute x9, waiting for transfers between devices, on_req(): lax.ppermute(x, 'req', [(i, i ^ bit) for i in range(n_req)])  5.93 us
    pallas_call x3, Pallas kernels, per_device(): call(functools.partial(primal_load_kernel, iteration), (load_shape, big_t...  5.59 us
    pallas_call x1, Pallas kernels, per_device(): call(first_pull_kernel, (pull_shape, struct(slots, req_blocks, dtype=BF16...  2.98 us
  transfers between devices with their start and end apart: 40, of which 31 were waited for; matrix products, arithmetic and copies ran while one was open for 1% of the time, Pallas kernels for 1%

commit v1 on v0

--- a/solution.py
+++ b/solution.py
@@ -184,18 +184,22 @@
     groups = slots // GROUP
     tiles, refs = refs[:groups], refs[groups:]
     sum_primal = refs.pop(0) if iteration > 0 else None
-    load_out, primal_out, sum_out, sq_out = refs
+    load_out, primal_out, *refs = refs
+    sum_out = refs.pop(0) if iteration < ITERS - 1 else None
+    sq_out = refs.pop(0) if iteration > 0 else None
     test_blocks = primal.shape[0]
     parts = (pull_own, pull_1, pull_2, pull_3)
     pull = sum_four(parts, slice(0, test_blocks))
-    sq_out[...] = sum_four(parts, slice(test_blocks, test_blocks + STAT_ROWS))
+    if sq_out is not None:
+        sq_out[...] = sum_four(parts, slice(test_blocks, test_blocks + STAT_ROWS))
     old = primal[...]
     new = jnp.clip(old - step_primal * (costs[...] - pull + scal[0:1, :] * runtimes[...]), 0.0, 1.0)
     extrap = (2.0 * new - old).astype(BF16).astype(F32)
     total = new if sum_primal is None else sum_primal[...] + new
     primal_next, total_next = average(params, iteration, total, new)
     primal_out[...] = primal_next
-    sum_out[...] = total_next
+    if sum_out is not None:
+        sum_out[...] = total_next
     padded = jnp.concatenate([extrap, jnp.zeros((slots - test_blocks, LANES), F32)], axis=0)
     picked = gather_rows(pick_cols[...], padded)
     contrib = [load_group(picked, tiles, group) for group in range(groups)]
@@ -323,7 +327,7 @@
                 [HBM] * len(given),
                 [pltpu.VMEM((rest, *group_shape.shape), BF16), *[pltpu.VMEM(x.shape, x.dtype) for x in given[1:]]]
                 + [pltpu.SemaphoreType.DMA((n,)) for n in (len(given) - 1, slots // GROUP)],
-            )(*given)
+            )(*[pltpu.with_memory_space_constraint(x, pltpu.HBM) for x in given[:4]], given[4])
             tiles += call(
                 rest_kernel, [group_shape] * rest, [HBM, VMEM], [pltpu.SemaphoreType.DMA((rest,))]
             )(coverage_tiles, pick_cols)
@@ -338,12 +342,12 @@
         with jax.named_scope("sum_req"):
             parts = [pull, *on_req(pull)]
         given = (*parts, params, pick_cols, place_rows, primal, scal, costs, runs, *tiles, *sum_primal)
-        load, primal, total, sq = call(
-            functools.partial(primal_load_kernel, iteration), (load_shape, big_t, big_t, small), [VMEM] * len(given)
-        )(*given)
-        sum_primal = (total,)
+        outs = (load_shape, big_t) + (big_t,) * (iteration < ITERS - 1) + (small,) * (iteration > 0)
+        load, primal, *more = call(functools.partial(primal_load_kernel, iteration), outs, [VMEM] * len(given))(*given)
+        if iteration < ITERS - 1:
+            sum_primal = (more.pop(0),)
         if iteration > 0:
-            sq_list.append(sq)
+            sq_list.append(more.pop(0))
         summed = total_tst(load)
         if iteration < ITERS - 1:
             summed = hand_on(summed)

time: 113 us -> 111 us (0.982)
  local copies, waits for them, and re-layouts: 2.32 us -> 0.18 us
    unnamed x17 -> x11, local copies, waits for them, and re-layouts: 2.17 us -> 0.03 us
where the time goes in v1:
time: 111 us
  starting transfers between devices  48.9 us (44%)
  waiting for transfers between devices  44.7 us (40%)
  Pallas kernels  13.4 us (12%)
  between operations  2.8 us (3%)
    ppermute x31, waiting for transfers between devices, on_mesh(): return lax.ppermute(x, ('tst', 'req'), pairs)  38.7 us
    ppermute x31, starting transfers between devices, on_mesh(): return lax.ppermute(x, ('tst', 'req'), pairs)  38.3 us
    ppermute x9, starting transfers between devices, on_req(): lax.ppermute(x, 'req', [(i, i ^ bit) for i in range(n_req)])  10.7 us
    ppermute x9, waiting for transfers between devices, on_req(): lax.ppermute(x, 'req', [(i, i ^ bit) for i in range(n_req)])  5.93 us
    pallas_call x3, Pallas kernels, per_device(): call(functools.partial(primal_load_kernel, iteration), outs, [VMEM] * len...  5.11 us
    pallas_call x1, Pallas kernels, per_device(): call(first_pull_kernel, (pull_shape, struct(slots, req_blocks, dtype=BF16...  4.07 us
  transfers between devices with their start and end apart: 40, of which 31 were waited for; matrix products, arithmetic and copies ran while one was open for 1% of the time, Pallas kernels for 1%

profile of v1, /device:TPU:1, one launch (start us, length us, event | category | flops | bytes accessed | tf_op | source)
XLA Modules:
  0.0 110.9 jit_solution(1600394132053473878)
XLA Ops:
  1.3 4.1 %shard_map.147 = (f32[72,128]{1,0:T(8,128)S(1)}, bf16[128,128]{1,0:T(8,128)(2,1)S(1)}, f32[128,128]{1,0:T(8,128)S(1)}, bf16[128,128]{1,0:T(8,128)(2,1)S(1)}, f32...) custom-call(bf16[128,128,128]{2,1,0:T(8,128)(2,1)} %tiles_in.3, ...), custom_call_target="tpu_custom_call" | custom-call | tf_op jit(solution)/shard_map/pallas_call | solution.py:320
  5.4 3.7 %collective-permute-start.2 = (f32[72,128]{1,0:T(8,128)S(1)}, f32[72,128]{1,0:T(8,128)S(1)}, u32[]{:S(2)}, u32[]{:S(2)}) collective-permute-start(f32[72,128]{1,0:T(8,128)S(1)} %get-tuple-element.41.refs_0_), channel_id=1, source_target_pairs={{0,2},{1,3},{2,0},{3,1},{4,6},{5,7},{6,4},{7,5},{8,10},{9,11},{10,... | collective-permute-start | bytes 110600 | tf_op jit(solution)/shard_map/sum_req/ppermute | solution.py:282
  13.5 1.6 %shard_map.149 = (f32[136,128]{1,0:T(8,128)S(1)}, f32[64,128]{1,0:T(8,128)S(1)}, f32[64,128]{1,0:T(8,128)S(1)}) custom-call(f32[72,128]{1,0:T(8,128)S(1)} %get-tuple-element.41.refs_0_, f32[72,128]{1,0:T(8,128)S(1)} %collective-permute-done.refs_1_, f32[72,128]{1,0:T(8,128)S(1)} %collective-permute-done.1.refs_2_, ...), custom_call_target="tpu_custom_call" | custom-call | tf_op jit(solution)/shard_map/pallas_call | solution.py:346
  15.1 2.3 %collective-permute-start.3 = (f32[136,128]{1,0:T(8,128)S(1)}, f32[136,128]{1,0:T(8,128)S(1)}, u32[]{:S(2)}, u32[]{:S(2)}) collective-permute-start(f32[136,128]{1,0:T(8,128)S(1)} %get-tuple-element.52), channel_id=1, source_target_pairs={{0,4},{1,5},{2,6},{3,7},{4,0},{5,1},{6,2},{7,3},{8,12},{9,13},{10,... | collective-permute-start | bytes 208904 | tf_op jit(solution)/shard_map/sum_core/ppermute | solution.py:273
  18.3 2.6 %collective-permute-start.6 = (f32[136,128]{1,0:T(8,128)S(1)}, f32[136,128]{1,0:T(8,128)S(1)}, u32[]{:S(2)}, u32[]{:S(2)}) collective-permute-start(f32[136,128]{1,0:T(8,128)S(1)} %add.79), channel_id=1, source_target_pairs={{0,1},{1,0},{2,3},{3,2},{4,132},{5,133},{6,134},{7,135},{8,9},{9,8... | collective-permute-start | bytes 208904 | tf_op jit(solution)/shard_map/sum_y/ppermute | solution.py:273
  23.0 2.2 %collective-permute-done.5 = f32[136,128]{1,0:T(8,128)S(1)} collective-permute-done((f32[136,128]{1,0:T(8,128)S(1)}, f32[136,128]{1,0:T(8,128)S(1)}, u32[]{:S(2)}, u32[]{:S(2)}) %collective-permute-start.5) | collective-permute-done | bytes 69664 | tf_op jit(solution)/shard_map/sum_y/ppermute | solution.py:273
  25.3 3.1 %collective-permute-start.9 = (f32[136,128]{1,0:T(8,128)S(1)}, f32[136,128]{1,0:T(8,128)S(1)}, u32[]{:S(2)}, u32[]{:S(2)}) collective-permute-start(f32[136,128]{1,0:T(8,128)S(1)} %add_add_fusion.5), channel_id=1, source_target_pairs={{0,1},{1,0},{2,3},{3,2},{4,20},{5,21},{6,22},{7,23},{8,9},{9,8},{1... | collective-permute-start | bytes 208904 | tf_op jit(solution)/shard_map/sum_z_inner/ppermute | solution.py:273
  30.1 3.4 %collective-permute-done.8 = f32[136,128]{1,0:T(8,128)S(1)} collective-permute-done((f32[136,128]{1,0:T(8,128)S(1)}, f32[136,128]{1,0:T(8,128)S(1)}, u32[]{:S(2)}, u32[]{:S(2)}) %collective-permute-start.8) | collective-permute-done | bytes 69664 | tf_op jit(solution)/shard_map/sum_z_inner/ppermute | solution.py:273
  33.7 3.7 %collective-permute-start.10 = (f32[136,128]{1,0:T(8,128)S(1)}, f32[136,128]{1,0:T(8,128)S(1)}, u32[]{:S(2)}, u32[]{:S(2)}) collective-permute-start(f32[136,128]{1,0:T(8,128)S(1)} %add_add_fusion.4), channel_id=1, source_target_pairs={{0,1},{1,0},{2,3},{3,2},{4,52},{5,53},{6,54},{7,55},{8,9},{9,8},{1... | collective-permute-start | bytes 208904 | tf_op jit(solution)/shard_map/sum_z_outer/ppermute | solution.py:273
  37.5 1.7 %collective-permute-done.10 = f32[136,128]{1,0:T(8,128)S(1)} collective-permute-done((f32[136,128]{1,0:T(8,128)S(1)}, f32[136,128]{1,0:T(8,128)S(1)}, u32[]{:S(2)}, u32[]{:S(2)}) %collective-permute-start.10) | collective-permute-done | bytes 69664 | tf_op jit(solution)/shard_map/sum_z_outer/ppermute | solution.py:273
  41.7 2.6 %collective-permute-start.14 = (f32[72,128]{1,0:T(8,128)S(1)}, f32[72,128]{1,0:T(8,128)S(1)}, u32[]{:S(2)}, u32[]{:S(2)}) collective-permute-start(f32[72,128]{1,0:T(8,128)S(1)} %get-tuple-element.55.refs_0_), channel_id=1, source_target_pairs={{0,2},{1,3},{2,0},{3,1},{4,6},{5,7},{6,4},{7,5},{8,10},{9,11},{10,... | collective-permute-start | bytes 110600 | tf_op jit(solution)/shard_map/sum_req/ppermute | solution.py:282
  46.0 2.3 %collective-permute-done.13.refs_2_ = f32[72,128]{1,0:T(8,128)S(1)} collective-permute-done((f32[72,128]{1,0:T(8,128)S(1)}, f32[72,128]{1,0:T(8,128)S(1)}, u32[]{:S(2)}, u32[]{:S(2)}) %collective-permute-start.13) | collective-permute-done | bytes 36896 | tf_op jit(solution)/shard_map/sum_req/ppermute | solution.py:282
  48.3 1.6 %shard_map.151 = (f32[136,128]{1,0:T(8,128)S(1)}, f32[64,128]{1,0:T(8,128)S(1)}, f32[64,128]{1,0:T(8,128)S(1)}, f32[8,128]{1,0:T(8,128)S(1)}) custom-call(f32[72,128]{1,0:T(8,128)S(1)} %get-tuple-element.55.refs_0_, f32[72,128]{1,0:T(8,128)S(1)} %collective-permute-done.12.refs_1_, f32[72,128]{1,0:T(8,128)S(1)} %collective-permute-done.13.refs_2_, ...), custom_call_target="tpu_custom_call" | custom-call | tf_op jit(solution)/shard_map/pallas_call | solution.py:346
  49.9 1.9 %collective-permute-start.15 = (f32[136,128]{1,0:T(8,128)S(1)}, f32[136,128]{1,0:T(8,128)S(1)}, u32[]{:S(2)}, u32[]{:S(2)}) collective-permute-start(f32[136,128]{1,0:T(8,128)S(1)} %get-tuple-element.59), channel_id=1, source_target_pairs={{0,4},{1,5},{2,6},{3,7},{4,0},{5,1},{6,2},{7,3},{8,12},{9,13},{10,... | collective-permute-start | bytes 208904 | tf_op jit(solution)/shard_map/sum_core/ppermute | solution.py:273
  52.7 1.9 %collective-permute-start.18 = (f32[136,128]{1,0:T(8,128)S(1)}, f32[136,128]{1,0:T(8,128)S(1)}, u32[]{:S(2)}, u32[]{:S(2)}) collective-permute-start(f32[136,128]{1,0:T(8,128)S(1)} %add.87), channel_id=1, source_target_pairs={{0,1},{1,0},{2,3},{3,2},{4,132},{5,133},{6,134},{7,135},{8,9},{9,8... | collective-permute-start | bytes 208904 | tf_op jit(solution)/shard_map/sum_y/ppermute | solution.py:273
  55.4 2.0 %collective-permute-done.18 = f32[136,128]{1,0:T(8,128)S(1)} collective-permute-done((f32[136,128]{1,0:T(8,128)S(1)}, f32[136,128]{1,0:T(8,128)S(1)}, u32[]{:S(2)}, u32[]{:S(2)}) %collective-permute-start.18) | collective-permute-done | bytes 69664 | tf_op jit(solution)/shard_map/sum_y/ppermute | solution.py:273
  57.4 1.5 %collective-permute-done.17 = f32[136,128]{1,0:T(8,128)S(1)} collective-permute-done((f32[136,128]{1,0:T(8,128)S(1)}, f32[136,128]{1,0:T(8,128)S(1)}, u32[]{:S(2)}, u32[]{:S(2)}) %collective-permute-start.17) | collective-permute-done | bytes 69664 | tf_op jit(solution)/shard_map/sum_y/ppermute | solution.py:273
  59.0 2.4 %collective-permute-start.21 = (f32[136,128]{1,0:T(8,128)S(1)}, f32[136,128]{1,0:T(8,128)S(1)}, u32[]{:S(2)}, u32[]{:S(2)}) collective-permute-start(f32[136,128]{1,0:T(8,128)S(1)} %add_add_fusion.3), channel_id=1, source_target_pairs={{0,1},{1,0},{2,3},{3,2},{4,20},{5,21},{6,22},{7,23},{8,9},{9,8},{1... | collective-permute-start | bytes 208904 | tf_op jit(solution)/shard_map/sum_z_inner/ppermute | solution.py:273
  61.4 1.6 %collective-permute-start.20 = (f32[136,128]{1,0:T(8,128)S(1)}, f32[136,128]{1,0:T(8,128)S(1)}, u32[]{:S(2)}, u32[]{:S(2)}) collective-permute-start(f32[136,128]{1,0:T(8,128)S(1)} %add_add_fusion.3), channel_id=1, source_target_pairs={{0,1},{1,0},{2,3},{3,2},{4,28},{5,29},{6,30},{7,31},{8,9},{9,8},{1... | collective-permute-start | bytes 208904 | tf_op jit(solution)/shard_map/sum_z_inner/ppermute | solution.py:273
  63.1 3.4 %collective-permute-done.20 = f32[136,128]{1,0:T(8,128)S(1)} collective-permute-done((f32[136,128]{1,0:T(8,128)S(1)}, f32[136,128]{1,0:T(8,128)S(1)}, u32[]{:S(2)}, u32[]{:S(2)}) %collective-permute-start.20) | collective-permute-done | bytes 69664 | tf_op jit(solution)/shard_map/sum_z_inner/ppermute | solution.py:273
  66.9 2.2 %collective-permute-start.22 = (f32[136,128]{1,0:T(8,128)S(1)}, f32[136,128]{1,0:T(8,128)S(1)}, u32[]{:S(2)}, u32[]{:S(2)}) collective-permute-start(f32[136,128]{1,0:T(8,128)S(1)} %add_add_fusion.2), channel_id=1, source_target_pairs={{0,1},{1,0},{2,3},{3,2},{4,52},{5,53},{6,54},{7,55},{8,9},{9,8},{1... | collective-permute-start | bytes 208904 | tf_op jit(solution)/shard_map/sum_z_outer/ppermute | solution.py:273
  69.1 3.1 %collective-permute-done.22 = f32[136,128]{1,0:T(8,128)S(1)} collective-permute-done((f32[136,128]{1,0:T(8,128)S(1)}, f32[136,128]{1,0:T(8,128)S(1)}, u32[]{:S(2)}, u32[]{:S(2)}) %collective-permute-start.22) | collective-permute-done | bytes 69664 | tf_op jit(solution)/shard_map/sum_z_outer/ppermute | solution.py:273
  77.4 1.7 %collective-permute-done.26.refs_3_ = f32[72,128]{1,0:T(8,128)S(1)} collective-permute-done((f32[72,128]{1,0:T(8,128)S(1)}, f32[72,128]{1,0:T(8,128)S(1)}, u32[]{:S(2)}, u32[]{:S(2)}) %collective-permute-start.26) | collective-permute-done | bytes 36896 | tf_op jit(solution)/shard_map/sum_req/ppermute | solution.py:282
  80.0 2.0 %shard_map.153 = (f32[136,128]{1,0:T(8,128)S(1)}, f32[64,128]{1,0:T(8,128)}, f32[8,128]{1,0:T(8,128)S(1)}) custom-call(f32[72,128]{1,0:T(8,128)S(1)} %get-tuple-element.62.refs_0_, f32[72,128]{1,0:T(8,128)S(1)} %collective-permute-done.24.refs_1_, f32[72,128]{1,0:T(8,128)S(1)} %collective-permute-done.25.refs_2_, ...), custom_call_target="tpu_custom_call" | custom-call | tf_op jit(solution)/shard_map/pallas_call | solution.py:346
  84.4 1.8 %collective-permute-start.30 = (f32[136,128]{1,0:T(8,128)S(1)}, f32[136,128]{1,0:T(8,128)S(1)}, u32[]{:S(2)}, u32[]{:S(2)}) collective-permute-start(f32[136,128]{1,0:T(8,128)S(1)} %add.95), channel_id=1, source_target_pairs={{0,1},{1,0},{2,3},{3,2},{4,132},{5,133},{6,134},{7,135},{8,9},{9,8... | collective-permute-start | bytes 208904 | tf_op jit(solution)/shard_map/sum_y/ppermute | solution.py:273
  87.1 2.0 %collective-permute-done.30 = f32[136,128]{1,0:T(8,128)S(1)} collective-permute-done((f32[136,128]{1,0:T(8,128)S(1)}, f32[136,128]{1,0:T(8,128)S(1)}, u32[]{:S(2)}, u32[]{:S(2)}) %collective-permute-start.30) | collective-permute-done | bytes 69664 | tf_op jit(solution)/shard_map/sum_y/ppermute | solution.py:273
  91.7 1.6 %collective-permute-start.32 = (f32[136,128]{1,0:T(8,128)S(1)}, f32[136,128]{1,0:T(8,128)S(1)}, u32[]{:S(2)}, u32[]{:S(2)}) collective-permute-start(f32[136,128]{1,0:T(8,128)S(1)} %add_add_fusion.1), channel_id=1, source_target_pairs={{0,1},{1,0},{2,3},{3,2},{4,28},{5,29},{6,30},{7,31},{8,9},{9,8},{1... | collective-permute-start | bytes 208904 | tf_op jit(solution)/shard_map/sum_z_inner/ppermute | solution.py:273
  93.3 2.1 %collective-permute-done.33 = f32[136,128]{1,0:T(8,128)S(1)} collective-permute-done((f32[136,128]{1,0:T(8,128)S(1)}, f32[136,128]{1,0:T(8,128)S(1)}, u32[]{:S(2)}, u32[]{:S(2)}) %collective-permute-start.33) | collective-permute-done | bytes 69664 | tf_op jit(solution)/shard_map/sum_z_inner/ppermute | solution.py:273
  97.3 2.3 %collective-permute-start.34 = (f32[136,128]{1,0:T(8,128)S(1)}, f32[136,128]{1,0:T(8,128)S(1)}, u32[]{:S(2)}, u32[]{:S(2)}) collective-permute-start(f32[136,128]{1,0:T(8,128)S(1)} %add_add_fusion), channel_id=1, source_target_pairs={{0,1},{1,0},{2,3},{3,2},{4,52},{5,53},{6,54},{7,55},{8,9},{9,8},{1... | collective-permute-start | bytes 208904 | tf_op jit(solution)/shard_map/sum_z_outer/ppermute | solution.py:273
  99.6 3.0 %collective-permute-done.34 = f32[136,128]{1,0:T(8,128)S(1)} collective-permute-done((f32[136,128]{1,0:T(8,128)S(1)}, f32[136,128]{1,0:T(8,128)S(1)}, u32[]{:S(2)}, u32[]{:S(2)}) %collective-permute-start.34) | collective-permute-done | bytes 69664 | tf_op jit(solution)/shard_map/sum_z_outer/ppermute | solution.py:273
  103.1 2.1 %collective-permute-start.38 = (f32[8,128]{1,0:T(8,128)S(1)}, f32[8,128]{1,0:T(8,128)S(1)}, u32[]{:S(2)}, u32[]{:S(2)}) collective-permute-start(f32[8,128]{1,0:T(8,128)S(1)} %get-tuple-element.74.last_0), channel_id=1, source_target_pairs={{0,64},{1,65},{2,66},{3,67},{4,6},{5,7},{6,4},{7,5},{8,72},{9,73},... | collective-permute-start | bytes 12296 | tf_op jit(solution)/shard_map/sum_req_last/ppermute | solution.py:273
  107.1 1.7 %collective-permute-done.37.last_2 = f32[8,128]{1,0:T(8,128)S(1)} collective-permute-done((f32[8,128]{1,0:T(8,128)S(1)}, f32[8,128]{1,0:T(8,128)S(1)}, u32[]{:S(2)}, u32[]{:S(2)}) %collective-permute-start.37) | collective-permute-done | bytes 4128 | tf_op jit(solution)/shard_map/sum_req_last/ppermute | solution.py:273
  (90 shorter events, 32.9 us)
Async XLA Ops:
  5.4 7.9 %collective-permute-start.2 = (f32[72,128]{1,0:T(8,128)S(1)}, f32[72,128]{1,0:T(8,128)S(1)}, u32[]{:S(2)}, u32[]{:S(2)}) collective-permute-start(f32[72,128]{1,0:T(8,128)S(1)} %get-tuple-element.41.refs_0_), channel_id=1, source_target_pairs={{0,2},{1,3},{2,0},{3,1},{4,6},{5,7},{6,4},{7,5},{8,10},{9,11},{10,... | collective-permute-start | bytes 110600 | tf_op jit(solution)/shard_map/sum_req/ppermute | solution.py:282
  9.0 4.3 %collective-permute-start.1 = (f32[72,128]{1,0:T(8,128)S(1)}, f32[72,128]{1,0:T(8,128)S(1)}, u32[]{:S(2)}, u32[]{:S(2)}) collective-permute-start(f32[72,128]{1,0:T(8,128)S(1)} %get-tuple-element.41.refs_0_), channel_id=1, source_target_pairs={{0,3},{1,2},{2,1},{3,0},{4,7},{5,6},{6,5},{7,4},{8,11},{9,10},{10,... | collective-permute-start | bytes 110600 | tf_op jit(solution)/shard_map/sum_req/ppermute | solution.py:282
  9.9 3.5 %collective-permute-start = (f32[72,128]{1,0:T(8,128)S(1)}, f32[72,128]{1,0:T(8,128)S(1)}, u32[]{:S(2)}, u32[]{:S(2)}) collective-permute-start(f32[72,128]{1,0:T(8,128)S(1)} %get-tuple-element.41.refs_0_), channel_id=1, source_target_pairs={{0,1},{1,0},{2,3},{3,2},{4,5},{5,4},{6,7},{7,6},{8,9},{9,8},{10,11... | collective-permute-start | bytes 110600 | tf_op jit(solution)/shard_map/sum_req/ppermute | solution.py:282
  18.3 4.8 %collective-permute-start.6 = (f32[136,128]{1,0:T(8,128)S(1)}, f32[136,128]{1,0:T(8,128)S(1)}, u32[]{:S(2)}, u32[]{:S(2)}) collective-permute-start(f32[136,128]{1,0:T(8,128)S(1)} %add.79), channel_id=1, source_target_pairs={{0,1},{1,0},{2,3},{3,2},{4,132},{5,133},{6,134},{7,135},{8,9},{9,8... | collective-permute-start | bytes 208904 | tf_op jit(solution)/shard_map/sum_y/ppermute | solution.py:273
  20.9 4.4 %collective-permute-start.5 = (f32[136,128]{1,0:T(8,128)S(1)}, f32[136,128]{1,0:T(8,128)S(1)}, u32[]{:S(2)}, u32[]{:S(2)}) collective-permute-start(f32[136,128]{1,0:T(8,128)S(1)} %add.79), channel_id=1, source_target_pairs={{0,1},{1,0},{2,3},{3,2},{4,196},{5,197},{6,198},{7,199},{8,9},{9,8... | collective-permute-start | bytes 208904 | tf_op jit(solution)/shard_map/sum_y/ppermute | solution.py:273
  21.7 3.6 %collective-permute-start.4 = (f32[136,128]{1,0:T(8,128)S(1)}, f32[136,128]{1,0:T(8,128)S(1)}, u32[]{:S(2)}, u32[]{:S(2)}) collective-permute-start(f32[136,128]{1,0:T(8,128)S(1)} %add.79), channel_id=1, source_target_pairs={{0,1},{1,0},{2,3},{3,2},{4,68},{5,69},{6,70},{7,71},{8,9},{9,8},{1... | collective-permute-start | bytes 208904 | tf_op jit(solution)/shard_map/sum_y/ppermute | solution.py:273
  25.3 4.8 %collective-permute-start.9 = (f32[136,128]{1,0:T(8,128)S(1)}, f32[136,128]{1,0:T(8,128)S(1)}, u32[]{:S(2)}, u32[]{:S(2)}) collective-permute-start(f32[136,128]{1,0:T(8,128)S(1)} %add_add_fusion.5), channel_id=1, source_target_pairs={{0,1},{1,0},{2,3},{3,2},{4,20},{5,21},{6,22},{7,23},{8,9},{9,8},{1... | collective-permute-start | bytes 208904 | tf_op jit(solution)/shard_map/sum_z_inner/ppermute | solution.py:273
  28.4 5.1 %collective-permute-start.8 = (f32[136,128]{1,0:T(8,128)S(1)}, f32[136,128]{1,0:T(8,128)S(1)}, u32[]{:S(2)}, u32[]{:S(2)}) collective-permute-start(f32[136,128]{1,0:T(8,128)S(1)} %add_add_fusion.5), channel_id=1, source_target_pairs={{0,1},{1,0},{2,3},{3,2},{4,28},{5,29},{6,30},{7,31},{8,9},{9,8},{1... | collective-permute-start | bytes 208904 | tf_op jit(solution)/shard_map/sum_z_inner/ppermute | solution.py:273
  29.8 3.9 %collective-permute-start.7 = (f32[136,128]{1,0:T(8,128)S(1)}, f32[136,128]{1,0:T(8,128)S(1)}, u32[]{:S(2)}, u32[]{:S(2)}) collective-permute-start(f32[136,128]{1,0:T(8,128)S(1)} %add_add_fusion.5), channel_id=1, source_target_pairs={{0,1},{1,0},{2,3},{3,2},{4,12},{5,13},{6,14},{7,15},{8,9},{9,8},{1... | collective-permute-start | bytes 208904 | tf_op jit(solution)/shard_map/sum_z_inner/ppermute | solution.py:273
  33.7 5.5 %collective-permute-start.10 = (f32[136,128]{1,0:T(8,128)S(1)}, f32[136,128]{1,0:T(8,128)S(1)}, u32[]{:S(2)}, u32[]{:S(2)}) collective-permute-start(f32[136,128]{1,0:T(8,128)S(1)} %add_add_fusion.4), channel_id=1, source_target_pairs={{0,1},{1,0},{2,3},{3,2},{4,52},{5,53},{6,54},{7,55},{8,9},{9,8},{1... | collective-permute-start | bytes 208904 | tf_op jit(solution)/shard_map/sum_z_outer/ppermute | solution.py:273
  41.7 4.3 %collective-permute-start.14 = (f32[72,128]{1,0:T(8,128)S(1)}, f32[72,128]{1,0:T(8,128)S(1)}, u32[]{:S(2)}, u32[]{:S(2)}) collective-permute-start(f32[72,128]{1,0:T(8,128)S(1)} %get-tuple-element.55.refs_0_), channel_id=1, source_target_pairs={{0,2},{1,3},{2,0},{3,1},{4,6},{5,7},{6,4},{7,5},{8,10},{9,11},{10,... | collective-permute-start | bytes 110600 | tf_op jit(solution)/shard_map/sum_req/ppermute | solution.py:282
  44.3 4.0 %collective-permute-start.13 = (f32[72,128]{1,0:T(8,128)S(1)}, f32[72,128]{1,0:T(8,128)S(1)}, u32[]{:S(2)}, u32[]{:S(2)}) collective-permute-start(f32[72,128]{1,0:T(8,128)S(1)} %get-tuple-element.55.refs_0_), channel_id=1, source_target_pairs={{0,3},{1,2},{2,1},{3,0},{4,7},{5,6},{6,5},{7,4},{8,11},{9,10},{10,... | collective-permute-start | bytes 110600 | tf_op jit(solution)/shard_map/sum_req/ppermute | solution.py:282
  52.7 4.8 %collective-permute-start.18 = (f32[136,128]{1,0:T(8,128)S(1)}, f32[136,128]{1,0:T(8,128)S(1)}, u32[]{:S(2)}, u32[]{:S(2)}) collective-permute-start(f32[136,128]{1,0:T(8,128)S(1)} %add.87), channel_id=1, source_target_pairs={{0,1},{1,0},{2,3},{3,2},{4,132},{5,133},{6,134},{7,135},{8,9},{9,8... | collective-permute-start | bytes 208904 | tf_op jit(solution)/shard_map/sum_y/ppermute | solution.py:273
  54.6 4.4 %collective-permute-start.17 = (f32[136,128]{1,0:T(8,128)S(1)}, f32[136,128]{1,0:T(8,128)S(1)}, u32[]{:S(2)}, u32[]{:S(2)}) collective-permute-start(f32[136,128]{1,0:T(8,128)S(1)} %add.87), channel_id=1, source_target_pairs={{0,1},{1,0},{2,3},{3,2},{4,196},{5,197},{6,198},{7,199},{8,9},{9,8... | collective-permute-start | bytes 208904 | tf_op jit(solution)/shard_map/sum_y/ppermute | solution.py:273
  55.3 3.6 %collective-permute-start.16 = (f32[136,128]{1,0:T(8,128)S(1)}, f32[136,128]{1,0:T(8,128)S(1)}, u32[]{:S(2)}, u32[]{:S(2)}) collective-permute-start(f32[136,128]{1,0:T(8,128)S(1)} %add.87), channel_id=1, source_target_pairs={{0,1},{1,0},{2,3},{3,2},{4,68},{5,69},{6,70},{7,71},{8,9},{9,8},{1... | collective-permute-start | bytes 208904 | tf_op jit(solution)/shard_map/sum_y/ppermute | solution.py:273
  59.0 4.1 %collective-permute-start.21 = (f32[136,128]{1,0:T(8,128)S(1)}, f32[136,128]{1,0:T(8,128)S(1)}, u32[]{:S(2)}, u32[]{:S(2)}) collective-permute-start(f32[136,128]{1,0:T(8,128)S(1)} %add_add_fusion.3), channel_id=1, source_target_pairs={{0,1},{1,0},{2,3},{3,2},{4,20},{5,21},{6,22},{7,23},{8,9},{9,8},{1... | collective-permute-start | bytes 208904 | tf_op jit(solution)/shard_map/sum_z_inner/ppermute | solution.py:273
  61.4 5.1 %collective-permute-start.20 = (f32[136,128]{1,0:T(8,128)S(1)}, f32[136,128]{1,0:T(8,128)S(1)}, u32[]{:S(2)}, u32[]{:S(2)}) collective-permute-start(f32[136,128]{1,0:T(8,128)S(1)} %add_add_fusion.3), channel_id=1, source_target_pairs={{0,1},{1,0},{2,3},{3,2},{4,28},{5,29},{6,30},{7,31},{8,9},{9,8},{1... | collective-permute-start | bytes 208904 | tf_op jit(solution)/shard_map/sum_z_inner/ppermute | solution.py:273
  63.0 3.9 %collective-permute-start.19 = (f32[136,128]{1,0:T(8,128)S(1)}, f32[136,128]{1,0:T(8,128)S(1)}, u32[]{:S(2)}, u32[]{:S(2)}) collective-permute-start(f32[136,128]{1,0:T(8,128)S(1)} %add_add_fusion.3), channel_id=1, source_target_pairs={{0,1},{1,0},{2,3},{3,2},{4,12},{5,13},{6,14},{7,15},{8,9},{9,8},{1... | collective-permute-start | bytes 208904 | tf_op jit(solution)/shard_map/sum_z_inner/ppermute | solution.py:273
  66.9 5.4 %collective-permute-start.22 = (f32[136,128]{1,0:T(8,128)S(1)}, f32[136,128]{1,0:T(8,128)S(1)}, u32[]{:S(2)}, u32[]{:S(2)}) collective-permute-start(f32[136,128]{1,0:T(8,128)S(1)} %add_add_fusion.2), channel_id=1, source_target_pairs={{0,1},{1,0},{2,3},{3,2},{4,52},{5,53},{6,54},{7,55},{8,9},{9,8},{1... | collective-permute-start | bytes 208904 | tf_op jit(solution)/shard_map/sum_z_outer/ppermute | solution.py:273
  74.7 4.3 %collective-permute-start.26 = (f32[72,128]{1,0:T(8,128)S(1)}, f32[72,128]{1,0:T(8,128)S(1)}, u32[]{:S(2)}, u32[]{:S(2)}) collective-permute-start(f32[72,128]{1,0:T(8,128)S(1)} %get-tuple-element.62.refs_0_), channel_id=1, source_target_pairs={{0,2},{1,3},{2,0},{3,1},{4,6},{5,7},{6,4},{7,5},{8,10},{9,11},{10,... | collective-permute-start | bytes 110600 | tf_op jit(solution)/shard_map/sum_req/ppermute | solution.py:282
  75.9 4.1 %collective-permute-start.25 = (f32[72,128]{1,0:T(8,128)S(1)}, f32[72,128]{1,0:T(8,128)S(1)}, u32[]{:S(2)}, u32[]{:S(2)}) collective-permute-start(f32[72,128]{1,0:T(8,128)S(1)} %get-tuple-element.62.refs_0_), channel_id=1, source_target_pairs={{0,3},{1,2},{2,1},{3,0},{4,7},{5,6},{6,5},{7,4},{8,11},{9,10},{10,... | collective-permute-start | bytes 110600 | tf_op jit(solution)/shard_map/sum_req/ppermute | solution.py:282
  76.7 3.3 %collective-permute-start.24 = (f32[72,128]{1,0:T(8,128)S(1)}, f32[72,128]{1,0:T(8,128)S(1)}, u32[]{:S(2)}, u32[]{:S(2)}) collective-permute-start(f32[72,128]{1,0:T(8,128)S(1)} %get-tuple-element.62.refs_0_), channel_id=1, source_target_pairs={{0,1},{1,0},{2,3},{3,2},{4,5},{5,4},{6,7},{7,6},{8,9},{9,8},{10,11... | collective-permute-start | bytes 110600 | tf_op jit(solution)/shard_map/sum_req/ppermute | solution.py:282
  84.4 4.8 %collective-permute-start.30 = (f32[136,128]{1,0:T(8,128)S(1)}, f32[136,128]{1,0:T(8,128)S(1)}, u32[]{:S(2)}, u32[]{:S(2)}) collective-permute-start(f32[136,128]{1,0:T(8,128)S(1)} %add.95), channel_id=1, source_target_pairs={{0,1},{1,0},{2,3},{3,2},{4,132},{5,133},{6,134},{7,135},{8,9},{9,8... | collective-permute-start | bytes 208904 | tf_op jit(solution)/shard_map/sum_y/ppermute | solution.py:273
  86.2 4.4 %collective-permute-start.29 = (f32[136,128]{1,0:T(8,128)S(1)}, f32[136,128]{1,0:T(8,128)S(1)}, u32[]{:S(2)}, u32[]{:S(2)}) collective-permute-start(f32[136,128]{1,0:T(8,128)S(1)} %add.95), channel_id=1, source_target_pairs={{0,1},{1,0},{2,3},{3,2},{4,196},{5,197},{6,198},{7,199},{8,9},{9,8... | collective-permute-start | bytes 208904 | tf_op jit(solution)/shard_map/sum_y/ppermute | solution.py:273
  86.8 3.7 %collective-permute-start.28 = (f32[136,128]{1,0:T(8,128)S(1)}, f32[136,128]{1,0:T(8,128)S(1)}, u32[]{:S(2)}, u32[]{:S(2)}) collective-permute-start(f32[136,128]{1,0:T(8,128)S(1)} %add.95), channel_id=1, source_target_pairs={{0,1},{1,0},{2,3},{3,2},{4,68},{5,69},{6,70},{7,71},{8,9},{9,8},{1... | collective-permute-start | bytes 208904 | tf_op jit(solution)/shard_map/sum_y/ppermute | solution.py:273
  90.6 4.9 %collective-permute-start.33 = (f32[136,128]{1,0:T(8,128)S(1)}, f32[136,128]{1,0:T(8,128)S(1)}, u32[]{:S(2)}, u32[]{:S(2)}) collective-permute-start(f32[136,128]{1,0:T(8,128)S(1)} %add_add_fusion.1), channel_id=1, source_target_pairs={{0,1},{1,0},{2,3},{3,2},{4,20},{5,21},{6,22},{7,23},{8,9},{9,8},{1... | collective-permute-start | bytes 208904 | tf_op jit(solution)/shard_map/sum_z_inner/ppermute | solution.py:273
  91.7 5.1 %collective-permute-start.32 = (f32[136,128]{1,0:T(8,128)S(1)}, f32[136,128]{1,0:T(8,128)S(1)}, u32[]{:S(2)}, u32[]{:S(2)}) collective-permute-start(f32[136,128]{1,0:T(8,128)S(1)} %add_add_fusion.1), channel_id=1, source_target_pairs={{0,1},{1,0},{2,3},{3,2},{4,28},{5,29},{6,30},{7,31},{8,9},{9,8},{1... | collective-permute-start | bytes 208904 | tf_op jit(solution)/shard_map/sum_z_inner/ppermute | solution.py:273
  93.3 3.9 %collective-permute-start.31 = (f32[136,128]{1,0:T(8,128)S(1)}, f32[136,128]{1,0:T(8,128)S(1)}, u32[]{:S(2)}, u32[]{:S(2)}) collective-permute-start(f32[136,128]{1,0:T(8,128)S(1)} %add_add_fusion.1), channel_id=1, source_target_pairs={{0,1},{1,0},{2,3},{3,2},{4,12},{5,13},{6,14},{7,15},{8,9},{9,8},{1... | collective-permute-start | bytes 208904 | tf_op jit(solution)/shard_map/sum_z_inner/ppermute | solution.py:273
  97.3 5.4 %collective-permute-start.34 = (f32[136,128]{1,0:T(8,128)S(1)}, f32[136,128]{1,0:T(8,128)S(1)}, u32[]{:S(2)}, u32[]{:S(2)}) collective-permute-start(f32[136,128]{1,0:T(8,128)S(1)} %add_add_fusion), channel_id=1, source_target_pairs={{0,1},{1,0},{2,3},{3,2},{4,52},{5,53},{6,54},{7,55},{8,9},{9,8},{1... | collective-permute-start | bytes 208904 | tf_op jit(solution)/shard_map/sum_z_outer/ppermute | solution.py:273
  102.7 7.5 %collective-permute-start.35 = (f32[136,128]{1,0:T(8,128)S(1)}, f32[136,128]{1,0:T(8,128)S(1)}, u32[]{:S(2)}, u32[]{:S(2)}) collective-permute-start(f32[136,128]{1,0:T(8,128)S(1)} %constant_dynamic-update-slice_fusion.state_own), channel_id=1, source_target_pairs={{0,4},{1,5},{2,6},{3,7},{4,0},{5,1},{6,2},{7,3},{8,12},{9,13},{10,... | collective-permute-start | bytes 208904 | tf_op jit(solution)/shard_map/back_core/ppermute | solution.py:273
  103.1 4.0 %collective-permute-start.38 = (f32[8,128]{1,0:T(8,128)S(1)}, f32[8,128]{1,0:T(8,128)S(1)}, u32[]{:S(2)}, u32[]{:S(2)}) collective-permute-start(f32[8,128]{1,0:T(8,128)S(1)} %get-tuple-element.74.last_0), channel_id=1, source_target_pairs={{0,64},{1,65},{2,66},{3,67},{4,6},{5,7},{6,4},{7,5},{8,72},{9,73},... | collective-permute-start | bytes 12296 | tf_op jit(solution)/shard_map/sum_req_last/ppermute | solution.py:273
  105.1 3.7 %collective-permute-start.37 = (f32[8,128]{1,0:T(8,128)S(1)}, f32[8,128]{1,0:T(8,128)S(1)}, u32[]{:S(2)}, u32[]{:S(2)}) collective-permute-start(f32[8,128]{1,0:T(8,128)S(1)} %get-tuple-element.74.last_0), channel_id=1, source_target_pairs={{0,64},{1,65},{2,66},{3,67},{4,7},{5,6},{6,5},{7,4},{8,72},{9,73},... | collective-permute-start | bytes 12296 | tf_op jit(solution)/shard_map/sum_req_last/ppermute | solution.py:273
  (13 other events, 112.2 us)

commit v2 on v1

--- a/solution.py
+++ b/solution.py
@@ -223,7 +223,8 @@
     norms_out[...] = out
 
 
-def results_kernel(params, state_own, state_other, norms_own, norms_other, dual_out, limit_out, norms_out):
+def results_kernel(params, state_own, state_other, norms_own, norms_other, primal, dual_out, limit_out, norms_out, primal_out):
+    primal_out[...] = primal[...]
     mine = params[1 + ITERS : 2 + ITERS, :] == 1.0
     req_blocks = dual_out.shape[0]
     dual_out[...] = jnp.where(mine, state_own[:req_blocks, :], state_other[:req_blocks, :])
@@ -284,14 +285,14 @@
     def total_tst(x):
         with jax.named_scope("sum_core"):
             x = x + swap_core(x)
+        with jax.named_scope("sum_z_outer"):
+            x = x + chips(x, 0, n_z - 2)
+        with jax.named_scope("sum_z_inner"):
+            a, b, c = [chips(x, 0, bits) for bits in (1, 3, 2)]
+            x = (x + a) + (b + c)
         with jax.named_scope("sum_y"):
             a, b, c = [chips(x, bits, 0) for bits in (1, 3, 2)]
             x = (x + a) + (b + c)
-        with jax.named_scope("sum_z_inner"):
-            a, b, c = [chips(x, 0, bits) for bits in (1, 3, 2)]
-            x = (x + a) + (b + c)
-        with jax.named_scope("sum_z_outer"):
-            x = x + chips(x, 0, n_z - 2)
         return x
 
     def hand_on(x):
@@ -362,8 +363,8 @@
     state = jnp.concatenate([dual, scal], axis=0)
     with jax.named_scope("back_core"):
         other = swap_core(state), swap_core(norms)
-    dual, limit, norms = call(results_kernel, (big_r, struct(1, 1), struct(2, ITERS)), [VMEM] * 5)(
-        params, state, other[0], norms, other[1]
+    dual, limit, norms, primal = call(results_kernel, (big_r, struct(1, 1), struct(2, ITERS), big_t), [VMEM] * 6)(
+        params, state, other[0], norms, other[1], primal
     )
     return primal.reshape(-1), dual.reshape(-1), limit.reshape(1), norms.T
 

time: 111 us -> 110 us (level)
  waiting for transfers between devices: 44.7 us -> 42.3 us
  starting transfers between devices: 48.9 us -> 51.1 us
    ppermute x31, waiting for transfers between devices: 38.7 us -> 36.4 us  [on_mesh(): return lax.ppermute(x, ('tst', 'req'), pairs)]
    ppermute x31, starting transfers between devices: 38.3 us -> 40.4 us  [on_mesh(): return lax.ppermute(x, ('tst', 'req'), pairs)]
where the time goes in v2:
time: 110 us
  starting transfers between devices  51.1 us (46%)
  waiting for transfers between devices  42.3 us (38%)
  Pallas kernels  13 us (12%)
  between operations  2.79 us (3%)
    ppermute x31, starting transfers between devices, on_mesh(): return lax.ppermute(x, ('tst', 'req'), pairs)  40.4 us
    ppermute x31, waiting for transfers between devices, on_mesh(): return lax.ppermute(x, ('tst', 'req'), pairs)  36.4 us
    ppermute x9, starting transfers between devices, on_req(): lax.ppermute(x, 'req', [(i, i ^ bit) for i in range(n_req)])  10.7 us
    ppermute x9, waiting for transfers between devices, on_req(): lax.ppermute(x, 'req', [(i, i ^ bit) for i in range(n_req)])  5.93 us
    pallas_call x3, Pallas kernels, per_device(): call(functools.partial(primal_load_kernel, iteration), outs, [VMEM] * len...  4.7 us
    pallas_call x1, Pallas kernels, per_device(): call(first_pull_kernel, (pull_shape, struct(slots, req_blocks, dtype=BF16...  4.07 us
  transfers between devices with their start and end apart: 40, of which 31 were waited for; matrix products, arithmetic and copies ran while one was open for 1% of the time, Pallas kernels for 1%

profile of v2, /device:TPU:1, one launch (start us, length us, event | category | flops | bytes accessed | tf_op | source)
XLA Modules:
  0.0 110.3 jit_solution(14977637190867615805)
XLA Ops:
  1.3 4.1 %shard_map.147 = (f32[72,128]{1,0:T(8,128)S(1)}, bf16[128,128]{1,0:T(8,128)(2,1)S(1)}, f32[128,128]{1,0:T(8,128)S(1)}, bf16[128,128]{1,0:T(8,128)(2,1)S(1)}, f32...) custom-call(bf16[128,128,128]{2,1,0:T(8,128)(2,1)} %tiles_in.3, ...), custom_call_target="tpu_custom_call" | custom-call | tf_op jit(solution)/shard_map/pallas_call | solution.py:321
  5.4 3.7 %collective-permute-start.2 = (f32[72,128]{1,0:T(8,128)S(1)}, f32[72,128]{1,0:T(8,128)S(1)}, u32[]{:S(2)}, u32[]{:S(2)}) collective-permute-start(f32[72,128]{1,0:T(8,128)S(1)} %get-tuple-element.42.refs_0_), channel_id=1, source_target_pairs={{0,2},{1,3},{2,0},{3,1},{4,6},{5,7},{6,4},{7,5},{8,10},{9,11},{10,... | collective-permute-start | bytes 110600 | tf_op jit(solution)/shard_map/sum_req/ppermute | solution.py:283
  13.5 1.6 %shard_map.149 = (f32[136,128]{1,0:T(8,128)S(1)}, f32[64,128]{1,0:T(8,128)S(1)}, f32[64,128]{1,0:T(8,128)S(1)}) custom-call(f32[72,128]{1,0:T(8,128)S(1)} %get-tuple-element.42.refs_0_, f32[72,128]{1,0:T(8,128)S(1)} %collective-permute-done.refs_1_, f32[72,128]{1,0:T(8,128)S(1)} %collective-permute-done.1.refs_2_, ...), custom_call_target="tpu_custom_call" | custom-call | tf_op jit(solution)/shard_map/pallas_call | solution.py:347
  15.1 2.3 %collective-permute-start.3 = (f32[136,128]{1,0:T(8,128)S(1)}, f32[136,128]{1,0:T(8,128)S(1)}, u32[]{:S(2)}, u32[]{:S(2)}) collective-permute-start(f32[136,128]{1,0:T(8,128)S(1)} %get-tuple-element.53), channel_id=1, source_target_pairs={{0,4},{1,5},{2,6},{3,7},{4,0},{5,1},{6,2},{7,3},{8,12},{9,13},{10,... | collective-permute-start | bytes 208904 | tf_op jit(solution)/shard_map/sum_core/ppermute | solution.py:274
  18.3 5.7 %collective-permute-start.4 = (f32[136,128]{1,0:T(8,128)S(1)}, f32[136,128]{1,0:T(8,128)S(1)}, u32[]{:S(2)}, u32[]{:S(2)}) collective-permute-start(f32[136,128]{1,0:T(8,128)S(1)} %add.79), channel_id=1, source_target_pairs={{0,1},{1,0},{2,3},{3,2},{4,52},{5,53},{6,54},{7,55},{8,9},{9,8},{1... | collective-permute-start | bytes 208904 | tf_op jit(solution)/shard_map/sum_z_outer/ppermute | solution.py:274
  24.0 1.8 %collective-permute-done.4 = f32[136,128]{1,0:T(8,128)S(1)} collective-permute-done((f32[136,128]{1,0:T(8,128)S(1)}, f32[136,128]{1,0:T(8,128)S(1)}, u32[]{:S(2)}, u32[]{:S(2)}) %collective-permute-start.4) | collective-permute-done | bytes 69664 | tf_op jit(solution)/shard_map/sum_z_outer/ppermute | solution.py:274
  27.0 2.4 %collective-permute-start.6 = (f32[136,128]{1,0:T(8,128)S(1)}, f32[136,128]{1,0:T(8,128)S(1)}, u32[]{:S(2)}, u32[]{:S(2)}) collective-permute-start(f32[136,128]{1,0:T(8,128)S(1)} %add.80), channel_id=1, source_target_pairs={{0,1},{1,0},{2,3},{3,2},{4,28},{5,29},{6,30},{7,31},{8,9},{9,8},{1... | collective-permute-start | bytes 208904 | tf_op jit(solution)/shard_map/sum_z_inner/ppermute | solution.py:274
  30.0 2.1 %collective-permute-done.6 = f32[136,128]{1,0:T(8,128)S(1)} collective-permute-done((f32[136,128]{1,0:T(8,128)S(1)}, f32[136,128]{1,0:T(8,128)S(1)}, u32[]{:S(2)}, u32[]{:S(2)}) %collective-permute-start.6) | collective-permute-done | bytes 69664 | tf_op jit(solution)/shard_map/sum_z_inner/ppermute | solution.py:274
  33.1 3.0 %collective-permute-start.10 = (f32[136,128]{1,0:T(8,128)S(1)}, f32[136,128]{1,0:T(8,128)S(1)}, u32[]{:S(2)}, u32[]{:S(2)}) collective-permute-start(f32[136,128]{1,0:T(8,128)S(1)} %add_add_fusion.5), channel_id=1, source_target_pairs={{0,1},{1,0},{2,3},{3,2},{4,132},{5,133},{6,134},{7,135},{8,9},{9,8... | collective-permute-start | bytes 208904 | tf_op jit(solution)/shard_map/sum_y/ppermute | solution.py:274
  37.8 2.6 %collective-permute-done.9 = f32[136,128]{1,0:T(8,128)S(1)} collective-permute-done((f32[136,128]{1,0:T(8,128)S(1)}, f32[136,128]{1,0:T(8,128)S(1)}, u32[]{:S(2)}, u32[]{:S(2)}) %collective-permute-start.9) | collective-permute-done | bytes 69664 | tf_op jit(solution)/shard_map/sum_y/ppermute | solution.py:274
  42.9 2.6 %collective-permute-start.14 = (f32[72,128]{1,0:T(8,128)S(1)}, f32[72,128]{1,0:T(8,128)S(1)}, u32[]{:S(2)}, u32[]{:S(2)}) collective-permute-start(f32[72,128]{1,0:T(8,128)S(1)} %get-tuple-element.56.refs_0_), channel_id=1, source_target_pairs={{0,2},{1,3},{2,0},{3,1},{4,6},{5,7},{6,4},{7,5},{8,10},{9,11},{10,... | collective-permute-start | bytes 110600 | tf_op jit(solution)/shard_map/sum_req/ppermute | solution.py:283
  47.2 2.3 %collective-permute-done.13.refs_2_ = f32[72,128]{1,0:T(8,128)S(1)} collective-permute-done((f32[72,128]{1,0:T(8,128)S(1)}, f32[72,128]{1,0:T(8,128)S(1)}, u32[]{:S(2)}, u32[]{:S(2)}) %collective-permute-start.13) | collective-permute-done | bytes 36896 | tf_op jit(solution)/shard_map/sum_req/ppermute | solution.py:283
  49.5 1.6 %shard_map.151 = (f32[136,128]{1,0:T(8,128)S(1)}, f32[64,128]{1,0:T(8,128)S(1)}, f32[64,128]{1,0:T(8,128)S(1)}, f32[8,128]{1,0:T(8,128)S(1)}) custom-call(f32[72,128]{1,0:T(8,128)S(1)} %get-tuple-element.56.refs_0_, f32[72,128]{1,0:T(8,128)S(1)} %collective-permute-done.12.refs_1_, f32[72,128]{1,0:T(8,128)S(1)} %collective-permute-done.13.refs_2_, ...), custom_call_target="tpu_custom_call" | custom-call | tf_op jit(solution)/shard_map/pallas_call | solution.py:347
  51.1 1.9 %collective-permute-start.15 = (f32[136,128]{1,0:T(8,128)S(1)}, f32[136,128]{1,0:T(8,128)S(1)}, u32[]{:S(2)}, u32[]{:S(2)}) collective-permute-start(f32[136,128]{1,0:T(8,128)S(1)} %get-tuple-element.60), channel_id=1, source_target_pairs={{0,4},{1,5},{2,6},{3,7},{4,0},{5,1},{6,2},{7,3},{8,12},{9,13},{10,... | collective-permute-start | bytes 208904 | tf_op jit(solution)/shard_map/sum_core/ppermute | solution.py:274
  53.9 3.2 %collective-permute-start.16 = (f32[136,128]{1,0:T(8,128)S(1)}, f32[136,128]{1,0:T(8,128)S(1)}, u32[]{:S(2)}, u32[]{:S(2)}) collective-permute-start(f32[136,128]{1,0:T(8,128)S(1)} %add.87), channel_id=1, source_target_pairs={{0,1},{1,0},{2,3},{3,2},{4,52},{5,53},{6,54},{7,55},{8,9},{9,8},{1... | collective-permute-start | bytes 208904 | tf_op jit(solution)/shard_map/sum_z_outer/ppermute | solution.py:274
  57.0 2.3 %collective-permute-done.16 = f32[136,128]{1,0:T(8,128)S(1)} collective-permute-done((f32[136,128]{1,0:T(8,128)S(1)}, f32[136,128]{1,0:T(8,128)S(1)}, u32[]{:S(2)}, u32[]{:S(2)}) %collective-permute-start.16) | collective-permute-done | bytes 69664 | tf_op jit(solution)/shard_map/sum_z_outer/ppermute | solution.py:274
  59.3 2.0 %collective-permute-start.19 = (f32[136,128]{1,0:T(8,128)S(1)}, f32[136,128]{1,0:T(8,128)S(1)}, u32[]{:S(2)}, u32[]{:S(2)}) collective-permute-start(f32[136,128]{1,0:T(8,128)S(1)} %add.88), channel_id=1, source_target_pairs={{0,1},{1,0},{2,3},{3,2},{4,20},{5,21},{6,22},{7,23},{8,9},{9,8},{1... | collective-permute-start | bytes 208904 | tf_op jit(solution)/shard_map/sum_z_inner/ppermute | solution.py:274
  61.4 1.8 %collective-permute-start.18 = (f32[136,128]{1,0:T(8,128)S(1)}, f32[136,128]{1,0:T(8,128)S(1)}, u32[]{:S(2)}, u32[]{:S(2)}) collective-permute-start(f32[136,128]{1,0:T(8,128)S(1)} %add.88), channel_id=1, source_target_pairs={{0,1},{1,0},{2,3},{3,2},{4,28},{5,29},{6,30},{7,31},{8,9},{9,8},{1... | collective-permute-start | bytes 208904 | tf_op jit(solution)/shard_map/sum_z_inner/ppermute | solution.py:274
  63.5 2.9 %collective-permute-done.18 = f32[136,128]{1,0:T(8,128)S(1)} collective-permute-done((f32[136,128]{1,0:T(8,128)S(1)}, f32[136,128]{1,0:T(8,128)S(1)}, u32[]{:S(2)}, u32[]{:S(2)}) %collective-permute-start.18) | collective-permute-done | bytes 69664 | tf_op jit(solution)/shard_map/sum_z_inner/ppermute | solution.py:274
  67.1 1.3 %collective-permute-start.22 = (f32[136,128]{1,0:T(8,128)S(1)}, f32[136,128]{1,0:T(8,128)S(1)}, u32[]{:S(2)}, u32[]{:S(2)}) collective-permute-start(f32[136,128]{1,0:T(8,128)S(1)} %add_add_fusion.3), channel_id=1, source_target_pairs={{0,1},{1,0},{2,3},{3,2},{4,132},{5,133},{6,134},{7,135},{8,9},{9,8... | collective-permute-start | bytes 208904 | tf_op jit(solution)/shard_map/sum_y/ppermute | solution.py:274
  69.8 2.0 %collective-permute-done.22 = f32[136,128]{1,0:T(8,128)S(1)} collective-permute-done((f32[136,128]{1,0:T(8,128)S(1)}, f32[136,128]{1,0:T(8,128)S(1)}, u32[]{:S(2)}, u32[]{:S(2)}) %collective-permute-start.22) | collective-permute-done | bytes 69664 | tf_op jit(solution)/shard_map/sum_y/ppermute | solution.py:274
  77.8 1.7 %collective-permute-done.26.refs_3_ = f32[72,128]{1,0:T(8,128)S(1)} collective-permute-done((f32[72,128]{1,0:T(8,128)S(1)}, f32[72,128]{1,0:T(8,128)S(1)}, u32[]{:S(2)}, u32[]{:S(2)}) %collective-permute-start.26) | collective-permute-done | bytes 36896 | tf_op jit(solution)/shard_map/sum_req/ppermute | solution.py:283
  80.5 1.6 %shard_map.153 = (f32[136,128]{1,0:T(8,128)S(1)}, f32[64,128]{1,0:T(8,128)S(1)}, f32[8,128]{1,0:T(8,128)S(1)}) custom-call(f32[72,128]{1,0:T(8,128)S(1)} %get-tuple-element.63.refs_0_, f32[72,128]{1,0:T(8,128)S(1)} %collective-permute-done.24.refs_1_, f32[72,128]{1,0:T(8,128)S(1)} %collective-permute-done.25.refs_2_, ...), custom_call_target="tpu_custom_call" | custom-call | tf_op jit(solution)/shard_map/pallas_call | solution.py:347
  82.0 1.5 %collective-permute-start.27 = (f32[136,128]{1,0:T(8,128)S(1)}, f32[136,128]{1,0:T(8,128)S(1)}, u32[]{:S(2)}, u32[]{:S(2)}) collective-permute-start(f32[136,128]{1,0:T(8,128)S(1)} %get-tuple-element.67), channel_id=1, source_target_pairs={{0,4},{1,5},{2,6},{3,7},{4,0},{5,1},{6,2},{7,3},{8,12},{9,13},{10,... | collective-permute-start | bytes 208904 | tf_op jit(solution)/shard_map/sum_core/ppermute | solution.py:274
  84.5 2.6 %collective-permute-start.28 = (f32[136,128]{1,0:T(8,128)S(1)}, f32[136,128]{1,0:T(8,128)S(1)}, u32[]{:S(2)}, u32[]{:S(2)}) collective-permute-start(f32[136,128]{1,0:T(8,128)S(1)} %add.95), channel_id=1, source_target_pairs={{0,1},{1,0},{2,3},{3,2},{4,52},{5,53},{6,54},{7,55},{8,9},{9,8},{1... | collective-permute-start | bytes 208904 | tf_op jit(solution)/shard_map/sum_z_outer/ppermute | solution.py:274
  87.1 2.8 %collective-permute-done.28 = f32[136,128]{1,0:T(8,128)S(1)} collective-permute-done((f32[136,128]{1,0:T(8,128)S(1)}, f32[136,128]{1,0:T(8,128)S(1)}, u32[]{:S(2)}, u32[]{:S(2)}) %collective-permute-start.28) | collective-permute-done | bytes 69664 | tf_op jit(solution)/shard_map/sum_z_outer/ppermute | solution.py:274
  90.8 1.6 %collective-permute-start.30 = (f32[136,128]{1,0:T(8,128)S(1)}, f32[136,128]{1,0:T(8,128)S(1)}, u32[]{:S(2)}, u32[]{:S(2)}) collective-permute-start(f32[136,128]{1,0:T(8,128)S(1)} %add.96), channel_id=1, source_target_pairs={{0,1},{1,0},{2,3},{3,2},{4,28},{5,29},{6,30},{7,31},{8,9},{9,8},{1... | collective-permute-start | bytes 208904 | tf_op jit(solution)/shard_map/sum_z_inner/ppermute | solution.py:274
  92.6 2.2 %collective-permute-done.31 = f32[136,128]{1,0:T(8,128)S(1)} collective-permute-done((f32[136,128]{1,0:T(8,128)S(1)}, f32[136,128]{1,0:T(8,128)S(1)}, u32[]{:S(2)}, u32[]{:S(2)}) %collective-permute-start.31) | collective-permute-done | bytes 69664 | tf_op jit(solution)/shard_map/sum_z_inner/ppermute | solution.py:274
  96.3 1.3 %collective-permute-start.34 = (f32[136,128]{1,0:T(8,128)S(1)}, f32[136,128]{1,0:T(8,128)S(1)}, u32[]{:S(2)}, u32[]{:S(2)}) collective-permute-start(f32[136,128]{1,0:T(8,128)S(1)} %add_add_fusion.1), channel_id=1, source_target_pairs={{0,1},{1,0},{2,3},{3,2},{4,132},{5,133},{6,134},{7,135},{8,9},{9,8... | collective-permute-start | bytes 208904 | tf_op jit(solution)/shard_map/sum_y/ppermute | solution.py:274
  99.1 2.0 %collective-permute-done.34 = f32[136,128]{1,0:T(8,128)S(1)} collective-permute-done((f32[136,128]{1,0:T(8,128)S(1)}, f32[136,128]{1,0:T(8,128)S(1)}, u32[]{:S(2)}, u32[]{:S(2)}) %collective-permute-start.34) | collective-permute-done | bytes 69664 | tf_op jit(solution)/shard_map/sum_y/ppermute | solution.py:274
  102.6 2.0 %collective-permute-start.38 = (f32[8,128]{1,0:T(8,128)S(1)}, f32[8,128]{1,0:T(8,128)S(1)}, u32[]{:S(2)}, u32[]{:S(2)}) collective-permute-start(f32[8,128]{1,0:T(8,128)S(1)} %get-tuple-element.74.last_0), channel_id=1, source_target_pairs={{0,64},{1,65},{2,66},{3,67},{4,6},{5,7},{6,4},{7,5},{8,72},{9,73},... | collective-permute-start | bytes 12296 | tf_op jit(solution)/shard_map/sum_req_last/ppermute | solution.py:274
  106.5 1.7 %collective-permute-done.37.last_2 = f32[8,128]{1,0:T(8,128)S(1)} collective-permute-done((f32[8,128]{1,0:T(8,128)S(1)}, f32[8,128]{1,0:T(8,128)S(1)}, u32[]{:S(2)}, u32[]{:S(2)}) %collective-permute-start.37) | collective-permute-done | bytes 4128 | tf_op jit(solution)/shard_map/sum_req_last/ppermute | solution.py:274
  (90 shorter events, 33.6 us)
Async XLA Ops:
  5.4 7.9 %collective-permute-start.2 = (f32[72,128]{1,0:T(8,128)S(1)}, f32[72,128]{1,0:T(8,128)S(1)}, u32[]{:S(2)}, u32[]{:S(2)}) collective-permute-start(f32[72,128]{1,0:T(8,128)S(1)} %get-tuple-element.42.refs_0_), channel_id=1, source_target_pairs={{0,2},{1,3},{2,0},{3,1},{4,6},{5,7},{6,4},{7,5},{8,10},{9,11},{10,... | collective-permute-start | bytes 110600 | tf_op jit(solution)/shard_map/sum_req/ppermute | solution.py:283
  9.0 4.3 %collective-permute-start.1 = (f32[72,128]{1,0:T(8,128)S(1)}, f32[72,128]{1,0:T(8,128)S(1)}, u32[]{:S(2)}, u32[]{:S(2)}) collective-permute-start(f32[72,128]{1,0:T(8,128)S(1)} %get-tuple-element.42.refs_0_), channel_id=1, source_target_pairs={{0,3},{1,2},{2,1},{3,0},{4,7},{5,6},{6,5},{7,4},{8,11},{9,10},{10,... | collective-permute-start | bytes 110600 | tf_op jit(solution)/shard_map/sum_req/ppermute | solution.py:283
  9.9 3.5 %collective-permute-start = (f32[72,128]{1,0:T(8,128)S(1)}, f32[72,128]{1,0:T(8,128)S(1)}, u32[]{:S(2)}, u32[]{:S(2)}) collective-permute-start(f32[72,128]{1,0:T(8,128)S(1)} %get-tuple-element.42.refs_0_), channel_id=1, source_target_pairs={{0,1},{1,0},{2,3},{3,2},{4,5},{5,4},{6,7},{7,6},{8,9},{9,8},{10,11... | collective-permute-start | bytes 110600 | tf_op jit(solution)/shard_map/sum_req/ppermute | solution.py:283
  18.3 7.5 %collective-permute-start.4 = (f32[136,128]{1,0:T(8,128)S(1)}, f32[136,128]{1,0:T(8,128)S(1)}, u32[]{:S(2)}, u32[]{:S(2)}) collective-permute-start(f32[136,128]{1,0:T(8,128)S(1)} %add.79), channel_id=1, source_target_pairs={{0,1},{1,0},{2,3},{3,2},{4,52},{5,53},{6,54},{7,55},{8,9},{9,8},{1... | collective-permute-start | bytes 208904 | tf_op jit(solution)/shard_map/sum_z_outer/ppermute | solution.py:274
  25.8 4.1 %collective-permute-start.7 = (f32[136,128]{1,0:T(8,128)S(1)}, f32[136,128]{1,0:T(8,128)S(1)}, u32[]{:S(2)}, u32[]{:S(2)}) collective-permute-start(f32[136,128]{1,0:T(8,128)S(1)} %add.80), channel_id=1, source_target_pairs={{0,1},{1,0},{2,3},{3,2},{4,20},{5,21},{6,22},{7,23},{8,9},{9,8},{1... | collective-permute-start | bytes 208904 | tf_op jit(solution)/shard_map/sum_z_inner/ppermute | solution.py:274
  27.0 5.0 %collective-permute-start.6 = (f32[136,128]{1,0:T(8,128)S(1)}, f32[136,128]{1,0:T(8,128)S(1)}, u32[]{:S(2)}, u32[]{:S(2)}) collective-permute-start(f32[136,128]{1,0:T(8,128)S(1)} %add.80), channel_id=1, source_target_pairs={{0,1},{1,0},{2,3},{3,2},{4,28},{5,29},{6,30},{7,31},{8,9},{9,8},{1... | collective-permute-start | bytes 208904 | tf_op jit(solution)/shard_map/sum_z_inner/ppermute | solution.py:274
  29.4 3.7 %collective-permute-start.5 = (f32[136,128]{1,0:T(8,128)S(1)}, f32[136,128]{1,0:T(8,128)S(1)}, u32[]{:S(2)}, u32[]{:S(2)}) collective-permute-start(f32[136,128]{1,0:T(8,128)S(1)} %add.80), channel_id=1, source_target_pairs={{0,1},{1,0},{2,3},{3,2},{4,12},{5,13},{6,14},{7,15},{8,9},{9,8},{1... | collective-permute-start | bytes 208904 | tf_op jit(solution)/shard_map/sum_z_inner/ppermute | solution.py:274
  33.1 4.8 %collective-permute-start.10 = (f32[136,128]{1,0:T(8,128)S(1)}, f32[136,128]{1,0:T(8,128)S(1)}, u32[]{:S(2)}, u32[]{:S(2)}) collective-permute-start(f32[136,128]{1,0:T(8,128)S(1)} %add_add_fusion.5), channel_id=1, source_target_pairs={{0,1},{1,0},{2,3},{3,2},{4,132},{5,133},{6,134},{7,135},{8,9},{9,8... | collective-permute-start | bytes 208904 | tf_op jit(solution)/shard_map/sum_y/ppermute | solution.py:274
  36.1 4.4 %collective-permute-start.9 = (f32[136,128]{1,0:T(8,128)S(1)}, f32[136,128]{1,0:T(8,128)S(1)}, u32[]{:S(2)}, u32[]{:S(2)}) collective-permute-start(f32[136,128]{1,0:T(8,128)S(1)} %add_add_fusion.5), channel_id=1, source_target_pairs={{0,1},{1,0},{2,3},{3,2},{4,196},{5,197},{6,198},{7,199},{8,9},{9,8... | collective-permute-start | bytes 208904 | tf_op jit(solution)/shard_map/sum_y/ppermute | solution.py:274
  36.8 3.6 %collective-permute-start.8 = (f32[136,128]{1,0:T(8,128)S(1)}, f32[136,128]{1,0:T(8,128)S(1)}, u32[]{:S(2)}, u32[]{:S(2)}) collective-permute-start(f32[136,128]{1,0:T(8,128)S(1)} %add_add_fusion.5), channel_id=1, source_target_pairs={{0,1},{1,0},{2,3},{3,2},{4,68},{5,69},{6,70},{7,71},{8,9},{9,8},{1... | collective-permute-start | bytes 208904 | tf_op jit(solution)/shard_map/sum_y/ppermute | solution.py:274
  42.9 4.3 %collective-permute-start.14 = (f32[72,128]{1,0:T(8,128)S(1)}, f32[72,128]{1,0:T(8,128)S(1)}, u32[]{:S(2)}, u32[]{:S(2)}) collective-permute-start(f32[72,128]{1,0:T(8,128)S(1)} %get-tuple-element.56.refs_0_), channel_id=1, source_target_pairs={{0,2},{1,3},{2,0},{3,1},{4,6},{5,7},{6,4},{7,5},{8,10},{9,11},{10,... | collective-permute-start | bytes 110600 | tf_op jit(solution)/shard_map/sum_req/ppermute | solution.py:283
  45.5 4.0 %collective-permute-start.13 = (f32[72,128]{1,0:T(8,128)S(1)}, f32[72,128]{1,0:T(8,128)S(1)}, u32[]{:S(2)}, u32[]{:S(2)}) collective-permute-start(f32[72,128]{1,0:T(8,128)S(1)} %get-tuple-element.56.refs_0_), channel_id=1, source_target_pairs={{0,3},{1,2},{2,1},{3,0},{4,7},{5,6},{6,5},{7,4},{8,11},{9,10},{10,... | collective-permute-start | bytes 110600 | tf_op jit(solution)/shard_map/sum_req/ppermute | solution.py:283
  53.9 5.5 %collective-permute-start.16 = (f32[136,128]{1,0:T(8,128)S(1)}, f32[136,128]{1,0:T(8,128)S(1)}, u32[]{:S(2)}, u32[]{:S(2)}) collective-permute-start(f32[136,128]{1,0:T(8,128)S(1)} %add.87), channel_id=1, source_target_pairs={{0,1},{1,0},{2,3},{3,2},{4,52},{5,53},{6,54},{7,55},{8,9},{9,8},{1... | collective-permute-start | bytes 208904 | tf_op jit(solution)/shard_map/sum_z_outer/ppermute | solution.py:274
  59.3 4.1 %collective-permute-start.19 = (f32[136,128]{1,0:T(8,128)S(1)}, f32[136,128]{1,0:T(8,128)S(1)}, u32[]{:S(2)}, u32[]{:S(2)}) collective-permute-start(f32[136,128]{1,0:T(8,128)S(1)} %add.88), channel_id=1, source_target_pairs={{0,1},{1,0},{2,3},{3,2},{4,20},{5,21},{6,22},{7,23},{8,9},{9,8},{1... | collective-permute-start | bytes 208904 | tf_op jit(solution)/shard_map/sum_z_inner/ppermute | solution.py:274
  61.4 5.1 %collective-permute-start.18 = (f32[136,128]{1,0:T(8,128)S(1)}, f32[136,128]{1,0:T(8,128)S(1)}, u32[]{:S(2)}, u32[]{:S(2)}) collective-permute-start(f32[136,128]{1,0:T(8,128)S(1)} %add.88), channel_id=1, source_target_pairs={{0,1},{1,0},{2,3},{3,2},{4,28},{5,29},{6,30},{7,31},{8,9},{9,8},{1... | collective-permute-start | bytes 208904 | tf_op jit(solution)/shard_map/sum_z_inner/ppermute | solution.py:274
  63.1 3.9 %collective-permute-start.17 = (f32[136,128]{1,0:T(8,128)S(1)}, f32[136,128]{1,0:T(8,128)S(1)}, u32[]{:S(2)}, u32[]{:S(2)}) collective-permute-start(f32[136,128]{1,0:T(8,128)S(1)} %add.88), channel_id=1, source_target_pairs={{0,1},{1,0},{2,3},{3,2},{4,12},{5,13},{6,14},{7,15},{8,9},{9,8},{1... | collective-permute-start | bytes 208904 | tf_op jit(solution)/shard_map/sum_z_inner/ppermute | solution.py:274
  67.1 4.8 %collective-permute-start.22 = (f32[136,128]{1,0:T(8,128)S(1)}, f32[136,128]{1,0:T(8,128)S(1)}, u32[]{:S(2)}, u32[]{:S(2)}) collective-permute-start(f32[136,128]{1,0:T(8,128)S(1)} %add_add_fusion.3), channel_id=1, source_target_pairs={{0,1},{1,0},{2,3},{3,2},{4,132},{5,133},{6,134},{7,135},{8,9},{9,8... | collective-permute-start | bytes 208904 | tf_op jit(solution)/shard_map/sum_y/ppermute | solution.py:274
  68.3 4.4 %collective-permute-start.21 = (f32[136,128]{1,0:T(8,128)S(1)}, f32[136,128]{1,0:T(8,128)S(1)}, u32[]{:S(2)}, u32[]{:S(2)}) collective-permute-start(f32[136,128]{1,0:T(8,128)S(1)} %add_add_fusion.3), channel_id=1, source_target_pairs={{0,1},{1,0},{2,3},{3,2},{4,196},{5,197},{6,198},{7,199},{8,9},{9,8... | collective-permute-start | bytes 208904 | tf_op jit(solution)/shard_map/sum_y/ppermute | solution.py:274
  69.1 3.6 %collective-permute-start.20 = (f32[136,128]{1,0:T(8,128)S(1)}, f32[136,128]{1,0:T(8,128)S(1)}, u32[]{:S(2)}, u32[]{:S(2)}) collective-permute-start(f32[136,128]{1,0:T(8,128)S(1)} %add_add_fusion.3), channel_id=1, source_target_pairs={{0,1},{1,0},{2,3},{3,2},{4,68},{5,69},{6,70},{7,71},{8,9},{9,8},{1... | collective-permute-start | bytes 208904 | tf_op jit(solution)/shard_map/sum_y/ppermute | solution.py:274
  75.1 4.3 %collective-permute-start.26 = (f32[72,128]{1,0:T(8,128)S(1)}, f32[72,128]{1,0:T(8,128)S(1)}, u32[]{:S(2)}, u32[]{:S(2)}) collective-permute-start(f32[72,128]{1,0:T(8,128)S(1)} %get-tuple-element.63.refs_0_), channel_id=1, source_target_pairs={{0,2},{1,3},{2,0},{3,1},{4,6},{5,7},{6,4},{7,5},{8,10},{9,11},{10,... | collective-permute-start | bytes 110600 | tf_op jit(solution)/shard_map/sum_req/ppermute | solution.py:283
  76.3 4.1 %collective-permute-start.25 = (f32[72,128]{1,0:T(8,128)S(1)}, f32[72,128]{1,0:T(8,128)S(1)}, u32[]{:S(2)}, u32[]{:S(2)}) collective-permute-start(f32[72,128]{1,0:T(8,128)S(1)} %get-tuple-element.63.refs_0_), channel_id=1, source_target_pairs={{0,3},{1,2},{2,1},{3,0},{4,7},{5,6},{6,5},{7,4},{8,11},{9,10},{10,... | collective-permute-start | bytes 110600 | tf_op jit(solution)/shard_map/sum_req/ppermute | solution.py:283
  77.2 3.3 %collective-permute-start.24 = (f32[72,128]{1,0:T(8,128)S(1)}, f32[72,128]{1,0:T(8,128)S(1)}, u32[]{:S(2)}, u32[]{:S(2)}) collective-permute-start(f32[72,128]{1,0:T(8,128)S(1)} %get-tuple-element.63.refs_0_), channel_id=1, source_target_pairs={{0,1},{1,0},{2,3},{3,2},{4,5},{5,4},{6,7},{7,6},{8,9},{9,8},{10,11... | collective-permute-start | bytes 110600 | tf_op jit(solution)/shard_map/sum_req/ppermute | solution.py:283
  84.5 5.4 %collective-permute-start.28 = (f32[136,128]{1,0:T(8,128)S(1)}, f32[136,128]{1,0:T(8,128)S(1)}, u32[]{:S(2)}, u32[]{:S(2)}) collective-permute-start(f32[136,128]{1,0:T(8,128)S(1)} %add.95), channel_id=1, source_target_pairs={{0,1},{1,0},{2,3},{3,2},{4,52},{5,53},{6,54},{7,55},{8,9},{9,8},{1... | collective-permute-start | bytes 208904 | tf_op jit(solution)/shard_map/sum_z_outer/ppermute | solution.py:274
  89.9 4.9 %collective-permute-start.31 = (f32[136,128]{1,0:T(8,128)S(1)}, f32[136,128]{1,0:T(8,128)S(1)}, u32[]{:S(2)}, u32[]{:S(2)}) collective-permute-start(f32[136,128]{1,0:T(8,128)S(1)} %add.96), channel_id=1, source_target_pairs={{0,1},{1,0},{2,3},{3,2},{4,20},{5,21},{6,22},{7,23},{8,9},{9,8},{1... | collective-permute-start | bytes 208904 | tf_op jit(solution)/shard_map/sum_z_inner/ppermute | solution.py:274
  90.8 5.1 %collective-permute-start.30 = (f32[136,128]{1,0:T(8,128)S(1)}, f32[136,128]{1,0:T(8,128)S(1)}, u32[]{:S(2)}, u32[]{:S(2)}) collective-permute-start(f32[136,128]{1,0:T(8,128)S(1)} %add.96), channel_id=1, source_target_pairs={{0,1},{1,0},{2,3},{3,2},{4,28},{5,29},{6,30},{7,31},{8,9},{9,8},{1... | collective-permute-start | bytes 208904 | tf_op jit(solution)/shard_map/sum_z_inner/ppermute | solution.py:274
  92.4 3.9 %collective-permute-start.29 = (f32[136,128]{1,0:T(8,128)S(1)}, f32[136,128]{1,0:T(8,128)S(1)}, u32[]{:S(2)}, u32[]{:S(2)}) collective-permute-start(f32[136,128]{1,0:T(8,128)S(1)} %add.96), channel_id=1, source_target_pairs={{0,1},{1,0},{2,3},{3,2},{4,12},{5,13},{6,14},{7,15},{8,9},{9,8},{1... | collective-permute-start | bytes 208904 | tf_op jit(solution)/shard_map/sum_z_inner/ppermute | solution.py:274
  96.3 4.8 %collective-permute-start.34 = (f32[136,128]{1,0:T(8,128)S(1)}, f32[136,128]{1,0:T(8,128)S(1)}, u32[]{:S(2)}, u32[]{:S(2)}) collective-permute-start(f32[136,128]{1,0:T(8,128)S(1)} %add_add_fusion.1), channel_id=1, source_target_pairs={{0,1},{1,0},{2,3},{3,2},{4,132},{5,133},{6,134},{7,135},{8,9},{9,8... | collective-permute-start | bytes 208904 | tf_op jit(solution)/shard_map/sum_y/ppermute | solution.py:274
  97.6 4.4 %collective-permute-start.33 = (f32[136,128]{1,0:T(8,128)S(1)}, f32[136,128]{1,0:T(8,128)S(1)}, u32[]{:S(2)}, u32[]{:S(2)}) collective-permute-start(f32[136,128]{1,0:T(8,128)S(1)} %add_add_fusion.1), channel_id=1, source_target_pairs={{0,1},{1,0},{2,3},{3,2},{4,196},{5,197},{6,198},{7,199},{8,9},{9,8... | collective-permute-start | bytes 208904 | tf_op jit(solution)/shard_map/sum_y/ppermute | solution.py:274
  98.7 3.3 %collective-permute-start.32 = (f32[136,128]{1,0:T(8,128)S(1)}, f32[136,128]{1,0:T(8,128)S(1)}, u32[]{:S(2)}, u32[]{:S(2)}) collective-permute-start(f32[136,128]{1,0:T(8,128)S(1)} %add_add_fusion.1), channel_id=1, source_target_pairs={{0,1},{1,0},{2,3},{3,2},{4,68},{5,69},{6,70},{7,71},{8,9},{9,8},{1... | collective-permute-start | bytes 208904 | tf_op jit(solution)/shard_map/sum_y/ppermute | solution.py:274
  102.1 7.5 %collective-permute-start.35 = (f32[136,128]{1,0:T(8,128)S(1)}, f32[136,128]{1,0:T(8,128)S(1)}, u32[]{:S(2)}, u32[]{:S(2)}) collective-permute-start(f32[136,128]{1,0:T(8,128)S(1)} %constant_dynamic-update-slice_fusion.state_own), channel_id=1, source_target_pairs={{0,4},{1,5},{2,6},{3,7},{4,0},{5,1},{6,2},{7,3},{8,12},{9,13},{10,... | collective-permute-start | bytes 208904 | tf_op jit(solution)/shard_map/back_core/ppermute | solution.py:274
  102.6 4.0 %collective-permute-start.38 = (f32[8,128]{1,0:T(8,128)S(1)}, f32[8,128]{1,0:T(8,128)S(1)}, u32[]{:S(2)}, u32[]{:S(2)}) collective-permute-start(f32[8,128]{1,0:T(8,128)S(1)} %get-tuple-element.74.last_0), channel_id=1, source_target_pairs={{0,64},{1,65},{2,66},{3,67},{4,6},{5,7},{6,4},{7,5},{8,72},{9,73},... | collective-permute-start | bytes 12296 | tf_op jit(solution)/shard_map/sum_req_last/ppermute | solution.py:274
  104.6 3.7 %collective-permute-start.37 = (f32[8,128]{1,0:T(8,128)S(1)}, f32[8,128]{1,0:T(8,128)S(1)}, u32[]{:S(2)}, u32[]{:S(2)}) collective-permute-start(f32[8,128]{1,0:T(8,128)S(1)} %get-tuple-element.74.last_0), channel_id=1, source_target_pairs={{0,64},{1,65},{2,66},{3,67},{4,7},{5,6},{6,5},{7,4},{8,72},{9,73},... | collective-permute-start | bytes 12296 | tf_op jit(solution)/shard_map/sum_req_last/ppermute | solution.py:274
  (13 other events, 114.6 us)

commit v3 on v2

--- a/solution.py
+++ b/solution.py
@@ -82,19 +82,23 @@
     return [fetched.at[n] for n in range(fetched.shape[0])]
 
 
-def rest_kernel(tiles_in, after, *refs):
+def rest_kernel(tiles_in, pick_rows, place_cols, place_rows, pick_cols, *refs):
     kept, sems = refs[:-1], refs[-1]
     copies = []
     for n, target in enumerate(kept):
         part = tiles_in.at[pl.ds((KEPT + n) * GROUP, GROUP)]
         copies.append(pltpu.make_async_copy(part, target, sems.at[n]))
         copies[-1].start()
+    place_rows[...] = pick_rows[...].astype(F32).T
+    slots, test_blocks = pick_cols.shape[0], place_cols.shape[0]
+    padded = jnp.concatenate([place_cols[...], jnp.zeros((slots - test_blocks, slots), F32)], axis=0)
+    pick_cols[...] = padded.T.astype(BF16)
     for copy in copies:
         copy.wait()
 
 
 def first_pull_kernel(
-    tiles_in, dual_in, rows_in, cols_in, live_in, pull_out, pick_rows, place_rows, pick_cols, place_cols, *refs
+    tiles_in, dual_in, rows_in, cols_in, live_in, pull_out, pick_rows, place_cols, *refs
 ):
     slots = tiles_in.shape[0]
     groups = slots // GROUP
@@ -116,12 +120,9 @@
     at_row = lax.broadcasted_iota(jnp.int32, (req_blocks, slots), 0) == rows[...]
     at_col = lax.broadcasted_iota(jnp.int32, (test_blocks, slots), 0) == cols[...]
     one_row = jnp.where(at_row, 1.0, 0.0)
-    one_col = jnp.where(at_col, 1.0, 0.0)
-    place_rows[...] = jnp.where(alive, one_row, 0.0)
-    place_cols[...] = jnp.where(alive, one_col, 0.0)
+    place_cols[...] = jnp.where(at_col & alive, 1.0, 0.0)
     pick = one_row.T.astype(BF16)
     pick_rows[...] = pick
-    pick_cols[...] = jnp.concatenate([one_col, jnp.zeros((slots - test_blocks, slots), F32)], axis=0).T.astype(BF16)
     picked = gather_rows(pick, dual[...])
     contrib = []
     for group in range(groups):
@@ -318,20 +319,23 @@
             given = (
                 coverage_tiles, dual, tile_rows.reshape(1, slots), tile_cols.reshape(1, slots), tile_counts.reshape(1, 1)
             )
-            pull, pick_rows, place_rows, pick_cols, place_cols, *tiles = call(
+            pull, pick_rows, place_cols, *tiles = call(
                 first_pull_kernel,
                 (
-                    pull_shape, struct(slots, req_blocks, dtype=BF16), struct(req_blocks, slots),
-                    struct(slots, slots, dtype=BF16), struct(test_blocks, slots),
+                    pull_shape, struct(slots, req_blocks, dtype=BF16), struct(test_blocks, slots),
                     *[group_shape] * KEPT,
                 ),
                 [HBM] * len(given),
                 [pltpu.VMEM((rest, *group_shape.shape), BF16), *[pltpu.VMEM(x.shape, x.dtype) for x in given[1:]]]
                 + [pltpu.SemaphoreType.DMA((n,)) for n in (len(given) - 1, slots // GROUP)],
             )(*[pltpu.with_memory_space_constraint(x, pltpu.HBM) for x in given[:4]], given[4])
-            tiles += call(
-                rest_kernel, [group_shape] * rest, [HBM, VMEM], [pltpu.SemaphoreType.DMA((rest,))]
-            )(coverage_tiles, pick_cols)
+            place_rows, pick_cols, *more = call(
+                rest_kernel,
+                [struct(req_blocks, slots), struct(slots, slots, dtype=BF16)] + [group_shape] * rest,
+                [HBM, VMEM, VMEM],
+                [pltpu.SemaphoreType.DMA((rest,))],
+            )(coverage_tiles, pick_rows, place_cols)
+            tiles += more
         else:
             given = (summed, params, pick_rows, place_cols, dual, scal, want, *tiles, *sum_dual)
             pull, dual, total, scal = call(

time: 110 us -> 110 us (level)
  transfers between devices with their start and end apart: 40 -> 40, of which waited for: 31 -> 31; matrix products, arithmetic and copies ran while one was open for 1% -> 0% of each run, Pallas kernels for 1% -> 1%
where the time goes in v3:
time: 110 us
  starting transfers between devices  50.5 us (46%)
  waiting for transfers between devices  42.9 us (39%)
  Pallas kernels  13 us (12%)
  between operations  2.83 us (3%)
    ppermute x31, starting transfers between devices, on_mesh(): return lax.ppermute(x, ('tst', 'req'), pairs)  40.4 us
    ppermute x31, waiting for transfers between devices, on_mesh(): return lax.ppermute(x, ('tst', 'req'), pairs)  36.4 us
    ppermute x9, starting transfers between devices, on_req(): lax.ppermute(x, 'req', [(i, i ^ bit) for i in range(n_req)])  10.1 us
    ppermute x9, waiting for transfers between devices, on_req(): lax.ppermute(x, 'req', [(i, i ^ bit) for i in range(n_req)])  6.56 us
    pallas_call x3, Pallas kernels, per_device(): call(functools.partial(primal_load_kernel, iteration), outs, [VMEM] * len...  4.7 us
    pallas_call x1, Pallas kernels, per_device(): call(first_pull_kernel, (pull_shape, struct(slots, req_blocks, dtype=BF16...  4.07 us
  transfers between devices with their start and end apart: 40, of which 31 were waited for; matrix products, arithmetic and copies ran while one was open for 0% of the time, Pallas kernels for 1%

profile of v3, /device:TPU:1, one launch (start us, length us, event | category | flops | bytes accessed | tf_op | source)
XLA Modules:
  0.0 109.7 jit_solution(4882826974510171269)
XLA Ops:
  1.3 4.1 %shard_map.147 = (f32[72,128]{1,0:T(8,128)S(1)}, bf16[128,128]{1,0:T(8,128)(2,1)S(1)}, f32[64,128]{1,0:T(8,128)S(1)}, bf16[16,128,128]{2,1,0:T(8,128)(2,1)S(1)},...) custom-call(bf16[128,128,128]{2,1,0:T(8,128)(2,1)} %tiles_in.3, ...), custom_call_target="tpu_custom_call" | custom-call | tf_op jit(solution)/shard_map/pallas_call | solution.py:322
  5.4 3.7 %collective-permute-start.2 = (f32[72,128]{1,0:T(8,128)S(1)}, f32[72,128]{1,0:T(8,128)S(1)}, u32[]{:S(2)}, u32[]{:S(2)}) collective-permute-start(f32[72,128]{1,0:T(8,128)S(1)} %get-tuple-element.42.refs_0_), channel_id=1, source_target_pairs={{0,2},{1,3},{2,0},{3,1},{4,6},{5,7},{6,4},{7,5},{8,10},{9,11},{10,... | collective-permute-start | bytes 110600 | tf_op jit(solution)/shard_map/sum_req/ppermute | solution.py:284
  13.5 1.6 %shard_map.149 = (f32[136,128]{1,0:T(8,128)S(1)}, f32[64,128]{1,0:T(8,128)S(1)}, f32[64,128]{1,0:T(8,128)S(1)}) custom-call(f32[72,128]{1,0:T(8,128)S(1)} %get-tuple-element.42.refs_0_, f32[72,128]{1,0:T(8,128)S(1)} %collective-permute-done.refs_1_, f32[72,128]{1,0:T(8,128)S(1)} %collective-permute-done.1.refs_2_, ...), custom_call_target="tpu_custom_call" | custom-call | tf_op jit(solution)/shard_map/pallas_call | solution.py:351
  15.1 1.9 %collective-permute-start.3 = (f32[136,128]{1,0:T(8,128)S(1)}, f32[136,128]{1,0:T(8,128)S(1)}, u32[]{:S(2)}, u32[]{:S(2)}) collective-permute-start(f32[136,128]{1,0:T(8,128)S(1)} %get-tuple-element.55), channel_id=1, source_target_pairs={{0,4},{1,5},{2,6},{3,7},{4,0},{5,1},{6,2},{7,3},{8,12},{9,13},{10,... | collective-permute-start | bytes 208904 | tf_op jit(solution)/shard_map/sum_core/ppermute | solution.py:275
  17.9 6.1 %collective-permute-start.4 = (f32[136,128]{1,0:T(8,128)S(1)}, f32[136,128]{1,0:T(8,128)S(1)}, u32[]{:S(2)}, u32[]{:S(2)}) collective-permute-start(f32[136,128]{1,0:T(8,128)S(1)} %add.79), channel_id=1, source_target_pairs={{0,1},{1,0},{2,3},{3,2},{4,52},{5,53},{6,54},{7,55},{8,9},{9,8},{1... | collective-permute-start | bytes 208904 | tf_op jit(solution)/shard_map/sum_z_outer/ppermute | solution.py:275
  24.0 1.8 %collective-permute-done.4 = f32[136,128]{1,0:T(8,128)S(1)} collective-permute-done((f32[136,128]{1,0:T(8,128)S(1)}, f32[136,128]{1,0:T(8,128)S(1)}, u32[]{:S(2)}, u32[]{:S(2)}) %collective-permute-start.4) | collective-permute-done | bytes 69664 | tf_op jit(solution)/shard_map/sum_z_outer/ppermute | solution.py:275
  27.0 2.4 %collective-permute-start.6 = (f32[136,128]{1,0:T(8,128)S(1)}, f32[136,128]{1,0:T(8,128)S(1)}, u32[]{:S(2)}, u32[]{:S(2)}) collective-permute-start(f32[136,128]{1,0:T(8,128)S(1)} %add.80), channel_id=1, source_target_pairs={{0,1},{1,0},{2,3},{3,2},{4,28},{5,29},{6,30},{7,31},{8,9},{9,8},{1... | collective-permute-start | bytes 208904 | tf_op jit(solution)/shard_map/sum_z_inner/ppermute | solution.py:275
  30.0 2.1 %collective-permute-done.6 = f32[136,128]{1,0:T(8,128)S(1)} collective-permute-done((f32[136,128]{1,0:T(8,128)S(1)}, f32[136,128]{1,0:T(8,128)S(1)}, u32[]{:S(2)}, u32[]{:S(2)}) %collective-permute-start.6) | collective-permute-done | bytes 69664 | tf_op jit(solution)/shard_map/sum_z_inner/ppermute | solution.py:275
  33.1 3.0 %collective-permute-start.10 = (f32[136,128]{1,0:T(8,128)S(1)}, f32[136,128]{1,0:T(8,128)S(1)}, u32[]{:S(2)}, u32[]{:S(2)}) collective-permute-start(f32[136,128]{1,0:T(8,128)S(1)} %add_add_fusion.5), channel_id=1, source_target_pairs={{0,1},{1,0},{2,3},{3,2},{4,132},{5,133},{6,134},{7,135},{8,9},{9,8... | collective-permute-start | bytes 208904 | tf_op jit(solution)/shard_map/sum_y/ppermute | solution.py:275
  37.8 2.6 %collective-permute-done.9 = f32[136,128]{1,0:T(8,128)S(1)} collective-permute-done((f32[136,128]{1,0:T(8,128)S(1)}, f32[136,128]{1,0:T(8,128)S(1)}, u32[]{:S(2)}, u32[]{:S(2)}) %collective-permute-start.9) | collective-permute-done | bytes 69664 | tf_op jit(solution)/shard_map/sum_y/ppermute | solution.py:275
  42.9 2.0 %collective-permute-start.14 = (f32[72,128]{1,0:T(8,128)S(1)}, f32[72,128]{1,0:T(8,128)S(1)}, u32[]{:S(2)}, u32[]{:S(2)}) collective-permute-start(f32[72,128]{1,0:T(8,128)S(1)} %get-tuple-element.56.refs_0_), channel_id=1, source_target_pairs={{0,2},{1,3},{2,0},{3,1},{4,6},{5,7},{6,4},{7,5},{8,10},{9,11},{10,... | collective-permute-start | bytes 110600 | tf_op jit(solution)/shard_map/sum_req/ppermute | solution.py:284
  45.8 1.5 %collective-permute-done.14.refs_3_ = f32[72,128]{1,0:T(8,128)S(1)} collective-permute-done((f32[72,128]{1,0:T(8,128)S(1)}, f32[72,128]{1,0:T(8,128)S(1)}, u32[]{:S(2)}, u32[]{:S(2)}) %collective-permute-start.14) | collective-permute-done | bytes 36896 | tf_op jit(solution)/shard_map/sum_req/ppermute | solution.py:284
  47.2 1.7 %collective-permute-done.13.refs_2_ = f32[72,128]{1,0:T(8,128)S(1)} collective-permute-done((f32[72,128]{1,0:T(8,128)S(1)}, f32[72,128]{1,0:T(8,128)S(1)}, u32[]{:S(2)}, u32[]{:S(2)}) %collective-permute-start.13) | collective-permute-done | bytes 36896 | tf_op jit(solution)/shard_map/sum_req/ppermute | solution.py:284
  48.9 1.6 %shard_map.151 = (f32[136,128]{1,0:T(8,128)S(1)}, f32[64,128]{1,0:T(8,128)S(1)}, f32[64,128]{1,0:T(8,128)S(1)}, f32[8,128]{1,0:T(8,128)S(1)}) custom-call(f32[72,128]{1,0:T(8,128)S(1)} %get-tuple-element.56.refs_0_, f32[72,128]{1,0:T(8,128)S(1)} %collective-permute-done.12.refs_1_, f32[72,128]{1,0:T(8,128)S(1)} %collective-permute-done.13.refs_2_, ...), custom_call_target="tpu_custom_call" | custom-call | tf_op jit(solution)/shard_map/pallas_call | solution.py:351
  50.5 1.9 %collective-permute-start.15 = (f32[136,128]{1,0:T(8,128)S(1)}, f32[136,128]{1,0:T(8,128)S(1)}, u32[]{:S(2)}, u32[]{:S(2)}) collective-permute-start(f32[136,128]{1,0:T(8,128)S(1)} %get-tuple-element.60), channel_id=1, source_target_pairs={{0,4},{1,5},{2,6},{3,7},{4,0},{5,1},{6,2},{7,3},{8,12},{9,13},{10,... | collective-permute-start | bytes 208904 | tf_op jit(solution)/shard_map/sum_core/ppermute | solution.py:275
  53.3 3.2 %collective-permute-start.16 = (f32[136,128]{1,0:T(8,128)S(1)}, f32[136,128]{1,0:T(8,128)S(1)}, u32[]{:S(2)}, u32[]{:S(2)}) collective-permute-start(f32[136,128]{1,0:T(8,128)S(1)} %add.87), channel_id=1, source_target_pairs={{0,1},{1,0},{2,3},{3,2},{4,52},{5,53},{6,54},{7,55},{8,9},{9,8},{1... | collective-permute-start | bytes 208904 | tf_op jit(solution)/shard_map/sum_z_outer/ppermute | solution.py:275
  56.4 2.3 %collective-permute-done.16 = f32[136,128]{1,0:T(8,128)S(1)} collective-permute-done((f32[136,128]{1,0:T(8,128)S(1)}, f32[136,128]{1,0:T(8,128)S(1)}, u32[]{:S(2)}, u32[]{:S(2)}) %collective-permute-start.16) | collective-permute-done | bytes 69664 | tf_op jit(solution)/shard_map/sum_z_outer/ppermute | solution.py:275
  58.7 2.0 %collective-permute-start.19 = (f32[136,128]{1,0:T(8,128)S(1)}, f32[136,128]{1,0:T(8,128)S(1)}, u32[]{:S(2)}, u32[]{:S(2)}) collective-permute-start(f32[136,128]{1,0:T(8,128)S(1)} %add.88), channel_id=1, source_target_pairs={{0,1},{1,0},{2,3},{3,2},{4,20},{5,21},{6,22},{7,23},{8,9},{9,8},{1... | collective-permute-start | bytes 208904 | tf_op jit(solution)/shard_map/sum_z_inner/ppermute | solution.py:275
  60.8 1.8 %collective-permute-start.18 = (f32[136,128]{1,0:T(8,128)S(1)}, f32[136,128]{1,0:T(8,128)S(1)}, u32[]{:S(2)}, u32[]{:S(2)}) collective-permute-start(f32[136,128]{1,0:T(8,128)S(1)} %add.88), channel_id=1, source_target_pairs={{0,1},{1,0},{2,3},{3,2},{4,28},{5,29},{6,30},{7,31},{8,9},{9,8},{1... | collective-permute-start | bytes 208904 | tf_op jit(solution)/shard_map/sum_z_inner/ppermute | solution.py:275
  62.9 2.9 %collective-permute-done.18 = f32[136,128]{1,0:T(8,128)S(1)} collective-permute-done((f32[136,128]{1,0:T(8,128)S(1)}, f32[136,128]{1,0:T(8,128)S(1)}, u32[]{:S(2)}, u32[]{:S(2)}) %collective-permute-start.18) | collective-permute-done | bytes 69664 | tf_op jit(solution)/shard_map/sum_z_inner/ppermute | solution.py:275
  69.2 2.0 %collective-permute-done.22 = f32[136,128]{1,0:T(8,128)S(1)} collective-permute-done((f32[136,128]{1,0:T(8,128)S(1)}, f32[136,128]{1,0:T(8,128)S(1)}, u32[]{:S(2)}, u32[]{:S(2)}) %collective-permute-start.22) | collective-permute-done | bytes 69664 | tf_op jit(solution)/shard_map/sum_y/ppermute | solution.py:275
  77.2 1.7 %collective-permute-done.26.refs_3_ = f32[72,128]{1,0:T(8,128)S(1)} collective-permute-done((f32[72,128]{1,0:T(8,128)S(1)}, f32[72,128]{1,0:T(8,128)S(1)}, u32[]{:S(2)}, u32[]{:S(2)}) %collective-permute-start.26) | collective-permute-done | bytes 36896 | tf_op jit(solution)/shard_map/sum_req/ppermute | solution.py:284
  79.9 1.6 %shard_map.153 = (f32[136,128]{1,0:T(8,128)S(1)}, f32[64,128]{1,0:T(8,128)S(1)}, f32[8,128]{1,0:T(8,128)S(1)}) custom-call(f32[72,128]{1,0:T(8,128)S(1)} %get-tuple-element.63.refs_0_, f32[72,128]{1,0:T(8,128)S(1)} %collective-permute-done.24.refs_1_, f32[72,128]{1,0:T(8,128)S(1)} %collective-permute-done.25.refs_2_, ...), custom_call_target="tpu_custom_call" | custom-call | tf_op jit(solution)/shard_map/pallas_call | solution.py:351
  81.4 1.5 %collective-permute-start.27 = (f32[136,128]{1,0:T(8,128)S(1)}, f32[136,128]{1,0:T(8,128)S(1)}, u32[]{:S(2)}, u32[]{:S(2)}) collective-permute-start(f32[136,128]{1,0:T(8,128)S(1)} %get-tuple-element.67), channel_id=1, source_target_pairs={{0,4},{1,5},{2,6},{3,7},{4,0},{5,1},{6,2},{7,3},{8,12},{9,13},{10,... | collective-permute-start | bytes 208904 | tf_op jit(solution)/shard_map/sum_core/ppermute | solution.py:275
  83.9 2.6 %collective-permute-start.28 = (f32[136,128]{1,0:T(8,128)S(1)}, f32[136,128]{1,0:T(8,128)S(1)}, u32[]{:S(2)}, u32[]{:S(2)}) collective-permute-start(f32[136,128]{1,0:T(8,128)S(1)} %add.95), channel_id=1, source_target_pairs={{0,1},{1,0},{2,3},{3,2},{4,52},{5,53},{6,54},{7,55},{8,9},{9,8},{1... | collective-permute-start | bytes 208904 | tf_op jit(solution)/shard_map/sum_z_outer/ppermute | solution.py:275
  86.5 2.8 %collective-permute-done.28 = f32[136,128]{1,0:T(8,128)S(1)} collective-permute-done((f32[136,128]{1,0:T(8,128)S(1)}, f32[136,128]{1,0:T(8,128)S(1)}, u32[]{:S(2)}, u32[]{:S(2)}) %collective-permute-start.28) | collective-permute-done | bytes 69664 | tf_op jit(solution)/shard_map/sum_z_outer/ppermute | solution.py:275
  90.2 1.6 %collective-permute-start.30 = (f32[136,128]{1,0:T(8,128)S(1)}, f32[136,128]{1,0:T(8,128)S(1)}, u32[]{:S(2)}, u32[]{:S(2)}) collective-permute-start(f32[136,128]{1,0:T(8,128)S(1)} %add.96), channel_id=1, source_target_pairs={{0,1},{1,0},{2,3},{3,2},{4,28},{5,29},{6,30},{7,31},{8,9},{9,8},{1... | collective-permute-start | bytes 208904 | tf_op jit(solution)/shard_map/sum_z_inner/ppermute | solution.py:275
  92.0 2.2 %collective-permute-done.31 = f32[136,128]{1,0:T(8,128)S(1)} collective-permute-done((f32[136,128]{1,0:T(8,128)S(1)}, f32[136,128]{1,0:T(8,128)S(1)}, u32[]{:S(2)}, u32[]{:S(2)}) %collective-permute-start.31) | collective-permute-done | bytes 69664 | tf_op jit(solution)/shard_map/sum_z_inner/ppermute | solution.py:275
  95.7 1.3 %collective-permute-start.34 = (f32[136,128]{1,0:T(8,128)S(1)}, f32[136,128]{1,0:T(8,128)S(1)}, u32[]{:S(2)}, u32[]{:S(2)}) collective-permute-start(f32[136,128]{1,0:T(8,128)S(1)} %add_add_fusion.1), channel_id=1, source_target_pairs={{0,1},{1,0},{2,3},{3,2},{4,132},{5,133},{6,134},{7,135},{8,9},{9,8... | collective-permute-start | bytes 208904 | tf_op jit(solution)/shard_map/sum_y/ppermute | solution.py:275
  98.5 2.0 %collective-permute-done.34 = f32[136,128]{1,0:T(8,128)S(1)} collective-permute-done((f32[136,128]{1,0:T(8,128)S(1)}, f32[136,128]{1,0:T(8,128)S(1)}, u32[]{:S(2)}, u32[]{:S(2)}) %collective-permute-start.34) | collective-permute-done | bytes 69664 | tf_op jit(solution)/shard_map/sum_y/ppermute | solution.py:275
  102.0 2.0 %collective-permute-start.38 = (f32[8,128]{1,0:T(8,128)S(1)}, f32[8,128]{1,0:T(8,128)S(1)}, u32[]{:S(2)}, u32[]{:S(2)}) collective-permute-start(f32[8,128]{1,0:T(8,128)S(1)} %get-tuple-element.74.last_0), channel_id=1, source_target_pairs={{0,64},{1,65},{2,66},{3,67},{4,6},{5,7},{6,4},{7,5},{8,72},{9,73},... | collective-permute-start | bytes 12296 | tf_op jit(solution)/shard_map/sum_req_last/ppermute | solution.py:275
  105.9 1.7 %collective-permute-done.37.last_2 = f32[8,128]{1,0:T(8,128)S(1)} collective-permute-done((f32[8,128]{1,0:T(8,128)S(1)}, f32[8,128]{1,0:T(8,128)S(1)}, u32[]{:S(2)}, u32[]{:S(2)}) %collective-permute-start.37) | collective-permute-done | bytes 4128 | tf_op jit(solution)/shard_map/sum_req_last/ppermute | solution.py:275
  (92 shorter events, 34.0 us)
Async XLA Ops:
  5.4 7.2 %collective-permute-start.2 = (f32[72,128]{1,0:T(8,128)S(1)}, f32[72,128]{1,0:T(8,128)S(1)}, u32[]{:S(2)}, u32[]{:S(2)}) collective-permute-start(f32[72,128]{1,0:T(8,128)S(1)} %get-tuple-element.42.refs_0_), channel_id=1, source_target_pairs={{0,2},{1,3},{2,0},{3,1},{4,6},{5,7},{6,4},{7,5},{8,10},{9,11},{10,... | collective-permute-start | bytes 110600 | tf_op jit(solution)/shard_map/sum_req/ppermute | solution.py:284
  9.1 4.3 %collective-permute-start.1 = (f32[72,128]{1,0:T(8,128)S(1)}, f32[72,128]{1,0:T(8,128)S(1)}, u32[]{:S(2)}, u32[]{:S(2)}) collective-permute-start(f32[72,128]{1,0:T(8,128)S(1)} %get-tuple-element.42.refs_0_), channel_id=1, source_target_pairs={{0,3},{1,2},{2,1},{3,0},{4,7},{5,6},{6,5},{7,4},{8,11},{9,10},{10,... | collective-permute-start | bytes 110600 | tf_op jit(solution)/shard_map/sum_req/ppermute | solution.py:284
  9.9 3.5 %collective-permute-start = (f32[72,128]{1,0:T(8,128)S(1)}, f32[72,128]{1,0:T(8,128)S(1)}, u32[]{:S(2)}, u32[]{:S(2)}) collective-permute-start(f32[72,128]{1,0:T(8,128)S(1)} %get-tuple-element.42.refs_0_), channel_id=1, source_target_pairs={{0,1},{1,0},{2,3},{3,2},{4,5},{5,4},{6,7},{7,6},{8,9},{9,8},{10,11... | collective-permute-start | bytes 110600 | tf_op jit(solution)/shard_map/sum_req/ppermute | solution.py:284
  17.9 7.9 %collective-permute-start.4 = (f32[136,128]{1,0:T(8,128)S(1)}, f32[136,128]{1,0:T(8,128)S(1)}, u32[]{:S(2)}, u32[]{:S(2)}) collective-permute-start(f32[136,128]{1,0:T(8,128)S(1)} %add.79), channel_id=1, source_target_pairs={{0,1},{1,0},{2,3},{3,2},{4,52},{5,53},{6,54},{7,55},{8,9},{9,8},{1... | collective-permute-start | bytes 208904 | tf_op jit(solution)/shard_map/sum_z_outer/ppermute | solution.py:275
  25.8 4.1 %collective-permute-start.7 = (f32[136,128]{1,0:T(8,128)S(1)}, f32[136,128]{1,0:T(8,128)S(1)}, u32[]{:S(2)}, u32[]{:S(2)}) collective-permute-start(f32[136,128]{1,0:T(8,128)S(1)} %add.80), channel_id=1, source_target_pairs={{0,1},{1,0},{2,3},{3,2},{4,20},{5,21},{6,22},{7,23},{8,9},{9,8},{1... | collective-permute-start | bytes 208904 | tf_op jit(solution)/shard_map/sum_z_inner/ppermute | solution.py:275
  27.0 5.0 %collective-permute-start.6 = (f32[136,128]{1,0:T(8,128)S(1)}, f32[136,128]{1,0:T(8,128)S(1)}, u32[]{:S(2)}, u32[]{:S(2)}) collective-permute-start(f32[136,128]{1,0:T(8,128)S(1)} %add.80), channel_id=1, source_target_pairs={{0,1},{1,0},{2,3},{3,2},{4,28},{5,29},{6,30},{7,31},{8,9},{9,8},{1... | collective-permute-start | bytes 208904 | tf_op jit(solution)/shard_map/sum_z_inner/ppermute | solution.py:275
  29.4 3.7 %collective-permute-start.5 = (f32[136,128]{1,0:T(8,128)S(1)}, f32[136,128]{1,0:T(8,128)S(1)}, u32[]{:S(2)}, u32[]{:S(2)}) collective-permute-start(f32[136,128]{1,0:T(8,128)S(1)} %add.80), channel_id=1, source_target_pairs={{0,1},{1,0},{2,3},{3,2},{4,12},{5,13},{6,14},{7,15},{8,9},{9,8},{1... | collective-permute-start | bytes 208904 | tf_op jit(solution)/shard_map/sum_z_inner/ppermute | solution.py:275
  33.1 4.8 %collective-permute-start.10 = (f32[136,128]{1,0:T(8,128)S(1)}, f32[136,128]{1,0:T(8,128)S(1)}, u32[]{:S(2)}, u32[]{:S(2)}) collective-permute-start(f32[136,128]{1,0:T(8,128)S(1)} %add_add_fusion.5), channel_id=1, source_target_pairs={{0,1},{1,0},{2,3},{3,2},{4,132},{5,133},{6,134},{7,135},{8,9},{9,8... | collective-permute-start | bytes 208904 | tf_op jit(solution)/shard_map/sum_y/ppermute | solution.py:275
  36.1 4.4 %collective-permute-start.9 = (f32[136,128]{1,0:T(8,128)S(1)}, f32[136,128]{1,0:T(8,128)S(1)}, u32[]{:S(2)}, u32[]{:S(2)}) collective-permute-start(f32[136,128]{1,0:T(8,128)S(1)} %add_add_fusion.5), channel_id=1, source_target_pairs={{0,1},{1,0},{2,3},{3,2},{4,196},{5,197},{6,198},{7,199},{8,9},{9,8... | collective-permute-start | bytes 208904 | tf_op jit(solution)/shard_map/sum_y/ppermute | solution.py:275
  36.9 3.6 %collective-permute-start.8 = (f32[136,128]{1,0:T(8,128)S(1)}, f32[136,128]{1,0:T(8,128)S(1)}, u32[]{:S(2)}, u32[]{:S(2)}) collective-permute-start(f32[136,128]{1,0:T(8,128)S(1)} %add_add_fusion.5), channel_id=1, source_target_pairs={{0,1},{1,0},{2,3},{3,2},{4,68},{5,69},{6,70},{7,71},{8,9},{9,8},{1... | collective-permute-start | bytes 208904 | tf_op jit(solution)/shard_map/sum_y/ppermute | solution.py:275
  42.9 4.3 %collective-permute-start.14 = (f32[72,128]{1,0:T(8,128)S(1)}, f32[72,128]{1,0:T(8,128)S(1)}, u32[]{:S(2)}, u32[]{:S(2)}) collective-permute-start(f32[72,128]{1,0:T(8,128)S(1)} %get-tuple-element.56.refs_0_), channel_id=1, source_target_pairs={{0,2},{1,3},{2,0},{3,1},{4,6},{5,7},{6,4},{7,5},{8,10},{9,11},{10,... | collective-permute-start | bytes 110600 | tf_op jit(solution)/shard_map/sum_req/ppermute | solution.py:284
  44.9 4.0 %collective-permute-start.13 = (f32[72,128]{1,0:T(8,128)S(1)}, f32[72,128]{1,0:T(8,128)S(1)}, u32[]{:S(2)}, u32[]{:S(2)}) collective-permute-start(f32[72,128]{1,0:T(8,128)S(1)} %get-tuple-element.56.refs_0_), channel_id=1, source_target_pairs={{0,3},{1,2},{2,1},{3,0},{4,7},{5,6},{6,5},{7,4},{8,11},{9,10},{10,... | collective-permute-start | bytes 110600 | tf_op jit(solution)/shard_map/sum_req/ppermute | solution.py:284
  53.3 5.5 %collective-permute-start.16 = (f32[136,128]{1,0:T(8,128)S(1)}, f32[136,128]{1,0:T(8,128)S(1)}, u32[]{:S(2)}, u32[]{:S(2)}) collective-permute-start(f32[136,128]{1,0:T(8,128)S(1)} %add.87), channel_id=1, source_target_pairs={{0,1},{1,0},{2,3},{3,2},{4,52},{5,53},{6,54},{7,55},{8,9},{9,8},{1... | collective-permute-start | bytes 208904 | tf_op jit(solution)/shard_map/sum_z_outer/ppermute | solution.py:275
  58.7 4.1 %collective-permute-start.19 = (f32[136,128]{1,0:T(8,128)S(1)}, f32[136,128]{1,0:T(8,128)S(1)}, u32[]{:S(2)}, u32[]{:S(2)}) collective-permute-start(f32[136,128]{1,0:T(8,128)S(1)} %add.88), channel_id=1, source_target_pairs={{0,1},{1,0},{2,3},{3,2},{4,20},{5,21},{6,22},{7,23},{8,9},{9,8},{1... | collective-permute-start | bytes 208904 | tf_op jit(solution)/shard_map/sum_z_inner/ppermute | solution.py:275
  60.8 5.1 %collective-permute-start.18 = (f32[136,128]{1,0:T(8,128)S(1)}, f32[136,128]{1,0:T(8,128)S(1)}, u32[]{:S(2)}, u32[]{:S(2)}) collective-permute-start(f32[136,128]{1,0:T(8,128)S(1)} %add.88), channel_id=1, source_target_pairs={{0,1},{1,0},{2,3},{3,2},{4,28},{5,29},{6,30},{7,31},{8,9},{9,8},{1... | collective-permute-start | bytes 208904 | tf_op jit(solution)/shard_map/sum_z_inner/ppermute | solution.py:275
  62.5 3.9 %collective-permute-start.17 = (f32[136,128]{1,0:T(8,128)S(1)}, f32[136,128]{1,0:T(8,128)S(1)}, u32[]{:S(2)}, u32[]{:S(2)}) collective-permute-start(f32[136,128]{1,0:T(8,128)S(1)} %add.88), channel_id=1, source_target_pairs={{0,1},{1,0},{2,3},{3,2},{4,12},{5,13},{6,14},{7,15},{8,9},{9,8},{1... | collective-permute-start | bytes 208904 | tf_op jit(solution)/shard_map/sum_z_inner/ppermute | solution.py:275
  66.4 4.8 %collective-permute-start.22 = (f32[136,128]{1,0:T(8,128)S(1)}, f32[136,128]{1,0:T(8,128)S(1)}, u32[]{:S(2)}, u32[]{:S(2)}) collective-permute-start(f32[136,128]{1,0:T(8,128)S(1)} %add_add_fusion.3), channel_id=1, source_target_pairs={{0,1},{1,0},{2,3},{3,2},{4,132},{5,133},{6,134},{7,135},{8,9},{9,8... | collective-permute-start | bytes 208904 | tf_op jit(solution)/shard_map/sum_y/ppermute | solution.py:275
  67.7 4.4 %collective-permute-start.21 = (f32[136,128]{1,0:T(8,128)S(1)}, f32[136,128]{1,0:T(8,128)S(1)}, u32[]{:S(2)}, u32[]{:S(2)}) collective-permute-start(f32[136,128]{1,0:T(8,128)S(1)} %add_add_fusion.3), channel_id=1, source_target_pairs={{0,1},{1,0},{2,3},{3,2},{4,196},{5,197},{6,198},{7,199},{8,9},{9,8... | collective-permute-start | bytes 208904 | tf_op jit(solution)/shard_map/sum_y/ppermute | solution.py:275
  68.5 3.6 %collective-permute-start.20 = (f32[136,128]{1,0:T(8,128)S(1)}, f32[136,128]{1,0:T(8,128)S(1)}, u32[]{:S(2)}, u32[]{:S(2)}) collective-permute-start(f32[136,128]{1,0:T(8,128)S(1)} %add_add_fusion.3), channel_id=1, source_target_pairs={{0,1},{1,0},{2,3},{3,2},{4,68},{5,69},{6,70},{7,71},{8,9},{9,8},{1... | collective-permute-start | bytes 208904 | tf_op jit(solution)/shard_map/sum_y/ppermute | solution.py:275
  74.5 4.3 %collective-permute-start.26 = (f32[72,128]{1,0:T(8,128)S(1)}, f32[72,128]{1,0:T(8,128)S(1)}, u32[]{:S(2)}, u32[]{:S(2)}) collective-permute-start(f32[72,128]{1,0:T(8,128)S(1)} %get-tuple-element.63.refs_0_), channel_id=1, source_target_pairs={{0,2},{1,3},{2,0},{3,1},{4,6},{5,7},{6,4},{7,5},{8,10},{9,11},{10,... | collective-permute-start | bytes 110600 | tf_op jit(solution)/shard_map/sum_req/ppermute | solution.py:284
  75.7 4.1 %collective-permute-start.25 = (f32[72,128]{1,0:T(8,128)S(1)}, f32[72,128]{1,0:T(8,128)S(1)}, u32[]{:S(2)}, u32[]{:S(2)}) collective-permute-start(f32[72,128]{1,0:T(8,128)S(1)} %get-tuple-element.63.refs_0_), channel_id=1, source_target_pairs={{0,3},{1,2},{2,1},{3,0},{4,7},{5,6},{6,5},{7,4},{8,11},{9,10},{10,... | collective-permute-start | bytes 110600 | tf_op jit(solution)/shard_map/sum_req/ppermute | solution.py:284
  76.6 3.2 %collective-permute-start.24 = (f32[72,128]{1,0:T(8,128)S(1)}, f32[72,128]{1,0:T(8,128)S(1)}, u32[]{:S(2)}, u32[]{:S(2)}) collective-permute-start(f32[72,128]{1,0:T(8,128)S(1)} %get-tuple-element.63.refs_0_), channel_id=1, source_target_pairs={{0,1},{1,0},{2,3},{3,2},{4,5},{5,4},{6,7},{7,6},{8,9},{9,8},{10,11... | collective-permute-start | bytes 110600 | tf_op jit(solution)/shard_map/sum_req/ppermute | solution.py:284
  83.9 5.4 %collective-permute-start.28 = (f32[136,128]{1,0:T(8,128)S(1)}, f32[136,128]{1,0:T(8,128)S(1)}, u32[]{:S(2)}, u32[]{:S(2)}) collective-permute-start(f32[136,128]{1,0:T(8,128)S(1)} %add.95), channel_id=1, source_target_pairs={{0,1},{1,0},{2,3},{3,2},{4,52},{5,53},{6,54},{7,55},{8,9},{9,8},{1... | collective-permute-start | bytes 208904 | tf_op jit(solution)/shard_map/sum_z_outer/ppermute | solution.py:275
  89.3 4.9 %collective-permute-start.31 = (f32[136,128]{1,0:T(8,128)S(1)}, f32[136,128]{1,0:T(8,128)S(1)}, u32[]{:S(2)}, u32[]{:S(2)}) collective-permute-start(f32[136,128]{1,0:T(8,128)S(1)} %add.96), channel_id=1, source_target_pairs={{0,1},{1,0},{2,3},{3,2},{4,20},{5,21},{6,22},{7,23},{8,9},{9,8},{1... | collective-permute-start | bytes 208904 | tf_op jit(solution)/shard_map/sum_z_inner/ppermute | solution.py:275
  90.2 5.1 %collective-permute-start.30 = (f32[136,128]{1,0:T(8,128)S(1)}, f32[136,128]{1,0:T(8,128)S(1)}, u32[]{:S(2)}, u32[]{:S(2)}) collective-permute-start(f32[136,128]{1,0:T(8,128)S(1)} %add.96), channel_id=1, source_target_pairs={{0,1},{1,0},{2,3},{3,2},{4,28},{5,29},{6,30},{7,31},{8,9},{9,8},{1... | collective-permute-start | bytes 208904 | tf_op jit(solution)/shard_map/sum_z_inner/ppermute | solution.py:275
  91.8 3.9 %collective-permute-start.29 = (f32[136,128]{1,0:T(8,128)S(1)}, f32[136,128]{1,0:T(8,128)S(1)}, u32[]{:S(2)}, u32[]{:S(2)}) collective-permute-start(f32[136,128]{1,0:T(8,128)S(1)} %add.96), channel_id=1, source_target_pairs={{0,1},{1,0},{2,3},{3,2},{4,12},{5,13},{6,14},{7,15},{8,9},{9,8},{1... | collective-permute-start | bytes 208904 | tf_op jit(solution)/shard_map/sum_z_inner/ppermute | solution.py:275
  95.7 4.8 %collective-permute-start.34 = (f32[136,128]{1,0:T(8,128)S(1)}, f32[136,128]{1,0:T(8,128)S(1)}, u32[]{:S(2)}, u32[]{:S(2)}) collective-permute-start(f32[136,128]{1,0:T(8,128)S(1)} %add_add_fusion.1), channel_id=1, source_target_pairs={{0,1},{1,0},{2,3},{3,2},{4,132},{5,133},{6,134},{7,135},{8,9},{9,8... | collective-permute-start | bytes 208904 | tf_op jit(solution)/shard_map/sum_y/ppermute | solution.py:275
  97.0 4.4 %collective-permute-start.33 = (f32[136,128]{1,0:T(8,128)S(1)}, f32[136,128]{1,0:T(8,128)S(1)}, u32[]{:S(2)}, u32[]{:S(2)}) collective-permute-start(f32[136,128]{1,0:T(8,128)S(1)} %add_add_fusion.1), channel_id=1, source_target_pairs={{0,1},{1,0},{2,3},{3,2},{4,196},{5,197},{6,198},{7,199},{8,9},{9,8... | collective-permute-start | bytes 208904 | tf_op jit(solution)/shard_map/sum_y/ppermute | solution.py:275
  98.1 3.3 %collective-permute-start.32 = (f32[136,128]{1,0:T(8,128)S(1)}, f32[136,128]{1,0:T(8,128)S(1)}, u32[]{:S(2)}, u32[]{:S(2)}) collective-permute-start(f32[136,128]{1,0:T(8,128)S(1)} %add_add_fusion.1), channel_id=1, source_target_pairs={{0,1},{1,0},{2,3},{3,2},{4,68},{5,69},{6,70},{7,71},{8,9},{9,8},{1... | collective-permute-start | bytes 208904 | tf_op jit(solution)/shard_map/sum_y/ppermute | solution.py:275
  101.5 7.5 %collective-permute-start.35 = (f32[136,128]{1,0:T(8,128)S(1)}, f32[136,128]{1,0:T(8,128)S(1)}, u32[]{:S(2)}, u32[]{:S(2)}) collective-permute-start(f32[136,128]{1,0:T(8,128)S(1)} %constant_dynamic-update-slice_fusion.state_own), channel_id=1, source_target_pairs={{0,4},{1,5},{2,6},{3,7},{4,0},{5,1},{6,2},{7,3},{8,12},{9,13},{10,... | collective-permute-start | bytes 208904 | tf_op jit(solution)/shard_map/back_core/ppermute | solution.py:275
  102.0 4.0 %collective-permute-start.38 = (f32[8,128]{1,0:T(8,128)S(1)}, f32[8,128]{1,0:T(8,128)S(1)}, u32[]{:S(2)}, u32[]{:S(2)}) collective-permute-start(f32[8,128]{1,0:T(8,128)S(1)} %get-tuple-element.74.last_0), channel_id=1, source_target_pairs={{0,64},{1,65},{2,66},{3,67},{4,6},{5,7},{6,4},{7,5},{8,72},{9,73},... | collective-permute-start | bytes 12296 | tf_op jit(solution)/shard_map/sum_req_last/ppermute | solution.py:275
  104.0 3.7 %collective-permute-start.37 = (f32[8,128]{1,0:T(8,128)S(1)}, f32[8,128]{1,0:T(8,128)S(1)}, u32[]{:S(2)}, u32[]{:S(2)}) collective-permute-start(f32[8,128]{1,0:T(8,128)S(1)} %get-tuple-element.74.last_0), channel_id=1, source_target_pairs={{0,64},{1,65},{2,66},{3,67},{4,7},{5,6},{6,5},{7,4},{8,72},{9,73},... | collective-permute-start | bytes 12296 | tf_op jit(solution)/shard_map/sum_req_last/ppermute | solution.py:275
  (14 other events, 125.4 us)

commit v4 on v3

--- a/solution.py
+++ b/solution.py
@@ -12,6 +12,7 @@
 STAT_ROWS = 8
 GROUP = 16
 KEPT = 6
+PIECES = 4
 
 step_primal = 0.6
 step_dual = 0.6
@@ -109,13 +110,15 @@
         small.append(pltpu.make_async_copy(source, target, sems.at[n]))
         small[-1].start()
     chunks = []
-    for n in range(groups):
-        chunks.append(pltpu.make_async_copy(tiles_in.at[pl.ds(n * GROUP, GROUP)], tiles[n], tile_sems.at[n]))
+    size = GROUP // PIECES
+    for n in range(groups * PIECES):
+        target = tiles[n // PIECES].at[pl.ds(n % PIECES * size, size)]
+        chunks.append(pltpu.make_async_copy(tiles_in.at[pl.ds(n * size, size)], target, tile_sems.at[n]))
         chunks[-1].start()
     for copy in small:
         copy.wait()
     req_blocks = dual.shape[0]
-    test_blocks = pull_out.shape[0] - STAT_ROWS
+    test_blocks = pull_out.shape[0]
     alive = lax.broadcasted_iota(jnp.int32, (1, slots), 1) < live[...]
     at_row = lax.broadcasted_iota(jnp.int32, (req_blocks, slots), 0) == rows[...]
     at_col = lax.broadcasted_iota(jnp.int32, (test_blocks, slots), 0) == cols[...]
@@ -126,10 +129,10 @@
     picked = gather_rows(pick, dual[...])
     contrib = []
     for group in range(groups):
-        chunks[group].wait()
+        for copy in chunks[group * PIECES : (group + 1) * PIECES]:
+            copy.wait()
         contrib.append(pull_group(picked, tiles, group))
-    pull_out[:test_blocks, :] = scatter_sum(place_cols[...], jnp.concatenate(contrib, axis=0))
-    pull_out[test_blocks:, :] = jnp.zeros((STAT_ROWS, LANES), F32)
+    pull_out[...] = scatter_sum(place_cols[...], jnp.concatenate(contrib, axis=0))
 
 
 def update_dual(iteration, inverse_tests, summed, params, dual, sum_dual, scal, demand):
@@ -322,12 +325,12 @@
             pull, pick_rows, place_cols, *tiles = call(
                 first_pull_kernel,
                 (
-                    pull_shape, struct(slots, req_blocks, dtype=BF16), struct(test_blocks, slots),
+                    big_t, struct(slots, req_blocks, dtype=BF16), struct(test_blocks, slots),
                     *[group_shape] * KEPT,
                 ),
                 [HBM] * len(given),
                 [pltpu.VMEM((rest, *group_shape.shape), BF16), *[pltpu.VMEM(x.shape, x.dtype) for x in given[1:]]]
-                + [pltpu.SemaphoreType.DMA((n,)) for n in (len(given) - 1, slots // GROUP)],
+                + [pltpu.SemaphoreType.DMA((n,)) for n in (len(given) - 1, slots // GROUP * PIECES)],
             )(*[pltpu.with_memory_space_constraint(x, pltpu.HBM) for x in given[:4]], given[4])
             place_rows, pick_cols, *more = call(
                 rest_kernel,

time: 110 us -> 110 us (level)
  no operation moved by 1% of the time
where the time goes in v4:
time: 110 us
  starting transfers between devices  50.5 us (46%)
  waiting for transfers between devices  42.9 us (39%)
  Pallas kernels  13.4 us (12%)
  between operations  2.84 us (3%)
    ppermute x31, starting transfers between devices, on_mesh(): return lax.ppermute(x, ('tst', 'req'), pairs)  40.4 us
    ppermute x31, waiting for transfers between devices, on_mesh(): return lax.ppermute(x, ('tst', 'req'), pairs)  36.4 us
    ppermute x9, starting transfers between devices, on_req(): lax.ppermute(x, 'req', [(i, i ^ bit) for i in range(n_req)])  10.1 us
    ppermute x9, waiting for transfers between devices, on_req(): lax.ppermute(x, 'req', [(i, i ^ bit) for i in range(n_req)])  6.52 us
    pallas_call x3, Pallas kernels, per_device(): call(functools.partial(primal_load_kernel, iteration), outs, [VMEM] * len...  4.7 us
    pallas_call x1, Pallas kernels, per_device(): call(first_pull_kernel, (big_t, struct(slots, req_blocks, dtype=BF16), st...  4.52 us
  transfers between devices with their start and end apart: 40, of which 31 were waited for; matrix products, arithmetic and copies ran while one was open for 0% of the time, Pallas kernels for 1%

profile of v4, /device:TPU:1, one launch (start us, length us, event | category | flops | bytes accessed | tf_op | source)
XLA Modules:
  0.0 110.1 jit_solution(15227249628755541581)
XLA Ops:
  1.3 4.5 %shard_map.147 = (f32[64,128]{1,0:T(8,128)S(1)}, bf16[128,128]{1,0:T(8,128)(2,1)S(1)}, f32[64,128]{1,0:T(8,128)S(1)}, bf16[16,128,128]{2,1,0:T(8,128)(2,1)S(1)},...) custom-call(bf16[128,128,128]{2,1,0:T(8,128)(2,1)} %tiles_in.3, ...), custom_call_target="tpu_custom_call" | custom-call | tf_op jit(solution)/shard_map/pallas_call | solution.py:325
  5.9 3.7 %collective-permute-start.2 = (f32[64,128]{1,0:T(8,128)S(1)}, f32[64,128]{1,0:T(8,128)S(1)}, u32[]{:S(2)}, u32[]{:S(2)}) collective-permute-start(f32[64,128]{1,0:T(8,128)S(1)} %get-tuple-element.42.refs_0_), channel_id=1, source_target_pairs={{0,2},{1,3},{2,0},{3,1},{4,6},{5,7},{6,4},{7,5},{8,10},{9,11},{10,... | collective-permute-start | bytes 98312 | tf_op jit(solution)/shard_map/sum_req/ppermute | solution.py:287
  13.9 1.6 %shard_map.149 = (f32[136,128]{1,0:T(8,128)S(1)}, f32[64,128]{1,0:T(8,128)S(1)}, f32[64,128]{1,0:T(8,128)S(1)}) custom-call(f32[64,128]{1,0:T(8,128)S(1)} %get-tuple-element.42.refs_0_, f32[64,128]{1,0:T(8,128)S(1)} %collective-permute-done.refs_1_, f32[64,128]{1,0:T(8,128)S(1)} %collective-permute-done.1.refs_2_, ...), custom_call_target="tpu_custom_call" | custom-call | tf_op jit(solution)/shard_map/pallas_call | solution.py:354
  15.5 1.9 %collective-permute-start.3 = (f32[136,128]{1,0:T(8,128)S(1)}, f32[136,128]{1,0:T(8,128)S(1)}, u32[]{:S(2)}, u32[]{:S(2)}) collective-permute-start(f32[136,128]{1,0:T(8,128)S(1)} %get-tuple-element.55), channel_id=1, source_target_pairs={{0,4},{1,5},{2,6},{3,7},{4,0},{5,1},{6,2},{7,3},{8,12},{9,13},{10,... | collective-permute-start | bytes 208904 | tf_op jit(solution)/shard_map/sum_core/ppermute | solution.py:278
  18.3 6.1 %collective-permute-start.4 = (f32[136,128]{1,0:T(8,128)S(1)}, f32[136,128]{1,0:T(8,128)S(1)}, u32[]{:S(2)}, u32[]{:S(2)}) collective-permute-start(f32[136,128]{1,0:T(8,128)S(1)} %add.79), channel_id=1, source_target_pairs={{0,1},{1,0},{2,3},{3,2},{4,52},{5,53},{6,54},{7,55},{8,9},{9,8},{1... | collective-permute-start | bytes 208904 | tf_op jit(solution)/shard_map/sum_z_outer/ppermute | solution.py:278
  24.4 1.8 %collective-permute-done.4 = f32[136,128]{1,0:T(8,128)S(1)} collective-permute-done((f32[136,128]{1,0:T(8,128)S(1)}, f32[136,128]{1,0:T(8,128)S(1)}, u32[]{:S(2)}, u32[]{:S(2)}) %collective-permute-start.4) | collective-permute-done | bytes 69664 | tf_op jit(solution)/shard_map/sum_z_outer/ppermute | solution.py:278
  27.4 2.4 %collective-permute-start.6 = (f32[136,128]{1,0:T(8,128)S(1)}, f32[136,128]{1,0:T(8,128)S(1)}, u32[]{:S(2)}, u32[]{:S(2)}) collective-permute-start(f32[136,128]{1,0:T(8,128)S(1)} %add.80), channel_id=1, source_target_pairs={{0,1},{1,0},{2,3},{3,2},{4,28},{5,29},{6,30},{7,31},{8,9},{9,8},{1... | collective-permute-start | bytes 208904 | tf_op jit(solution)/shard_map/sum_z_inner/ppermute | solution.py:278
  30.4 2.1 %collective-permute-done.6 = f32[136,128]{1,0:T(8,128)S(1)} collective-permute-done((f32[136,128]{1,0:T(8,128)S(1)}, f32[136,128]{1,0:T(8,128)S(1)}, u32[]{:S(2)}, u32[]{:S(2)}) %collective-permute-start.6) | collective-permute-done | bytes 69664 | tf_op jit(solution)/shard_map/sum_z_inner/ppermute | solution.py:278
  33.5 3.0 %collective-permute-start.10 = (f32[136,128]{1,0:T(8,128)S(1)}, f32[136,128]{1,0:T(8,128)S(1)}, u32[]{:S(2)}, u32[]{:S(2)}) collective-permute-start(f32[136,128]{1,0:T(8,128)S(1)} %add_add_fusion.5), channel_id=1, source_target_pairs={{0,1},{1,0},{2,3},{3,2},{4,132},{5,133},{6,134},{7,135},{8,9},{9,8... | collective-permute-start | bytes 208904 | tf_op jit(solution)/shard_map/sum_y/ppermute | solution.py:278
  38.2 2.6 %collective-permute-done.9 = f32[136,128]{1,0:T(8,128)S(1)} collective-permute-done((f32[136,128]{1,0:T(8,128)S(1)}, f32[136,128]{1,0:T(8,128)S(1)}, u32[]{:S(2)}, u32[]{:S(2)}) %collective-permute-start.9) | collective-permute-done | bytes 69664 | tf_op jit(solution)/shard_map/sum_y/ppermute | solution.py:278
  43.3 2.1 %collective-permute-start.14 = (f32[72,128]{1,0:T(8,128)S(1)}, f32[72,128]{1,0:T(8,128)S(1)}, u32[]{:S(2)}, u32[]{:S(2)}) collective-permute-start(f32[72,128]{1,0:T(8,128)S(1)} %get-tuple-element.56.refs_0_), channel_id=1, source_target_pairs={{0,2},{1,3},{2,0},{3,1},{4,6},{5,7},{6,4},{7,5},{8,10},{9,11},{10,... | collective-permute-start | bytes 110600 | tf_op jit(solution)/shard_map/sum_req/ppermute | solution.py:287
  46.2 1.4 %collective-permute-done.14.refs_3_ = f32[72,128]{1,0:T(8,128)S(1)} collective-permute-done((f32[72,128]{1,0:T(8,128)S(1)}, f32[72,128]{1,0:T(8,128)S(1)}, u32[]{:S(2)}, u32[]{:S(2)}) %collective-permute-start.14) | collective-permute-done | bytes 36896 | tf_op jit(solution)/shard_map/sum_req/ppermute | solution.py:287
  47.6 1.7 %collective-permute-done.13.refs_2_ = f32[72,128]{1,0:T(8,128)S(1)} collective-permute-done((f32[72,128]{1,0:T(8,128)S(1)}, f32[72,128]{1,0:T(8,128)S(1)}, u32[]{:S(2)}, u32[]{:S(2)}) %collective-permute-start.13) | collective-permute-done | bytes 36896 | tf_op jit(solution)/shard_map/sum_req/ppermute | solution.py:287
  49.4 1.6 %shard_map.151 = (f32[136,128]{1,0:T(8,128)S(1)}, f32[64,128]{1,0:T(8,128)S(1)}, f32[64,128]{1,0:T(8,128)S(1)}, f32[8,128]{1,0:T(8,128)S(1)}) custom-call(f32[72,128]{1,0:T(8,128)S(1)} %get-tuple-element.56.refs_0_, f32[72,128]{1,0:T(8,128)S(1)} %collective-permute-done.12.refs_1_, f32[72,128]{1,0:T(8,128)S(1)} %collective-permute-done.13.refs_2_, ...), custom_call_target="tpu_custom_call" | custom-call | tf_op jit(solution)/shard_map/pallas_call | solution.py:354
  50.9 1.9 %collective-permute-start.15 = (f32[136,128]{1,0:T(8,128)S(1)}, f32[136,128]{1,0:T(8,128)S(1)}, u32[]{:S(2)}, u32[]{:S(2)}) collective-permute-start(f32[136,128]{1,0:T(8,128)S(1)} %get-tuple-element.60), channel_id=1, source_target_pairs={{0,4},{1,5},{2,6},{3,7},{4,0},{5,1},{6,2},{7,3},{8,12},{9,13},{10,... | collective-permute-start | bytes 208904 | tf_op jit(solution)/shard_map/sum_core/ppermute | solution.py:278
  53.7 3.2 %collective-permute-start.16 = (f32[136,128]{1,0:T(8,128)S(1)}, f32[136,128]{1,0:T(8,128)S(1)}, u32[]{:S(2)}, u32[]{:S(2)}) collective-permute-start(f32[136,128]{1,0:T(8,128)S(1)} %add.87), channel_id=1, source_target_pairs={{0,1},{1,0},{2,3},{3,2},{4,52},{5,53},{6,54},{7,55},{8,9},{9,8},{1... | collective-permute-start | bytes 208904 | tf_op jit(solution)/shard_map/sum_z_outer/ppermute | solution.py:278
  56.9 2.3 %collective-permute-done.16 = f32[136,128]{1,0:T(8,128)S(1)} collective-permute-done((f32[136,128]{1,0:T(8,128)S(1)}, f32[136,128]{1,0:T(8,128)S(1)}, u32[]{:S(2)}, u32[]{:S(2)}) %collective-permute-start.16) | collective-permute-done | bytes 69664 | tf_op jit(solution)/shard_map/sum_z_outer/ppermute | solution.py:278
  59.2 2.0 %collective-permute-start.19 = (f32[136,128]{1,0:T(8,128)S(1)}, f32[136,128]{1,0:T(8,128)S(1)}, u32[]{:S(2)}, u32[]{:S(2)}) collective-permute-start(f32[136,128]{1,0:T(8,128)S(1)} %add.88), channel_id=1, source_target_pairs={{0,1},{1,0},{2,3},{3,2},{4,20},{5,21},{6,22},{7,23},{8,9},{9,8},{1... | collective-permute-start | bytes 208904 | tf_op jit(solution)/shard_map/sum_z_inner/ppermute | solution.py:278
  61.2 1.8 %collective-permute-start.18 = (f32[136,128]{1,0:T(8,128)S(1)}, f32[136,128]{1,0:T(8,128)S(1)}, u32[]{:S(2)}, u32[]{:S(2)}) collective-permute-start(f32[136,128]{1,0:T(8,128)S(1)} %add.88), channel_id=1, source_target_pairs={{0,1},{1,0},{2,3},{3,2},{4,28},{5,29},{6,30},{7,31},{8,9},{9,8},{1... | collective-permute-start | bytes 208904 | tf_op jit(solution)/shard_map/sum_z_inner/ppermute | solution.py:278
  63.3 2.9 %collective-permute-done.18 = f32[136,128]{1,0:T(8,128)S(1)} collective-permute-done((f32[136,128]{1,0:T(8,128)S(1)}, f32[136,128]{1,0:T(8,128)S(1)}, u32[]{:S(2)}, u32[]{:S(2)}) %collective-permute-start.18) | collective-permute-done | bytes 69664 | tf_op jit(solution)/shard_map/sum_z_inner/ppermute | solution.py:278
  69.6 2.0 %collective-permute-done.22 = f32[136,128]{1,0:T(8,128)S(1)} collective-permute-done((f32[136,128]{1,0:T(8,128)S(1)}, f32[136,128]{1,0:T(8,128)S(1)}, u32[]{:S(2)}, u32[]{:S(2)}) %collective-permute-start.22) | collective-permute-done | bytes 69664 | tf_op jit(solution)/shard_map/sum_y/ppermute | solution.py:278
  77.6 1.7 %collective-permute-done.26.refs_3_ = f32[72,128]{1,0:T(8,128)S(1)} collective-permute-done((f32[72,128]{1,0:T(8,128)S(1)}, f32[72,128]{1,0:T(8,128)S(1)}, u32[]{:S(2)}, u32[]{:S(2)}) %collective-permute-start.26) | collective-permute-done | bytes 36896 | tf_op jit(solution)/shard_map/sum_req/ppermute | solution.py:287
  80.3 1.6 %shard_map.153 = (f32[136,128]{1,0:T(8,128)S(1)}, f32[64,128]{1,0:T(8,128)S(1)}, f32[8,128]{1,0:T(8,128)S(1)}) custom-call(f32[72,128]{1,0:T(8,128)S(1)} %get-tuple-element.63.refs_0_, f32[72,128]{1,0:T(8,128)S(1)} %collective-permute-done.24.refs_1_, f32[72,128]{1,0:T(8,128)S(1)} %collective-permute-done.25.refs_2_, ...), custom_call_target="tpu_custom_call" | custom-call | tf_op jit(solution)/shard_map/pallas_call | solution.py:354
  81.9 1.5 %collective-permute-start.27 = (f32[136,128]{1,0:T(8,128)S(1)}, f32[136,128]{1,0:T(8,128)S(1)}, u32[]{:S(2)}, u32[]{:S(2)}) collective-permute-start(f32[136,128]{1,0:T(8,128)S(1)} %get-tuple-element.67), channel_id=1, source_target_pairs={{0,4},{1,5},{2,6},{3,7},{4,0},{5,1},{6,2},{7,3},{8,12},{9,13},{10,... | collective-permute-start | bytes 208904 | tf_op jit(solution)/shard_map/sum_core/ppermute | solution.py:278
  84.3 2.6 %collective-permute-start.28 = (f32[136,128]{1,0:T(8,128)S(1)}, f32[136,128]{1,0:T(8,128)S(1)}, u32[]{:S(2)}, u32[]{:S(2)}) collective-permute-start(f32[136,128]{1,0:T(8,128)S(1)} %add.95), channel_id=1, source_target_pairs={{0,1},{1,0},{2,3},{3,2},{4,52},{5,53},{6,54},{7,55},{8,9},{9,8},{1... | collective-permute-start | bytes 208904 | tf_op jit(solution)/shard_map/sum_z_outer/ppermute | solution.py:278
  86.9 2.8 %collective-permute-done.28 = f32[136,128]{1,0:T(8,128)S(1)} collective-permute-done((f32[136,128]{1,0:T(8,128)S(1)}, f32[136,128]{1,0:T(8,128)S(1)}, u32[]{:S(2)}, u32[]{:S(2)}) %collective-permute-start.28) | collective-permute-done | bytes 69664 | tf_op jit(solution)/shard_map/sum_z_outer/ppermute | solution.py:278
  90.6 1.6 %collective-permute-start.30 = (f32[136,128]{1,0:T(8,128)S(1)}, f32[136,128]{1,0:T(8,128)S(1)}, u32[]{:S(2)}, u32[]{:S(2)}) collective-permute-start(f32[136,128]{1,0:T(8,128)S(1)} %add.96), channel_id=1, source_target_pairs={{0,1},{1,0},{2,3},{3,2},{4,28},{5,29},{6,30},{7,31},{8,9},{9,8},{1... | collective-permute-start | bytes 208904 | tf_op jit(solution)/shard_map/sum_z_inner/ppermute | solution.py:278
  92.5 2.2 %collective-permute-done.31 = f32[136,128]{1,0:T(8,128)S(1)} collective-permute-done((f32[136,128]{1,0:T(8,128)S(1)}, f32[136,128]{1,0:T(8,128)S(1)}, u32[]{:S(2)}, u32[]{:S(2)}) %collective-permute-start.31) | collective-permute-done | bytes 69664 | tf_op jit(solution)/shard_map/sum_z_inner/ppermute | solution.py:278
  96.2 1.3 %collective-permute-start.34 = (f32[136,128]{1,0:T(8,128)S(1)}, f32[136,128]{1,0:T(8,128)S(1)}, u32[]{:S(2)}, u32[]{:S(2)}) collective-permute-start(f32[136,128]{1,0:T(8,128)S(1)} %add_add_fusion.1), channel_id=1, source_target_pairs={{0,1},{1,0},{2,3},{3,2},{4,132},{5,133},{6,134},{7,135},{8,9},{9,8... | collective-permute-start | bytes 208904 | tf_op jit(solution)/shard_map/sum_y/ppermute | solution.py:278
  98.9 2.0 %collective-permute-done.34 = f32[136,128]{1,0:T(8,128)S(1)} collective-permute-done((f32[136,128]{1,0:T(8,128)S(1)}, f32[136,128]{1,0:T(8,128)S(1)}, u32[]{:S(2)}, u32[]{:S(2)}) %collective-permute-start.34) | collective-permute-done | bytes 69664 | tf_op jit(solution)/shard_map/sum_y/ppermute | solution.py:278
  102.4 2.0 %collective-permute-start.38 = (f32[8,128]{1,0:T(8,128)S(1)}, f32[8,128]{1,0:T(8,128)S(1)}, u32[]{:S(2)}, u32[]{:S(2)}) collective-permute-start(f32[8,128]{1,0:T(8,128)S(1)} %get-tuple-element.74.last_0), channel_id=1, source_target_pairs={{0,64},{1,65},{2,66},{3,67},{4,6},{5,7},{6,4},{7,5},{8,72},{9,73},... | collective-permute-start | bytes 12296 | tf_op jit(solution)/shard_map/sum_req_last/ppermute | solution.py:278
  106.4 1.7 %collective-permute-done.37.last_2 = f32[8,128]{1,0:T(8,128)S(1)} collective-permute-done((f32[8,128]{1,0:T(8,128)S(1)}, f32[8,128]{1,0:T(8,128)S(1)}, u32[]{:S(2)}, u32[]{:S(2)}) %collective-permute-start.37) | collective-permute-done | bytes 4128 | tf_op jit(solution)/shard_map/sum_req_last/ppermute | solution.py:278
  (92 shorter events, 34.0 us)
Async XLA Ops:
  5.9 7.2 %collective-permute-start.2 = (f32[64,128]{1,0:T(8,128)S(1)}, f32[64,128]{1,0:T(8,128)S(1)}, u32[]{:S(2)}, u32[]{:S(2)}) collective-permute-start(f32[64,128]{1,0:T(8,128)S(1)} %get-tuple-element.42.refs_0_), channel_id=1, source_target_pairs={{0,2},{1,3},{2,0},{3,1},{4,6},{5,7},{6,4},{7,5},{8,10},{9,11},{10,... | collective-permute-start | bytes 98312 | tf_op jit(solution)/shard_map/sum_req/ppermute | solution.py:287
  9.5 4.3 %collective-permute-start.1 = (f32[64,128]{1,0:T(8,128)S(1)}, f32[64,128]{1,0:T(8,128)S(1)}, u32[]{:S(2)}, u32[]{:S(2)}) collective-permute-start(f32[64,128]{1,0:T(8,128)S(1)} %get-tuple-element.42.refs_0_), channel_id=1, source_target_pairs={{0,3},{1,2},{2,1},{3,0},{4,7},{5,6},{6,5},{7,4},{8,11},{9,10},{10,... | collective-permute-start | bytes 98312 | tf_op jit(solution)/shard_map/sum_req/ppermute | solution.py:287
  10.4 3.4 %collective-permute-start = (f32[64,128]{1,0:T(8,128)S(1)}, f32[64,128]{1,0:T(8,128)S(1)}, u32[]{:S(2)}, u32[]{:S(2)}) collective-permute-start(f32[64,128]{1,0:T(8,128)S(1)} %get-tuple-element.42.refs_0_), channel_id=1, source_target_pairs={{0,1},{1,0},{2,3},{3,2},{4,5},{5,4},{6,7},{7,6},{8,9},{9,8},{10,11... | collective-permute-start | bytes 98312 | tf_op jit(solution)/shard_map/sum_req/ppermute | solution.py:287
  18.3 7.9 %collective-permute-start.4 = (f32[136,128]{1,0:T(8,128)S(1)}, f32[136,128]{1,0:T(8,128)S(1)}, u32[]{:S(2)}, u32[]{:S(2)}) collective-permute-start(f32[136,128]{1,0:T(8,128)S(1)} %add.79), channel_id=1, source_target_pairs={{0,1},{1,0},{2,3},{3,2},{4,52},{5,53},{6,54},{7,55},{8,9},{9,8},{1... | collective-permute-start | bytes 208904 | tf_op jit(solution)/shard_map/sum_z_outer/ppermute | solution.py:278
  26.2 4.1 %collective-permute-start.7 = (f32[136,128]{1,0:T(8,128)S(1)}, f32[136,128]{1,0:T(8,128)S(1)}, u32[]{:S(2)}, u32[]{:S(2)}) collective-permute-start(f32[136,128]{1,0:T(8,128)S(1)} %add.80), channel_id=1, source_target_pairs={{0,1},{1,0},{2,3},{3,2},{4,20},{5,21},{6,22},{7,23},{8,9},{9,8},{1... | collective-permute-start | bytes 208904 | tf_op jit(solution)/shard_map/sum_z_inner/ppermute | solution.py:278
  27.4 5.0 %collective-permute-start.6 = (f32[136,128]{1,0:T(8,128)S(1)}, f32[136,128]{1,0:T(8,128)S(1)}, u32[]{:S(2)}, u32[]{:S(2)}) collective-permute-start(f32[136,128]{1,0:T(8,128)S(1)} %add.80), channel_id=1, source_target_pairs={{0,1},{1,0},{2,3},{3,2},{4,28},{5,29},{6,30},{7,31},{8,9},{9,8},{1... | collective-permute-start | bytes 208904 | tf_op jit(solution)/shard_map/sum_z_inner/ppermute | solution.py:278
  29.8 3.7 %collective-permute-start.5 = (f32[136,128]{1,0:T(8,128)S(1)}, f32[136,128]{1,0:T(8,128)S(1)}, u32[]{:S(2)}, u32[]{:S(2)}) collective-permute-start(f32[136,128]{1,0:T(8,128)S(1)} %add.80), channel_id=1, source_target_pairs={{0,1},{1,0},{2,3},{3,2},{4,12},{5,13},{6,14},{7,15},{8,9},{9,8},{1... | collective-permute-start | bytes 208904 | tf_op jit(solution)/shard_map/sum_z_inner/ppermute | solution.py:278
  33.5 4.8 %collective-permute-start.10 = (f32[136,128]{1,0:T(8,128)S(1)}, f32[136,128]{1,0:T(8,128)S(1)}, u32[]{:S(2)}, u32[]{:S(2)}) collective-permute-start(f32[136,128]{1,0:T(8,128)S(1)} %add_add_fusion.5), channel_id=1, source_target_pairs={{0,1},{1,0},{2,3},{3,2},{4,132},{5,133},{6,134},{7,135},{8,9},{9,8... | collective-permute-start | bytes 208904 | tf_op jit(solution)/shard_map/sum_y/ppermute | solution.py:278
  36.5 4.4 %collective-permute-start.9 = (f32[136,128]{1,0:T(8,128)S(1)}, f32[136,128]{1,0:T(8,128)S(1)}, u32[]{:S(2)}, u32[]{:S(2)}) collective-permute-start(f32[136,128]{1,0:T(8,128)S(1)} %add_add_fusion.5), channel_id=1, source_target_pairs={{0,1},{1,0},{2,3},{3,2},{4,196},{5,197},{6,198},{7,199},{8,9},{9,8... | collective-permute-start | bytes 208904 | tf_op jit(solution)/shard_map/sum_y/ppermute | solution.py:278
  37.3 3.6 %collective-permute-start.8 = (f32[136,128]{1,0:T(8,128)S(1)}, f32[136,128]{1,0:T(8,128)S(1)}, u32[]{:S(2)}, u32[]{:S(2)}) collective-permute-start(f32[136,128]{1,0:T(8,128)S(1)} %add_add_fusion.5), channel_id=1, source_target_pairs={{0,1},{1,0},{2,3},{3,2},{4,68},{5,69},{6,70},{7,71},{8,9},{9,8},{1... | collective-permute-start | bytes 208904 | tf_op jit(solution)/shard_map/sum_y/ppermute | solution.py:278
  43.3 4.3 %collective-permute-start.14 = (f32[72,128]{1,0:T(8,128)S(1)}, f32[72,128]{1,0:T(8,128)S(1)}, u32[]{:S(2)}, u32[]{:S(2)}) collective-permute-start(f32[72,128]{1,0:T(8,128)S(1)} %get-tuple-element.56.refs_0_), channel_id=1, source_target_pairs={{0,2},{1,3},{2,0},{3,1},{4,6},{5,7},{6,4},{7,5},{8,10},{9,11},{10,... | collective-permute-start | bytes 110600 | tf_op jit(solution)/shard_map/sum_req/ppermute | solution.py:287
  45.4 4.0 %collective-permute-start.13 = (f32[72,128]{1,0:T(8,128)S(1)}, f32[72,128]{1,0:T(8,128)S(1)}, u32[]{:S(2)}, u32[]{:S(2)}) collective-permute-start(f32[72,128]{1,0:T(8,128)S(1)} %get-tuple-element.56.refs_0_), channel_id=1, source_target_pairs={{0,3},{1,2},{2,1},{3,0},{4,7},{5,6},{6,5},{7,4},{8,11},{9,10},{10,... | collective-permute-start | bytes 110600 | tf_op jit(solution)/shard_map/sum_req/ppermute | solution.py:287
  53.7 5.5 %collective-permute-start.16 = (f32[136,128]{1,0:T(8,128)S(1)}, f32[136,128]{1,0:T(8,128)S(1)}, u32[]{:S(2)}, u32[]{:S(2)}) collective-permute-start(f32[136,128]{1,0:T(8,128)S(1)} %add.87), channel_id=1, source_target_pairs={{0,1},{1,0},{2,3},{3,2},{4,52},{5,53},{6,54},{7,55},{8,9},{9,8},{1... | collective-permute-start | bytes 208904 | tf_op jit(solution)/shard_map/sum_z_outer/ppermute | solution.py:278
  59.2 4.1 %collective-permute-start.19 = (f32[136,128]{1,0:T(8,128)S(1)}, f32[136,128]{1,0:T(8,128)S(1)}, u32[]{:S(2)}, u32[]{:S(2)}) collective-permute-start(f32[136,128]{1,0:T(8,128)S(1)} %add.88), channel_id=1, source_target_pairs={{0,1},{1,0},{2,3},{3,2},{4,20},{5,21},{6,22},{7,23},{8,9},{9,8},{1... | collective-permute-start | bytes 208904 | tf_op jit(solution)/shard_map/sum_z_inner/ppermute | solution.py:278
  61.2 5.1 %collective-permute-start.18 = (f32[136,128]{1,0:T(8,128)S(1)}, f32[136,128]{1,0:T(8,128)S(1)}, u32[]{:S(2)}, u32[]{:S(2)}) collective-permute-start(f32[136,128]{1,0:T(8,128)S(1)} %add.88), channel_id=1, source_target_pairs={{0,1},{1,0},{2,3},{3,2},{4,28},{5,29},{6,30},{7,31},{8,9},{9,8},{1... | collective-permute-start | bytes 208904 | tf_op jit(solution)/shard_map/sum_z_inner/ppermute | solution.py:278
  63.0 3.9 %collective-permute-start.17 = (f32[136,128]{1,0:T(8,128)S(1)}, f32[136,128]{1,0:T(8,128)S(1)}, u32[]{:S(2)}, u32[]{:S(2)}) collective-permute-start(f32[136,128]{1,0:T(8,128)S(1)} %add.88), channel_id=1, source_target_pairs={{0,1},{1,0},{2,3},{3,2},{4,12},{5,13},{6,14},{7,15},{8,9},{9,8},{1... | collective-permute-start | bytes 208904 | tf_op jit(solution)/shard_map/sum_z_inner/ppermute | solution.py:278
  66.9 4.8 %collective-permute-start.22 = (f32[136,128]{1,0:T(8,128)S(1)}, f32[136,128]{1,0:T(8,128)S(1)}, u32[]{:S(2)}, u32[]{:S(2)}) collective-permute-start(f32[136,128]{1,0:T(8,128)S(1)} %add_add_fusion.3), channel_id=1, source_target_pairs={{0,1},{1,0},{2,3},{3,2},{4,132},{5,133},{6,134},{7,135},{8,9},{9,8... | collective-permute-start | bytes 208904 | tf_op jit(solution)/shard_map/sum_y/ppermute | solution.py:278
  68.2 4.4 %collective-permute-start.21 = (f32[136,128]{1,0:T(8,128)S(1)}, f32[136,128]{1,0:T(8,128)S(1)}, u32[]{:S(2)}, u32[]{:S(2)}) collective-permute-start(f32[136,128]{1,0:T(8,128)S(1)} %add_add_fusion.3), channel_id=1, source_target_pairs={{0,1},{1,0},{2,3},{3,2},{4,196},{5,197},{6,198},{7,199},{8,9},{9,8... | collective-permute-start | bytes 208904 | tf_op jit(solution)/shard_map/sum_y/ppermute | solution.py:278
  68.9 3.6 %collective-permute-start.20 = (f32[136,128]{1,0:T(8,128)S(1)}, f32[136,128]{1,0:T(8,128)S(1)}, u32[]{:S(2)}, u32[]{:S(2)}) collective-permute-start(f32[136,128]{1,0:T(8,128)S(1)} %add_add_fusion.3), channel_id=1, source_target_pairs={{0,1},{1,0},{2,3},{3,2},{4,68},{5,69},{6,70},{7,71},{8,9},{9,8},{1... | collective-permute-start | bytes 208904 | tf_op jit(solution)/shard_map/sum_y/ppermute | solution.py:278
  75.0 4.3 %collective-permute-start.26 = (f32[72,128]{1,0:T(8,128)S(1)}, f32[72,128]{1,0:T(8,128)S(1)}, u32[]{:S(2)}, u32[]{:S(2)}) collective-permute-start(f32[72,128]{1,0:T(8,128)S(1)} %get-tuple-element.63.refs_0_), channel_id=1, source_target_pairs={{0,2},{1,3},{2,0},{3,1},{4,6},{5,7},{6,4},{7,5},{8,10},{9,11},{10,... | collective-permute-start | bytes 110600 | tf_op jit(solution)/shard_map/sum_req/ppermute | solution.py:287
  76.2 4.1 %collective-permute-start.25 = (f32[72,128]{1,0:T(8,128)S(1)}, f32[72,128]{1,0:T(8,128)S(1)}, u32[]{:S(2)}, u32[]{:S(2)}) collective-permute-start(f32[72,128]{1,0:T(8,128)S(1)} %get-tuple-element.63.refs_0_), channel_id=1, source_target_pairs={{0,3},{1,2},{2,1},{3,0},{4,7},{5,6},{6,5},{7,4},{8,11},{9,10},{10,... | collective-permute-start | bytes 110600 | tf_op jit(solution)/shard_map/sum_req/ppermute | solution.py:287
  77.1 3.3 %collective-permute-start.24 = (f32[72,128]{1,0:T(8,128)S(1)}, f32[72,128]{1,0:T(8,128)S(1)}, u32[]{:S(2)}, u32[]{:S(2)}) collective-permute-start(f32[72,128]{1,0:T(8,128)S(1)} %get-tuple-element.63.refs_0_), channel_id=1, source_target_pairs={{0,1},{1,0},{2,3},{3,2},{4,5},{5,4},{6,7},{7,6},{8,9},{9,8},{10,11... | collective-permute-start | bytes 110600 | tf_op jit(solution)/shard_map/sum_req/ppermute | solution.py:287
  84.3 5.4 %collective-permute-start.28 = (f32[136,128]{1,0:T(8,128)S(1)}, f32[136,128]{1,0:T(8,128)S(1)}, u32[]{:S(2)}, u32[]{:S(2)}) collective-permute-start(f32[136,128]{1,0:T(8,128)S(1)} %add.95), channel_id=1, source_target_pairs={{0,1},{1,0},{2,3},{3,2},{4,52},{5,53},{6,54},{7,55},{8,9},{9,8},{1... | collective-permute-start | bytes 208904 | tf_op jit(solution)/shard_map/sum_z_outer/ppermute | solution.py:278
  89.7 4.9 %collective-permute-start.31 = (f32[136,128]{1,0:T(8,128)S(1)}, f32[136,128]{1,0:T(8,128)S(1)}, u32[]{:S(2)}, u32[]{:S(2)}) collective-permute-start(f32[136,128]{1,0:T(8,128)S(1)} %add.96), channel_id=1, source_target_pairs={{0,1},{1,0},{2,3},{3,2},{4,20},{5,21},{6,22},{7,23},{8,9},{9,8},{1... | collective-permute-start | bytes 208904 | tf_op jit(solution)/shard_map/sum_z_inner/ppermute | solution.py:278
  90.6 5.1 %collective-permute-start.30 = (f32[136,128]{1,0:T(8,128)S(1)}, f32[136,128]{1,0:T(8,128)S(1)}, u32[]{:S(2)}, u32[]{:S(2)}) collective-permute-start(f32[136,128]{1,0:T(8,128)S(1)} %add.96), channel_id=1, source_target_pairs={{0,1},{1,0},{2,3},{3,2},{4,28},{5,29},{6,30},{7,31},{8,9},{9,8},{1... | collective-permute-start | bytes 208904 | tf_op jit(solution)/shard_map/sum_z_inner/ppermute | solution.py:278
  92.2 3.9 %collective-permute-start.29 = (f32[136,128]{1,0:T(8,128)S(1)}, f32[136,128]{1,0:T(8,128)S(1)}, u32[]{:S(2)}, u32[]{:S(2)}) collective-permute-start(f32[136,128]{1,0:T(8,128)S(1)} %add.96), channel_id=1, source_target_pairs={{0,1},{1,0},{2,3},{3,2},{4,12},{5,13},{6,14},{7,15},{8,9},{9,8},{1... | collective-permute-start | bytes 208904 | tf_op jit(solution)/shard_map/sum_z_inner/ppermute | solution.py:278
  96.2 4.8 %collective-permute-start.34 = (f32[136,128]{1,0:T(8,128)S(1)}, f32[136,128]{1,0:T(8,128)S(1)}, u32[]{:S(2)}, u32[]{:S(2)}) collective-permute-start(f32[136,128]{1,0:T(8,128)S(1)} %add_add_fusion.1), channel_id=1, source_target_pairs={{0,1},{1,0},{2,3},{3,2},{4,132},{5,133},{6,134},{7,135},{8,9},{9,8... | collective-permute-start | bytes 208904 | tf_op jit(solution)/shard_map/sum_y/ppermute | solution.py:278
  97.5 4.4 %collective-permute-start.33 = (f32[136,128]{1,0:T(8,128)S(1)}, f32[136,128]{1,0:T(8,128)S(1)}, u32[]{:S(2)}, u32[]{:S(2)}) collective-permute-start(f32[136,128]{1,0:T(8,128)S(1)} %add_add_fusion.1), channel_id=1, source_target_pairs={{0,1},{1,0},{2,3},{3,2},{4,196},{5,197},{6,198},{7,199},{8,9},{9,8... | collective-permute-start | bytes 208904 | tf_op jit(solution)/shard_map/sum_y/ppermute | solution.py:278
  98.6 3.3 %collective-permute-start.32 = (f32[136,128]{1,0:T(8,128)S(1)}, f32[136,128]{1,0:T(8,128)S(1)}, u32[]{:S(2)}, u32[]{:S(2)}) collective-permute-start(f32[136,128]{1,0:T(8,128)S(1)} %add_add_fusion.1), channel_id=1, source_target_pairs={{0,1},{1,0},{2,3},{3,2},{4,68},{5,69},{6,70},{7,71},{8,9},{9,8},{1... | collective-permute-start | bytes 208904 | tf_op jit(solution)/shard_map/sum_y/ppermute | solution.py:278
  102.0 7.5 %collective-permute-start.35 = (f32[136,128]{1,0:T(8,128)S(1)}, f32[136,128]{1,0:T(8,128)S(1)}, u32[]{:S(2)}, u32[]{:S(2)}) collective-permute-start(f32[136,128]{1,0:T(8,128)S(1)} %constant_dynamic-update-slice_fusion.state_own), channel_id=1, source_target_pairs={{0,4},{1,5},{2,6},{3,7},{4,0},{5,1},{6,2},{7,3},{8,12},{9,13},{10,... | collective-permute-start | bytes 208904 | tf_op jit(solution)/shard_map/back_core/ppermute | solution.py:278
  102.4 4.0 %collective-permute-start.38 = (f32[8,128]{1,0:T(8,128)S(1)}, f32[8,128]{1,0:T(8,128)S(1)}, u32[]{:S(2)}, u32[]{:S(2)}) collective-permute-start(f32[8,128]{1,0:T(8,128)S(1)} %get-tuple-element.74.last_0), channel_id=1, source_target_pairs={{0,64},{1,65},{2,66},{3,67},{4,6},{5,7},{6,4},{7,5},{8,72},{9,73},... | collective-permute-start | bytes 12296 | tf_op jit(solution)/shard_map/sum_req_last/ppermute | solution.py:278
  104.4 3.7 %collective-permute-start.37 = (f32[8,128]{1,0:T(8,128)S(1)}, f32[8,128]{1,0:T(8,128)S(1)}, u32[]{:S(2)}, u32[]{:S(2)}) collective-permute-start(f32[8,128]{1,0:T(8,128)S(1)} %get-tuple-element.74.last_0), channel_id=1, source_target_pairs={{0,64},{1,65},{2,66},{3,67},{4,7},{5,6},{6,5},{7,4},{8,72},{9,73},... | collective-permute-start | bytes 12296 | tf_op jit(solution)/shard_map/sum_req_last/ppermute | solution.py:278
  (14 other events, 127.0 us)

commit v5 on v3

--- a/solution.py
+++ b/solution.py
@@ -278,7 +278,7 @@
         return on_mesh(x, lambda y, z, c, r: (y, z, 1 - c, r))
 
     def chips(x, y_bits, z_bits):
-        return on_mesh(x, lambda y, z, c, r: (y ^ y_bits, z ^ z_bits, c, r) if c == 1 else (y, z, c, r ^ 1))
+        return on_mesh(x, lambda y, z, c, r: (y ^ y_bits, z ^ z_bits, c, r) if c == 1 else (y ^ (z_bits > 0), z ^ (y_bits > 0), c, r))
 
     def on_req(x):
         return [lax.ppermute(x, "req", [(i, i ^ bit) for i in range(n_req)]) for bit in (1, 3, 2)]

time: 110 us -> 110 us (level)
  transfers between devices with their start and end apart: 40 -> 40, of which waited for: 31 -> 30; matrix products, arithmetic and copies ran while one was open for 0% -> 0% of each run, Pallas kernels for 1% -> 1%
where the time goes in v5:
time: 110 us
  starting transfers between devices  49.8 us (45%)
  waiting for transfers between devices  43.5 us (40%)
  Pallas kernels  13 us (12%)
  between operations  2.83 us (3%)
    ppermute x31, starting transfers between devices, on_mesh(): return lax.ppermute(x, ('tst', 'req'), pairs)  39.7 us
    ppermute x31, waiting for transfers between devices, on_mesh(): return lax.ppermute(x, ('tst', 'req'), pairs)  36.9 us
    ppermute x9, starting transfers between devices, on_req(): lax.ppermute(x, 'req', [(i, i ^ bit) for i in range(n_req)])  10.1 us
    ppermute x9, waiting for transfers between devices, on_req(): lax.ppermute(x, 'req', [(i, i ^ bit) for i in range(n_req)])  6.59 us
    pallas_call x3, Pallas kernels, per_device(): call(functools.partial(primal_load_kernel, iteration), outs, [VMEM] * len...  4.7 us
    pallas_call x1, Pallas kernels, per_device(): call(first_pull_kernel, (pull_shape, struct(slots, req_blocks, dtype=BF16...  4.07 us
  transfers between devices with their start and end apart: 40, of which 30 were waited for; matrix products, arithmetic and copies ran while one was open for 0% of the time, Pallas kernels for 1%

profile of v5, /device:TPU:1, one launch (start us, length us, event | category | flops | bytes accessed | tf_op | source)
XLA Modules:
  0.0 109.6 jit_solution(10925031907463755667)
XLA Ops:
  1.3 4.1 %shard_map.147 = (f32[72,128]{1,0:T(8,128)S(1)}, bf16[128,128]{1,0:T(8,128)(2,1)S(1)}, f32[64,128]{1,0:T(8,128)S(1)}, bf16[16,128,128]{2,1,0:T(8,128)(2,1)S(1)},...) custom-call(bf16[128,128,128]{2,1,0:T(8,128)(2,1)} %tiles_in.3, ...), custom_call_target="tpu_custom_call" | custom-call | tf_op jit(solution)/shard_map/pallas_call | solution.py:322
  5.4 3.7 %collective-permute-start.2 = (f32[72,128]{1,0:T(8,128)S(1)}, f32[72,128]{1,0:T(8,128)S(1)}, u32[]{:S(2)}, u32[]{:S(2)}) collective-permute-start(f32[72,128]{1,0:T(8,128)S(1)} %get-tuple-element.42.refs_0_), channel_id=1, source_target_pairs={{0,2},{1,3},{2,0},{3,1},{4,6},{5,7},{6,4},{7,5},{8,10},{9,11},{10,... | collective-permute-start | bytes 110600 | tf_op jit(solution)/shard_map/sum_req/ppermute | solution.py:284
  13.5 1.6 %shard_map.149 = (f32[136,128]{1,0:T(8,128)S(1)}, f32[64,128]{1,0:T(8,128)S(1)}, f32[64,128]{1,0:T(8,128)S(1)}) custom-call(f32[72,128]{1,0:T(8,128)S(1)} %get-tuple-element.42.refs_0_, f32[72,128]{1,0:T(8,128)S(1)} %collective-permute-done.refs_1_, f32[72,128]{1,0:T(8,128)S(1)} %collective-permute-done.1.refs_2_, ...), custom_call_target="tpu_custom_call" | custom-call | tf_op jit(solution)/shard_map/pallas_call | solution.py:351
  15.1 1.9 %collective-permute-start.3 = (f32[136,128]{1,0:T(8,128)S(1)}, f32[136,128]{1,0:T(8,128)S(1)}, u32[]{:S(2)}, u32[]{:S(2)}) collective-permute-start(f32[136,128]{1,0:T(8,128)S(1)} %get-tuple-element.55), channel_id=1, source_target_pairs={{0,4},{1,5},{2,6},{3,7},{4,0},{5,1},{6,2},{7,3},{8,12},{9,13},{10,... | collective-permute-start | bytes 208904 | tf_op jit(solution)/shard_map/sum_core/ppermute | solution.py:275
  17.9 6.1 %collective-permute-start.4 = (f32[136,128]{1,0:T(8,128)S(1)}, f32[136,128]{1,0:T(8,128)S(1)}, u32[]{:S(2)}, u32[]{:S(2)}) collective-permute-start(f32[136,128]{1,0:T(8,128)S(1)} %add.79), channel_id=1, source_target_pairs={{0,64},{1,65},{2,66},{3,67},{4,52},{5,53},{6,54},{7,55},{8,72},{9,... | collective-permute-start | bytes 208904 | tf_op jit(solution)/shard_map/sum_z_outer/ppermute | solution.py:275
  24.0 1.8 %collective-permute-done.4 = f32[136,128]{1,0:T(8,128)S(1)} collective-permute-done((f32[136,128]{1,0:T(8,128)S(1)}, f32[136,128]{1,0:T(8,128)S(1)}, u32[]{:S(2)}, u32[]{:S(2)}) %collective-permute-start.4) | collective-permute-done | bytes 69664 | tf_op jit(solution)/shard_map/sum_z_outer/ppermute | solution.py:275
  27.0 2.4 %collective-permute-start.6 = (f32[136,128]{1,0:T(8,128)S(1)}, f32[136,128]{1,0:T(8,128)S(1)}, u32[]{:S(2)}, u32[]{:S(2)}) collective-permute-start(f32[136,128]{1,0:T(8,128)S(1)} %add.80), channel_id=1, source_target_pairs={{0,64},{1,65},{2,66},{3,67},{4,28},{5,29},{6,30},{7,31},{8,72},{9,... | collective-permute-start | bytes 208904 | tf_op jit(solution)/shard_map/sum_z_inner/ppermute | solution.py:275
  30.0 2.1 %collective-permute-done.6 = f32[136,128]{1,0:T(8,128)S(1)} collective-permute-done((f32[136,128]{1,0:T(8,128)S(1)}, f32[136,128]{1,0:T(8,128)S(1)}, u32[]{:S(2)}, u32[]{:S(2)}) %collective-permute-start.6) | collective-permute-done | bytes 69664 | tf_op jit(solution)/shard_map/sum_z_inner/ppermute | solution.py:275
  33.5 3.3 %collective-permute-start.10 = (f32[136,128]{1,0:T(8,128)S(1)}, f32[136,128]{1,0:T(8,128)S(1)}, u32[]{:S(2)}, u32[]{:S(2)}) collective-permute-start(f32[136,128]{1,0:T(8,128)S(1)} %add_add_fusion.5), channel_id=1, source_target_pairs={{0,8},{1,9},{2,10},{3,11},{4,132},{5,133},{6,134},{7,135},{8,0},{9... | collective-permute-start | bytes 208904 | tf_op jit(solution)/shard_map/sum_y/ppermute | solution.py:275
  38.5 2.7 %collective-permute-done.9 = f32[136,128]{1,0:T(8,128)S(1)} collective-permute-done((f32[136,128]{1,0:T(8,128)S(1)}, f32[136,128]{1,0:T(8,128)S(1)}, u32[]{:S(2)}, u32[]{:S(2)}) %collective-permute-start.9) | collective-permute-done | bytes 69664 | tf_op jit(solution)/shard_map/sum_y/ppermute | solution.py:275
  43.6 2.0 %collective-permute-start.14 = (f32[72,128]{1,0:T(8,128)S(1)}, f32[72,128]{1,0:T(8,128)S(1)}, u32[]{:S(2)}, u32[]{:S(2)}) collective-permute-start(f32[72,128]{1,0:T(8,128)S(1)} %get-tuple-element.56.refs_0_), channel_id=1, source_target_pairs={{0,2},{1,3},{2,0},{3,1},{4,6},{5,7},{6,4},{7,5},{8,10},{9,11},{10,... | collective-permute-start | bytes 110600 | tf_op jit(solution)/shard_map/sum_req/ppermute | solution.py:284
  46.4 1.5 %collective-permute-done.14.refs_3_ = f32[72,128]{1,0:T(8,128)S(1)} collective-permute-done((f32[72,128]{1,0:T(8,128)S(1)}, f32[72,128]{1,0:T(8,128)S(1)}, u32[]{:S(2)}, u32[]{:S(2)}) %collective-permute-start.14) | collective-permute-done | bytes 36896 | tf_op jit(solution)/shard_map/sum_req/ppermute | solution.py:284
  47.9 1.7 %collective-permute-done.13.refs_2_ = f32[72,128]{1,0:T(8,128)S(1)} collective-permute-done((f32[72,128]{1,0:T(8,128)S(1)}, f32[72,128]{1,0:T(8,128)S(1)}, u32[]{:S(2)}, u32[]{:S(2)}) %collective-permute-start.13) | collective-permute-done | bytes 36896 | tf_op jit(solution)/shard_map/sum_req/ppermute | solution.py:284
  49.6 1.6 %shard_map.151 = (f32[136,128]{1,0:T(8,128)S(1)}, f32[64,128]{1,0:T(8,128)S(1)}, f32[64,128]{1,0:T(8,128)S(1)}, f32[8,128]{1,0:T(8,128)S(1)}) custom-call(f32[72,128]{1,0:T(8,128)S(1)} %get-tuple-element.56.refs_0_, f32[72,128]{1,0:T(8,128)S(1)} %collective-permute-done.12.refs_1_, f32[72,128]{1,0:T(8,128)S(1)} %collective-permute-done.13.refs_2_, ...), custom_call_target="tpu_custom_call" | custom-call | tf_op jit(solution)/shard_map/pallas_call | solution.py:351
  51.2 1.9 %collective-permute-start.15 = (f32[136,128]{1,0:T(8,128)S(1)}, f32[136,128]{1,0:T(8,128)S(1)}, u32[]{:S(2)}, u32[]{:S(2)}) collective-permute-start(f32[136,128]{1,0:T(8,128)S(1)} %get-tuple-element.60), channel_id=1, source_target_pairs={{0,4},{1,5},{2,6},{3,7},{4,0},{5,1},{6,2},{7,3},{8,12},{9,13},{10,... | collective-permute-start | bytes 208904 | tf_op jit(solution)/shard_map/sum_core/ppermute | solution.py:275
  53.9 2.5 %collective-permute-start.16 = (f32[136,128]{1,0:T(8,128)S(1)}, f32[136,128]{1,0:T(8,128)S(1)}, u32[]{:S(2)}, u32[]{:S(2)}) collective-permute-start(f32[136,128]{1,0:T(8,128)S(1)} %add.87), channel_id=1, source_target_pairs={{0,64},{1,65},{2,66},{3,67},{4,52},{5,53},{6,54},{7,55},{8,72},{9,... | collective-permute-start | bytes 208904 | tf_op jit(solution)/shard_map/sum_z_outer/ppermute | solution.py:275
  56.4 2.9 %collective-permute-done.16 = f32[136,128]{1,0:T(8,128)S(1)} collective-permute-done((f32[136,128]{1,0:T(8,128)S(1)}, f32[136,128]{1,0:T(8,128)S(1)}, u32[]{:S(2)}, u32[]{:S(2)}) %collective-permute-start.16) | collective-permute-done | bytes 69664 | tf_op jit(solution)/shard_map/sum_z_outer/ppermute | solution.py:275
  59.3 1.4 %collective-permute-start.19 = (f32[136,128]{1,0:T(8,128)S(1)}, f32[136,128]{1,0:T(8,128)S(1)}, u32[]{:S(2)}, u32[]{:S(2)}) collective-permute-start(f32[136,128]{1,0:T(8,128)S(1)} %add.88), channel_id=1, source_target_pairs={{0,64},{1,65},{2,66},{3,67},{4,20},{5,21},{6,22},{7,23},{8,72},{9,... | collective-permute-start | bytes 208904 | tf_op jit(solution)/shard_map/sum_z_inner/ppermute | solution.py:275
  62.1 2.2 %collective-permute-done.19 = f32[136,128]{1,0:T(8,128)S(1)} collective-permute-done((f32[136,128]{1,0:T(8,128)S(1)}, f32[136,128]{1,0:T(8,128)S(1)}, u32[]{:S(2)}, u32[]{:S(2)}) %collective-permute-start.19) | collective-permute-done | bytes 69664 | tf_op jit(solution)/shard_map/sum_z_inner/ppermute | solution.py:275
  64.2 1.5 %collective-permute-done.18 = f32[136,128]{1,0:T(8,128)S(1)} collective-permute-done((f32[136,128]{1,0:T(8,128)S(1)}, f32[136,128]{1,0:T(8,128)S(1)}, u32[]{:S(2)}, u32[]{:S(2)}) %collective-permute-start.18) | collective-permute-done | bytes 69664 | tf_op jit(solution)/shard_map/sum_z_inner/ppermute | solution.py:275
  68.5 2.0 %collective-permute-done.22 = f32[136,128]{1,0:T(8,128)S(1)} collective-permute-done((f32[136,128]{1,0:T(8,128)S(1)}, f32[136,128]{1,0:T(8,128)S(1)}, u32[]{:S(2)}, u32[]{:S(2)}) %collective-permute-start.22) | collective-permute-done | bytes 69664 | tf_op jit(solution)/shard_map/sum_y/ppermute | solution.py:275
  76.5 1.7 %collective-permute-done.26.refs_3_ = f32[72,128]{1,0:T(8,128)S(1)} collective-permute-done((f32[72,128]{1,0:T(8,128)S(1)}, f32[72,128]{1,0:T(8,128)S(1)}, u32[]{:S(2)}, u32[]{:S(2)}) %collective-permute-start.26) | collective-permute-done | bytes 36896 | tf_op jit(solution)/shard_map/sum_req/ppermute | solution.py:284
  79.2 1.6 %shard_map.153 = (f32[136,128]{1,0:T(8,128)S(1)}, f32[64,128]{1,0:T(8,128)S(1)}, f32[8,128]{1,0:T(8,128)S(1)}) custom-call(f32[72,128]{1,0:T(8,128)S(1)} %get-tuple-element.63.refs_0_, f32[72,128]{1,0:T(8,128)S(1)} %collective-permute-done.24.refs_1_, f32[72,128]{1,0:T(8,128)S(1)} %collective-permute-done.25.refs_2_, ...), custom_call_target="tpu_custom_call" | custom-call | tf_op jit(solution)/shard_map/pallas_call | solution.py:351
  80.8 1.5 %collective-permute-start.27 = (f32[136,128]{1,0:T(8,128)S(1)}, f32[136,128]{1,0:T(8,128)S(1)}, u32[]{:S(2)}, u32[]{:S(2)}) collective-permute-start(f32[136,128]{1,0:T(8,128)S(1)} %get-tuple-element.67), channel_id=1, source_target_pairs={{0,4},{1,5},{2,6},{3,7},{4,0},{5,1},{6,2},{7,3},{8,12},{9,13},{10,... | collective-permute-start | bytes 208904 | tf_op jit(solution)/shard_map/sum_core/ppermute | solution.py:275
  83.2 2.9 %collective-permute-start.28 = (f32[136,128]{1,0:T(8,128)S(1)}, f32[136,128]{1,0:T(8,128)S(1)}, u32[]{:S(2)}, u32[]{:S(2)}) collective-permute-start(f32[136,128]{1,0:T(8,128)S(1)} %add.95), channel_id=1, source_target_pairs={{0,64},{1,65},{2,66},{3,67},{4,52},{5,53},{6,54},{7,55},{8,72},{9,... | collective-permute-start | bytes 208904 | tf_op jit(solution)/shard_map/sum_z_outer/ppermute | solution.py:275
  86.2 2.4 %collective-permute-done.28 = f32[136,128]{1,0:T(8,128)S(1)} collective-permute-done((f32[136,128]{1,0:T(8,128)S(1)}, f32[136,128]{1,0:T(8,128)S(1)}, u32[]{:S(2)}, u32[]{:S(2)}) %collective-permute-start.28) | collective-permute-done | bytes 69664 | tf_op jit(solution)/shard_map/sum_z_outer/ppermute | solution.py:275
  89.7 1.6 %collective-permute-start.30 = (f32[136,128]{1,0:T(8,128)S(1)}, f32[136,128]{1,0:T(8,128)S(1)}, u32[]{:S(2)}, u32[]{:S(2)}) collective-permute-start(f32[136,128]{1,0:T(8,128)S(1)} %add.96), channel_id=1, source_target_pairs={{0,64},{1,65},{2,66},{3,67},{4,28},{5,29},{6,30},{7,31},{8,72},{9,... | collective-permute-start | bytes 208904 | tf_op jit(solution)/shard_map/sum_z_inner/ppermute | solution.py:275
  91.4 2.2 %collective-permute-done.31 = f32[136,128]{1,0:T(8,128)S(1)} collective-permute-done((f32[136,128]{1,0:T(8,128)S(1)}, f32[136,128]{1,0:T(8,128)S(1)}, u32[]{:S(2)}, u32[]{:S(2)}) %collective-permute-start.31) | collective-permute-done | bytes 69664 | tf_op jit(solution)/shard_map/sum_z_inner/ppermute | solution.py:275
  95.2 1.7 %collective-permute-start.34 = (f32[136,128]{1,0:T(8,128)S(1)}, f32[136,128]{1,0:T(8,128)S(1)}, u32[]{:S(2)}, u32[]{:S(2)}) collective-permute-start(f32[136,128]{1,0:T(8,128)S(1)} %add_add_fusion.1), channel_id=1, source_target_pairs={{0,8},{1,9},{2,10},{3,11},{4,132},{5,133},{6,134},{7,135},{8,0},{9... | collective-permute-start | bytes 208904 | tf_op jit(solution)/shard_map/sum_y/ppermute | solution.py:275
  98.1 1.8 %collective-permute-done.34 = f32[136,128]{1,0:T(8,128)S(1)} collective-permute-done((f32[136,128]{1,0:T(8,128)S(1)}, f32[136,128]{1,0:T(8,128)S(1)}, u32[]{:S(2)}, u32[]{:S(2)}) %collective-permute-start.34) | collective-permute-done | bytes 69664 | tf_op jit(solution)/shard_map/sum_y/ppermute | solution.py:275
  101.7 2.1 %collective-permute-start.38 = (f32[8,128]{1,0:T(8,128)S(1)}, f32[8,128]{1,0:T(8,128)S(1)}, u32[]{:S(2)}, u32[]{:S(2)}) collective-permute-start(f32[8,128]{1,0:T(8,128)S(1)} %get-tuple-element.74.last_0), channel_id=1, source_target_pairs={{0,64},{1,65},{2,66},{3,67},{4,6},{5,7},{6,4},{7,5},{8,72},{9,73},... | collective-permute-start | bytes 12296 | tf_op jit(solution)/shard_map/sum_req_last/ppermute | solution.py:275
  105.8 1.7 %collective-permute-done.37.last_2 = f32[8,128]{1,0:T(8,128)S(1)} collective-permute-done((f32[8,128]{1,0:T(8,128)S(1)}, f32[8,128]{1,0:T(8,128)S(1)}, u32[]{:S(2)}, u32[]{:S(2)}) %collective-permute-start.37) | collective-permute-done | bytes 4128 | tf_op jit(solution)/shard_map/sum_req_last/ppermute | solution.py:275
  (92 shorter events, 35.0 us)
Async XLA Ops:
  5.4 7.2 %collective-permute-start.2 = (f32[72,128]{1,0:T(8,128)S(1)}, f32[72,128]{1,0:T(8,128)S(1)}, u32[]{:S(2)}, u32[]{:S(2)}) collective-permute-start(f32[72,128]{1,0:T(8,128)S(1)} %get-tuple-element.42.refs_0_), channel_id=1, source_target_pairs={{0,2},{1,3},{2,0},{3,1},{4,6},{5,7},{6,4},{7,5},{8,10},{9,11},{10,... | collective-permute-start | bytes 110600 | tf_op jit(solution)/shard_map/sum_req/ppermute | solution.py:284
  9.1 4.3 %collective-permute-start.1 = (f32[72,128]{1,0:T(8,128)S(1)}, f32[72,128]{1,0:T(8,128)S(1)}, u32[]{:S(2)}, u32[]{:S(2)}) collective-permute-start(f32[72,128]{1,0:T(8,128)S(1)} %get-tuple-element.42.refs_0_), channel_id=1, source_target_pairs={{0,3},{1,2},{2,1},{3,0},{4,7},{5,6},{6,5},{7,4},{8,11},{9,10},{10,... | collective-permute-start | bytes 110600 | tf_op jit(solution)/shard_map/sum_req/ppermute | solution.py:284
  9.9 3.5 %collective-permute-start = (f32[72,128]{1,0:T(8,128)S(1)}, f32[72,128]{1,0:T(8,128)S(1)}, u32[]{:S(2)}, u32[]{:S(2)}) collective-permute-start(f32[72,128]{1,0:T(8,128)S(1)} %get-tuple-element.42.refs_0_), channel_id=1, source_target_pairs={{0,1},{1,0},{2,3},{3,2},{4,5},{5,4},{6,7},{7,6},{8,9},{9,8},{10,11... | collective-permute-start | bytes 110600 | tf_op jit(solution)/shard_map/sum_req/ppermute | solution.py:284
  17.9 7.9 %collective-permute-start.4 = (f32[136,128]{1,0:T(8,128)S(1)}, f32[136,128]{1,0:T(8,128)S(1)}, u32[]{:S(2)}, u32[]{:S(2)}) collective-permute-start(f32[136,128]{1,0:T(8,128)S(1)} %add.79), channel_id=1, source_target_pairs={{0,64},{1,65},{2,66},{3,67},{4,52},{5,53},{6,54},{7,55},{8,72},{9,... | collective-permute-start | bytes 208904 | tf_op jit(solution)/shard_map/sum_z_outer/ppermute | solution.py:275
  25.8 4.1 %collective-permute-start.7 = (f32[136,128]{1,0:T(8,128)S(1)}, f32[136,128]{1,0:T(8,128)S(1)}, u32[]{:S(2)}, u32[]{:S(2)}) collective-permute-start(f32[136,128]{1,0:T(8,128)S(1)} %add.80), channel_id=1, source_target_pairs={{0,64},{1,65},{2,66},{3,67},{4,20},{5,21},{6,22},{7,23},{8,72},{9,... | collective-permute-start | bytes 208904 | tf_op jit(solution)/shard_map/sum_z_inner/ppermute | solution.py:275
  27.0 5.0 %collective-permute-start.6 = (f32[136,128]{1,0:T(8,128)S(1)}, f32[136,128]{1,0:T(8,128)S(1)}, u32[]{:S(2)}, u32[]{:S(2)}) collective-permute-start(f32[136,128]{1,0:T(8,128)S(1)} %add.80), channel_id=1, source_target_pairs={{0,64},{1,65},{2,66},{3,67},{4,28},{5,29},{6,30},{7,31},{8,72},{9,... | collective-permute-start | bytes 208904 | tf_op jit(solution)/shard_map/sum_z_inner/ppermute | solution.py:275
  29.4 4.1 %collective-permute-start.5 = (f32[136,128]{1,0:T(8,128)S(1)}, f32[136,128]{1,0:T(8,128)S(1)}, u32[]{:S(2)}, u32[]{:S(2)}) collective-permute-start(f32[136,128]{1,0:T(8,128)S(1)} %add.80), channel_id=1, source_target_pairs={{0,64},{1,65},{2,66},{3,67},{4,12},{5,13},{6,14},{7,15},{8,72},{9,... | collective-permute-start | bytes 208904 | tf_op jit(solution)/shard_map/sum_z_inner/ppermute | solution.py:275
  33.5 5.0 %collective-permute-start.10 = (f32[136,128]{1,0:T(8,128)S(1)}, f32[136,128]{1,0:T(8,128)S(1)}, u32[]{:S(2)}, u32[]{:S(2)}) collective-permute-start(f32[136,128]{1,0:T(8,128)S(1)} %add_add_fusion.5), channel_id=1, source_target_pairs={{0,8},{1,9},{2,10},{3,11},{4,132},{5,133},{6,134},{7,135},{8,0},{9... | collective-permute-start | bytes 208904 | tf_op jit(solution)/shard_map/sum_y/ppermute | solution.py:275
  36.8 4.4 %collective-permute-start.9 = (f32[136,128]{1,0:T(8,128)S(1)}, f32[136,128]{1,0:T(8,128)S(1)}, u32[]{:S(2)}, u32[]{:S(2)}) collective-permute-start(f32[136,128]{1,0:T(8,128)S(1)} %add_add_fusion.5), channel_id=1, source_target_pairs={{0,8},{1,9},{2,10},{3,11},{4,196},{5,197},{6,198},{7,199},{8,0},{9... | collective-permute-start | bytes 208904 | tf_op jit(solution)/shard_map/sum_y/ppermute | solution.py:275
  37.5 3.6 %collective-permute-start.8 = (f32[136,128]{1,0:T(8,128)S(1)}, f32[136,128]{1,0:T(8,128)S(1)}, u32[]{:S(2)}, u32[]{:S(2)}) collective-permute-start(f32[136,128]{1,0:T(8,128)S(1)} %add_add_fusion.5), channel_id=1, source_target_pairs={{0,8},{1,9},{2,10},{3,11},{4,68},{5,69},{6,70},{7,71},{8,0},{9,1},... | collective-permute-start | bytes 208904 | tf_op jit(solution)/shard_map/sum_y/ppermute | solution.py:275
  43.6 4.3 %collective-permute-start.14 = (f32[72,128]{1,0:T(8,128)S(1)}, f32[72,128]{1,0:T(8,128)S(1)}, u32[]{:S(2)}, u32[]{:S(2)}) collective-permute-start(f32[72,128]{1,0:T(8,128)S(1)} %get-tuple-element.56.refs_0_), channel_id=1, source_target_pairs={{0,2},{1,3},{2,0},{3,1},{4,6},{5,7},{6,4},{7,5},{8,10},{9,11},{10,... | collective-permute-start | bytes 110600 | tf_op jit(solution)/shard_map/sum_req/ppermute | solution.py:284
  45.6 4.0 %collective-permute-start.13 = (f32[72,128]{1,0:T(8,128)S(1)}, f32[72,128]{1,0:T(8,128)S(1)}, u32[]{:S(2)}, u32[]{:S(2)}) collective-permute-start(f32[72,128]{1,0:T(8,128)S(1)} %get-tuple-element.56.refs_0_), channel_id=1, source_target_pairs={{0,3},{1,2},{2,1},{3,0},{4,7},{5,6},{6,5},{7,4},{8,11},{9,10},{10,... | collective-permute-start | bytes 110600 | tf_op jit(solution)/shard_map/sum_req/ppermute | solution.py:284
  46.4 3.2 %collective-permute-start.12 = (f32[72,128]{1,0:T(8,128)S(1)}, f32[72,128]{1,0:T(8,128)S(1)}, u32[]{:S(2)}, u32[]{:S(2)}) collective-permute-start(f32[72,128]{1,0:T(8,128)S(1)} %get-tuple-element.56.refs_0_), channel_id=1, source_target_pairs={{0,1},{1,0},{2,3},{3,2},{4,5},{5,4},{6,7},{7,6},{8,9},{9,8},{10,11... | collective-permute-start | bytes 110600 | tf_op jit(solution)/shard_map/sum_req/ppermute | solution.py:284
  53.9 5.4 %collective-permute-start.16 = (f32[136,128]{1,0:T(8,128)S(1)}, f32[136,128]{1,0:T(8,128)S(1)}, u32[]{:S(2)}, u32[]{:S(2)}) collective-permute-start(f32[136,128]{1,0:T(8,128)S(1)} %add.87), channel_id=1, source_target_pairs={{0,64},{1,65},{2,66},{3,67},{4,52},{5,53},{6,54},{7,55},{8,72},{9,... | collective-permute-start | bytes 208904 | tf_op jit(solution)/shard_map/sum_z_outer/ppermute | solution.py:275
  59.3 4.9 %collective-permute-start.19 = (f32[136,128]{1,0:T(8,128)S(1)}, f32[136,128]{1,0:T(8,128)S(1)}, u32[]{:S(2)}, u32[]{:S(2)}) collective-permute-start(f32[136,128]{1,0:T(8,128)S(1)} %add.88), channel_id=1, source_target_pairs={{0,64},{1,65},{2,66},{3,67},{4,20},{5,21},{6,22},{7,23},{8,72},{9,... | collective-permute-start | bytes 208904 | tf_op jit(solution)/shard_map/sum_z_inner/ppermute | solution.py:275
  60.8 5.0 %collective-permute-start.18 = (f32[136,128]{1,0:T(8,128)S(1)}, f32[136,128]{1,0:T(8,128)S(1)}, u32[]{:S(2)}, u32[]{:S(2)}) collective-permute-start(f32[136,128]{1,0:T(8,128)S(1)} %add.88), channel_id=1, source_target_pairs={{0,64},{1,65},{2,66},{3,67},{4,28},{5,29},{6,30},{7,31},{8,72},{9,... | collective-permute-start | bytes 208904 | tf_op jit(solution)/shard_map/sum_z_inner/ppermute | solution.py:275
  61.8 4.0 %collective-permute-start.17 = (f32[136,128]{1,0:T(8,128)S(1)}, f32[136,128]{1,0:T(8,128)S(1)}, u32[]{:S(2)}, u32[]{:S(2)}) collective-permute-start(f32[136,128]{1,0:T(8,128)S(1)} %add.88), channel_id=1, source_target_pairs={{0,64},{1,65},{2,66},{3,67},{4,12},{5,13},{6,14},{7,15},{8,72},{9,... | collective-permute-start | bytes 208904 | tf_op jit(solution)/shard_map/sum_z_inner/ppermute | solution.py:275
  65.7 4.8 %collective-permute-start.22 = (f32[136,128]{1,0:T(8,128)S(1)}, f32[136,128]{1,0:T(8,128)S(1)}, u32[]{:S(2)}, u32[]{:S(2)}) collective-permute-start(f32[136,128]{1,0:T(8,128)S(1)} %add_add_fusion.3), channel_id=1, source_target_pairs={{0,8},{1,9},{2,10},{3,11},{4,132},{5,133},{6,134},{7,135},{8,0},{9... | collective-permute-start | bytes 208904 | tf_op jit(solution)/shard_map/sum_y/ppermute | solution.py:275
  67.0 4.4 %collective-permute-start.21 = (f32[136,128]{1,0:T(8,128)S(1)}, f32[136,128]{1,0:T(8,128)S(1)}, u32[]{:S(2)}, u32[]{:S(2)}) collective-permute-start(f32[136,128]{1,0:T(8,128)S(1)} %add_add_fusion.3), channel_id=1, source_target_pairs={{0,8},{1,9},{2,10},{3,11},{4,196},{5,197},{6,198},{7,199},{8,0},{9... | collective-permute-start | bytes 208904 | tf_op jit(solution)/shard_map/sum_y/ppermute | solution.py:275
  67.8 3.6 %collective-permute-start.20 = (f32[136,128]{1,0:T(8,128)S(1)}, f32[136,128]{1,0:T(8,128)S(1)}, u32[]{:S(2)}, u32[]{:S(2)}) collective-permute-start(f32[136,128]{1,0:T(8,128)S(1)} %add_add_fusion.3), channel_id=1, source_target_pairs={{0,8},{1,9},{2,10},{3,11},{4,68},{5,69},{6,70},{7,71},{8,0},{9,1},... | collective-permute-start | bytes 208904 | tf_op jit(solution)/shard_map/sum_y/ppermute | solution.py:275
  73.8 4.3 %collective-permute-start.26 = (f32[72,128]{1,0:T(8,128)S(1)}, f32[72,128]{1,0:T(8,128)S(1)}, u32[]{:S(2)}, u32[]{:S(2)}) collective-permute-start(f32[72,128]{1,0:T(8,128)S(1)} %get-tuple-element.63.refs_0_), channel_id=1, source_target_pairs={{0,2},{1,3},{2,0},{3,1},{4,6},{5,7},{6,4},{7,5},{8,10},{9,11},{10,... | collective-permute-start | bytes 110600 | tf_op jit(solution)/shard_map/sum_req/ppermute | solution.py:284
  75.0 4.2 %collective-permute-start.25 = (f32[72,128]{1,0:T(8,128)S(1)}, f32[72,128]{1,0:T(8,128)S(1)}, u32[]{:S(2)}, u32[]{:S(2)}) collective-permute-start(f32[72,128]{1,0:T(8,128)S(1)} %get-tuple-element.63.refs_0_), channel_id=1, source_target_pairs={{0,3},{1,2},{2,1},{3,0},{4,7},{5,6},{6,5},{7,4},{8,11},{9,10},{10,... | collective-permute-start | bytes 110600 | tf_op jit(solution)/shard_map/sum_req/ppermute | solution.py:284
  75.9 3.2 %collective-permute-start.24 = (f32[72,128]{1,0:T(8,128)S(1)}, f32[72,128]{1,0:T(8,128)S(1)}, u32[]{:S(2)}, u32[]{:S(2)}) collective-permute-start(f32[72,128]{1,0:T(8,128)S(1)} %get-tuple-element.63.refs_0_), channel_id=1, source_target_pairs={{0,1},{1,0},{2,3},{3,2},{4,5},{5,4},{6,7},{7,6},{8,9},{9,8},{10,11... | collective-permute-start | bytes 110600 | tf_op jit(solution)/shard_map/sum_req/ppermute | solution.py:284
  83.2 5.4 %collective-permute-start.28 = (f32[136,128]{1,0:T(8,128)S(1)}, f32[136,128]{1,0:T(8,128)S(1)}, u32[]{:S(2)}, u32[]{:S(2)}) collective-permute-start(f32[136,128]{1,0:T(8,128)S(1)} %add.95), channel_id=1, source_target_pairs={{0,64},{1,65},{2,66},{3,67},{4,52},{5,53},{6,54},{7,55},{8,72},{9,... | collective-permute-start | bytes 208904 | tf_op jit(solution)/shard_map/sum_z_outer/ppermute | solution.py:275
  88.6 4.9 %collective-permute-start.31 = (f32[136,128]{1,0:T(8,128)S(1)}, f32[136,128]{1,0:T(8,128)S(1)}, u32[]{:S(2)}, u32[]{:S(2)}) collective-permute-start(f32[136,128]{1,0:T(8,128)S(1)} %add.96), channel_id=1, source_target_pairs={{0,64},{1,65},{2,66},{3,67},{4,20},{5,21},{6,22},{7,23},{8,72},{9,... | collective-permute-start | bytes 208904 | tf_op jit(solution)/shard_map/sum_z_inner/ppermute | solution.py:275
  89.7 5.1 %collective-permute-start.30 = (f32[136,128]{1,0:T(8,128)S(1)}, f32[136,128]{1,0:T(8,128)S(1)}, u32[]{:S(2)}, u32[]{:S(2)}) collective-permute-start(f32[136,128]{1,0:T(8,128)S(1)} %add.96), channel_id=1, source_target_pairs={{0,64},{1,65},{2,66},{3,67},{4,28},{5,29},{6,30},{7,31},{8,72},{9,... | collective-permute-start | bytes 208904 | tf_op jit(solution)/shard_map/sum_z_inner/ppermute | solution.py:275
  91.2 3.9 %collective-permute-start.29 = (f32[136,128]{1,0:T(8,128)S(1)}, f32[136,128]{1,0:T(8,128)S(1)}, u32[]{:S(2)}, u32[]{:S(2)}) collective-permute-start(f32[136,128]{1,0:T(8,128)S(1)} %add.96), channel_id=1, source_target_pairs={{0,64},{1,65},{2,66},{3,67},{4,12},{5,13},{6,14},{7,15},{8,72},{9,... | collective-permute-start | bytes 208904 | tf_op jit(solution)/shard_map/sum_z_inner/ppermute | solution.py:275
  95.2 4.8 %collective-permute-start.34 = (f32[136,128]{1,0:T(8,128)S(1)}, f32[136,128]{1,0:T(8,128)S(1)}, u32[]{:S(2)}, u32[]{:S(2)}) collective-permute-start(f32[136,128]{1,0:T(8,128)S(1)} %add_add_fusion.1), channel_id=1, source_target_pairs={{0,8},{1,9},{2,10},{3,11},{4,132},{5,133},{6,134},{7,135},{8,0},{9... | collective-permute-start | bytes 208904 | tf_op jit(solution)/shard_map/sum_y/ppermute | solution.py:275
  96.9 4.4 %collective-permute-start.33 = (f32[136,128]{1,0:T(8,128)S(1)}, f32[136,128]{1,0:T(8,128)S(1)}, u32[]{:S(2)}, u32[]{:S(2)}) collective-permute-start(f32[136,128]{1,0:T(8,128)S(1)} %add_add_fusion.1), channel_id=1, source_target_pairs={{0,8},{1,9},{2,10},{3,11},{4,196},{5,197},{6,198},{7,199},{8,0},{9... | collective-permute-start | bytes 208904 | tf_op jit(solution)/shard_map/sum_y/ppermute | solution.py:275
  101.4 7.5 %collective-permute-start.35 = (f32[136,128]{1,0:T(8,128)S(1)}, f32[136,128]{1,0:T(8,128)S(1)}, u32[]{:S(2)}, u32[]{:S(2)}) collective-permute-start(f32[136,128]{1,0:T(8,128)S(1)} %constant_dynamic-update-slice_fusion.state_own), channel_id=1, source_target_pairs={{0,4},{1,5},{2,6},{3,7},{4,0},{5,1},{6,2},{7,3},{8,12},{9,13},{10,... | collective-permute-start | bytes 208904 | tf_op jit(solution)/shard_map/back_core/ppermute | solution.py:275
  101.7 4.0 %collective-permute-start.38 = (f32[8,128]{1,0:T(8,128)S(1)}, f32[8,128]{1,0:T(8,128)S(1)}, u32[]{:S(2)}, u32[]{:S(2)}) collective-permute-start(f32[8,128]{1,0:T(8,128)S(1)} %get-tuple-element.74.last_0), channel_id=1, source_target_pairs={{0,64},{1,65},{2,66},{3,67},{4,6},{5,7},{6,4},{7,5},{8,72},{9,73},... | collective-permute-start | bytes 12296 | tf_op jit(solution)/shard_map/sum_req_last/ppermute | solution.py:275
  103.8 3.7 %collective-permute-start.37 = (f32[8,128]{1,0:T(8,128)S(1)}, f32[8,128]{1,0:T(8,128)S(1)}, u32[]{:S(2)}, u32[]{:S(2)}) collective-permute-start(f32[8,128]{1,0:T(8,128)S(1)} %get-tuple-element.74.last_0), channel_id=1, source_target_pairs={{0,64},{1,65},{2,66},{3,67},{4,7},{5,6},{6,5},{7,4},{8,72},{9,73},... | collective-permute-start | bytes 12296 | tf_op jit(solution)/shard_map/sum_req_last/ppermute | solution.py:275
  (14 other events, 126.8 us)
